TPU v7x, 32 devices: a whole 2x2x4 slice. The times are simulated.
32 devices in a mesh: dp: 8 (over y, x, core), head: 4 (over z).
Axes of the slice: x: 2, y: 2, z: 4, core: 2. Of those that a mesh axis runs over, the one named last changes fastest.
Arguments:
- tokens: bfloat16 [16384, 1024], P(('dp', 'head')), may hold values from -6 to 6
- input_norm_gain: float32 [1024], replicated, may hold values from 0.5 to 1.5
- proj_in: bfloat16 [1024, 8, 4, 128], P(None, 'head'), may hold values from -0.1875 to 0.1875
- proj_out: bfloat16 [8, 128, 1024], P('head'), may hold values from -0.1875 to 0.1875
- bias_slope: float32 [8], P('head'), may hold values from -0.8 to 0.3
- lengths: int32 [8, 16], P('dp'), may hold values from 1 to 1024, 2048 in all within a row
- cotangent: bfloat16 [16384, 1024], P(('dp', 'head')), may hold values from -6 to 6
Outputs:
- mixed: bfloat16 [16384, 1024], P(('dp', 'head'))
- token_gradient: float32 [16384, 1024], P(('dp', 'head'))
- norm_gain_gradient: float32 [1024], replicated
- grad_proj_in: float32 [1024, 8, 4, 128], P(None, 'head')
- grad_proj_out: float32 [8, 128, 1024], P('head')
- grad_slope: float32 [8], P('head')
Inputs may be any that keep to these rules, and one draw needn't show every extreme that they name: Each row of lengths lists the history lengths of the 16 users of one group, summing to 2048; the longest in every row is exactly 1024.
All inputs are finite; a program needn't handle non-finite values.
Results may differ from a plain program's by a relative error of at most 0.034.
Values may be sent and summed in bfloat16 or wider, within the bound.
No kernel may reach another device: no remote copies, remote signals or barrier semaphores. Data moves between devices by JAX's collectives and lax.ppermute only.
A program may use at most 192 MiB of HBM per device.

v0:
```python
import functools

import jax
import jax.numpy as jnp
from jax import lax
from jax.experimental import pallas as pl
from jax.experimental.pallas import tpu as pltpu
from jax.sharding import PartitionSpec as P

EPSILON = 1e-05
BF = jnp.bfloat16
F32 = jnp.float32
AXES = ("dp", "head")
NT = (((1,), (1,)), ((), ()))
TN = (((0,), (0,)), ((), ()))
NN = (((1,), (0,)), ((), ()))


def dot(a, b, dims=NN):
    return lax.dot_general(a, b, dims, preferred_element_type=F32)


def silu_slope(values):
    sigma = jax.nn.sigmoid(values)
    return sigma * (1.0 + values * (1.0 - sigma))


def tanh_slope(values):
    sigma = 0.5 + 0.5 * jnp.tanh(0.5 * values)
    return sigma * (1.0 + values * (1.0 - sigma))


def fill_distance(dist, blocks, rows):
    row = lax.broadcasted_iota(jnp.int32, (rows, rows), 0)
    column = lax.broadcasted_iota(jnp.int32, (rows, rows), 1)

    def one(step, carry):
        offset = jnp.maximum(step * rows + row - column, 0).astype(F32)
        dist[step] = jnp.log(1.0 + offset)
        return carry

    lax.fori_loop(0, blocks, one, 0)


def half_score(q, k, slope, distance, visible, scale):
    u = dot(q, k, NT) * (0.5 * scale) + (0.5 * slope) * distance
    return jnp.where(visible, u, -1.0e4)


def visible_pairs(starts_ref, i, j, rows):
    row = lax.broadcasted_iota(jnp.int32, (rows, rows), 0) + i * rows
    column = lax.broadcasted_iota(jnp.int32, (rows, rows), 1) + j * rows
    first = starts_ref[pl.ds(pl.multiple_of(i * rows, rows), rows), :]
    return (column >= first) & (column <= row)


def forward_kernel(
    nh, dim, rows, blocks, low, held, sent, slopes, starts_ref, w_ref, *refs
):
    pieces = refs[:blocks]
    out_ref, act_ref, pre_ref, dist, acc = refs[blocks:]
    for b in range(blocks):
        pre = dot(pieces[b][...], w_ref[...], NT)
        half = 0.5 * pre
        pre_ref[b * rows : (b + 1) * rows, :] = pre.astype(BF)
        act_ref[b * rows : (b + 1) * rows, :] = (half + half * jnp.tanh(half)).astype(BF)
    fill_distance(dist, blocks, rows)
    scale = dim ** (-0.5)
    part = nh * dim

    def at(block):
        return pl.ds(pl.multiple_of(block * rows, rows), rows)

    def query_block(i, carry):
        acc[...] = jnp.zeros_like(acc)

        def key_block(j, inner):
            visible = visible_pairs(starts_ref, i, j, rows)
            distance = dist[i - j]
            for h in range(nh):
                q = act_ref[at(held[i]), part + h * dim : part + (h + 1) * dim]
                k = act_ref[at(held[j]), 2 * part + h * dim : 2 * part + (h + 1) * dim]
                v = act_ref[at(held[j]), h * dim : (h + 1) * dim]
                u = half_score(q, k, slopes[h], distance, visible, scale)
                w = (u + u * jnp.tanh(u)).astype(BF)
                acc[:, h * dim : (h + 1) * dim] += dot(w, v)
            return inner

        lax.fori_loop(low[i], i + 1, key_block, 0)
        out_ref[at(sent[i]), :] = acc[...].astype(BF)
        return carry

    lax.fori_loop(0, blocks, query_block, 0)


def backward_kernel(
    nh, dim, rows, blocks, low, held, sent, slopes, starts_ref, act_ref, pre_ref, datt_ref,
    out_ref, slope_ref, dist, dq, dk, dv, gs
):
    fill_distance(dist, blocks, rows)
    scale = dim ** (-0.5)
    part = nh * dim
    dk[...] = jnp.zeros_like(dk)
    dv[...] = jnp.zeros_like(dv)
    gs[...] = jnp.zeros_like(gs)

    def at(block):
        return pl.ds(pl.multiple_of(block * rows, rows), rows)

    def query_block(i, carry):
        dq[...] = jnp.zeros_like(dq)
        mine = held[i]

        def key_block(j, inner):
            visible = visible_pairs(starts_ref, i, j, rows)
            distance = dist[i - j]
            theirs = held[j]
            for h in range(nh):
                cols = slice(h * dim, (h + 1) * dim)
                q = act_ref[at(mine), part + h * dim : part + (h + 1) * dim]
                k = act_ref[at(theirs), 2 * part + h * dim : 2 * part + (h + 1) * dim]
                v = act_ref[at(theirs), cols]
                da = datt_ref[at(sent[i]), cols]
                u = half_score(q, k, slopes[h], distance, visible, scale)
                t = jnp.tanh(u)
                w = u + u * t
                ds = dot(da, v, NT) * ((1.0 + t) + w * (1.0 - t))
                gs[h] += jnp.sum((ds * distance).reshape(rows // 8, 8, rows), axis=0)
                wb = w.astype(BF)
                db = ds.astype(BF)
                dv[at(theirs), cols] += dot(wb, da, TN)
                dk[at(theirs), cols] += dot(db, q, TN)
                dq[:, cols] += dot(db, k)
            return inner

        lax.fori_loop(low[i], i + 1, key_block, 0)
        slope = tanh_slope(pre_ref[at(mine), part : 2 * part].astype(F32))
        out_ref[at(mine), part : 2 * part] = (dq[...] * (0.5 * scale) * slope).astype(BF)
        return carry

    lax.fori_loop(0, blocks, query_block, 0)

    def finish(b, carry):
        slope_v = tanh_slope(pre_ref[at(b), :part].astype(F32))
        out_ref[at(b), :part] = (dv[at(b), :] * slope_v).astype(BF)
        slope_k = tanh_slope(pre_ref[at(b), 2 * part :].astype(F32))
        out_ref[at(b), 2 * part :] = (dk[at(b), :] * (0.5 * scale) * slope_k).astype(BF)
        return carry

    lax.fori_loop(0, blocks, finish, 0)
    for h in range(nh):
        slope_ref[h] = 0.5 * gs[h]


def attention_cost(nh, dim, total, matmuls):
    pairs = total * total // 5
    return pl.CostEstimate(
        flops=30 * matmuls * nh * dim * pairs,
        bytes_accessed=total * nh * dim * 2 * 2 * matmuls,
        transcendentals=nh * pairs,
    )


def attend(nh, dim, rows, tables, slopes, starts, w, pieces):
    blocks = len(pieces)
    total = blocks * rows
    wide = jax.ShapeDtypeStruct((total, 3 * nh * dim), BF)
    smem = pl.BlockSpec(memory_space=pltpu.SMEM)
    vmem = pl.BlockSpec(memory_space=pltpu.VMEM)
    return pl.pallas_call(
        functools.partial(forward_kernel, nh, dim, rows, blocks),
        out_shape=(jax.ShapeDtypeStruct((total, nh * dim), BF), wide, wide),
        in_specs=[smem] * 4 + [vmem] * (2 + blocks),
        out_specs=(vmem,) * 3,
        scratch_shapes=[
            pltpu.VMEM((blocks, rows, rows), F32),
            pltpu.VMEM((rows, nh * dim), F32),
        ],
        compiler_params=pltpu.CompilerParams(vmem_limit_bytes=40 * 2**20),
        cost_estimate=attention_cost(nh, dim, total, 2),
    )(*tables, slopes, starts, w, *pieces)


def unpack_kernel(nh, dim, w_ref, after_ref, own_ref, gate_ref):
    part = nh * dim
    for h in range(nh):
        for kind in range(4):
            x = w_ref[:, h * 4 + kind, :]
            x = x.astype(F32).T.astype(BF)
            at = ((kind - 1) * nh + h) * dim
            if kind:
                own_ref[at : at + dim, :] = x
            else:
                gate_ref[h * dim : (h + 1) * dim, :] = x


def unpack(nh, dim, proj_in, after):
    width = proj_in.shape[0]
    vmem = pl.BlockSpec(memory_space=pltpu.VMEM)
    return pl.pallas_call(
        functools.partial(unpack_kernel, nh, dim),
        out_shape=(
            jax.ShapeDtypeStruct((3 * nh * dim, width), BF),
            jax.ShapeDtypeStruct((nh * dim, width), BF),
        ),
        in_specs=[vmem, pl.BlockSpec(memory_space=pl.ANY)],
        out_specs=(vmem,) * 2,
        compiler_params=pltpu.CompilerParams(vmem_limit_bytes=24 * 2**20),
        cost_estimate=pl.CostEstimate(flops=2 * 10**10, bytes_accessed=8 * 2**20, transcendentals=0),
    )(proj_in.reshape(width, nh * 4, dim), after)


def prepare_kernel(
    n, n_dp, slab, z_ref, all_ref, normed_ref, cot_ref, after_ref,
    gate_w_ref, out_w_ref, pre_gate_ref, d_gated_ref
):
    part = n_dp * slab
    for t in range(n):
        q = z_ref[0] ^ t
        for s in range(n_dp):
            at = t * part + s * slab
            gate_w_ref[at : at + slab, :] = all_ref[s, q, 0]
            out_w_ref[at : at + slab, :] = all_ref[s, q, 1]
    for t in range(n):
        at = slice(t * part, (t + 1) * part)
        pre_gate_ref[:, at] = dot(normed_ref[...], gate_w_ref[at, :], NT)
        d_gated_ref[:, at] = dot(cot_ref[...], out_w_ref[at, :], NT)


def prepare(n, n_dp, slab, z, everything, normed, cotangent, after):
    rows, width = normed.shape
    vmem = pl.BlockSpec(memory_space=pltpu.VMEM)
    columns = n * n_dp * slab
    return pl.pallas_call(
        functools.partial(prepare_kernel, n, n_dp, slab),
        out_shape=(
            jax.ShapeDtypeStruct((columns, width), BF),
            jax.ShapeDtypeStruct((columns, width), BF),
            jax.ShapeDtypeStruct((rows, columns), F32),
            jax.ShapeDtypeStruct((rows, columns), F32),
        ),
        in_specs=[pl.BlockSpec(memory_space=pltpu.SMEM)]
        + [vmem] * 3
        + [pl.BlockSpec(memory_space=pl.ANY)],
        out_specs=(vmem,) * 4,
        compiler_params=pltpu.CompilerParams(vmem_limit_bytes=32 * 2**20),
        cost_estimate=pl.CostEstimate(
            flops=20 * rows * width * columns, bytes_accessed=16 * 2**20, transcendentals=0
        ),
    )(z.reshape(1), everything, normed, cotangent, after)


def assemble_kernel(nh, dim, n_dp, first_ref, second_ref, in_ref, out_ref, rows_ref):
    part = nh * dim
    slab = part // n_dp
    side = first_ref.shape[2]
    for s in range(n_dp):
        for side_at, ref in ((0, first_ref), (1, second_ref)):
            x = ref[s].astype(F32)
            columns = slice(side_at * side, (side_at + 1) * side)
            rows_ref[3 * s * slab : 3 * (s + 1) * slab, columns] = x[: 3 * slab]
            at = 3 * part + s * slab
            rows_ref[at : at + slab, columns] = x[3 * slab : 4 * slab]
            out_ref[s * slab : (s + 1) * slab, columns] = x[4 * slab : 5 * slab]
    for h in range(nh):
        for kind in range(4):
            at = kind * part + h * dim
            in_ref[:, h * 4 + (kind + 1) % 4, :] = rows_ref[at : at + dim, :].T


def assemble(nh, dim, n_dp, width, first, second):
    vmem = pl.BlockSpec(memory_space=pltpu.VMEM)
    return pl.pallas_call(
        functools.partial(assemble_kernel, nh, dim, n_dp),
        out_shape=(
            jax.ShapeDtypeStruct((width, nh * 4, dim), F32),
            jax.ShapeDtypeStruct((nh * dim, width), F32),
        ),
        in_specs=[vmem] * 2,
        out_specs=(vmem,) * 2,
        scratch_shapes=[pltpu.VMEM((4 * nh * dim, width), F32)],
        compiler_params=pltpu.CompilerParams(vmem_limit_bytes=40 * 2**20),
        cost_estimate=pl.CostEstimate(flops=0, bytes_accessed=8 * 2**20, transcendentals=0),
    )(first, second)


def attend_back(nh, dim, rows, tables, slopes, starts, act, pre, d_attended):
    total = act.shape[0]
    blocks = total // rows
    smem = pl.BlockSpec(memory_space=pltpu.SMEM)
    vmem = pl.BlockSpec(memory_space=pltpu.VMEM)
    return pl.pallas_call(
        functools.partial(backward_kernel, nh, dim, rows, blocks),
        out_shape=(
            jax.ShapeDtypeStruct(act.shape, BF),
            jax.ShapeDtypeStruct((nh, 8, rows), F32),
        ),
        in_specs=[smem] * 4 + [vmem] * 4,
        out_specs=(vmem, vmem),
        scratch_shapes=[
            pltpu.VMEM((blocks, rows, rows), F32),
            pltpu.VMEM((rows, nh * dim), F32),
            pltpu.VMEM((total, nh * dim), F32),
            pltpu.VMEM((total, nh * dim), F32),
            pltpu.VMEM((nh, 8, rows), F32),
        ],
        compiler_params=pltpu.CompilerParams(vmem_limit_bytes=48 * 2**20),
        cost_estimate=attention_cost(nh, dim, total, 5),
    )(*tables, slopes, starts, act, pre, d_attended)


def body(
    n_dp, n, tokens, input_norm_gain, proj_in, proj_out, bias_slope, lengths, cotangent
):
    local_rows, width = tokens.shape
    nh, dim = proj_in.shape[1], proj_in.shape[3]
    part = nh * dim
    rows = local_rows // 2
    half = n // 2
    dp = lax.axis_index("dp")
    z = lax.axis_index("head")
    c = dp & 1
    host = (z >= half).astype(jnp.int32)
    is_home = c == host

    def move(x, target):
        pairs = []
        for d in range(n_dp):
            for s in range(n):
                e, t = target(d, s)
                pairs.append((d * n + s, e * n + t))
        return lax.ppermute(x, AXES, pairs)

    def core_swap(x):
        return move(x, lambda d, s: (d ^ 1, s))

    def z_swap(x, bit):
        return move(x, lambda d, s: (d, s ^ bit))

    def dp_swap(x, bit):
        return move(x, lambda d, s: (d ^ bit, s))

    def send_target(r):
        def target(d, s):
            core = int(s >= half)
            return ((d & ~1) | core, s ^ r ^ ((d & 1) * half))

        return target

    def back_target(r):
        forward = {}
        for d in range(n_dp):
            for s in range(n):
                forward[send_target(r)(d, s)] = (d, s)
        return lambda d, s: forward[(d, s)]

    def cross(x):
        return move(x, lambda d, s: (d, s ^ ((d & 1) * half)))

    token_single = tokens.astype(F32)
    centred_input = jnp.mean(token_single, axis=1, keepdims=True)
    spread = jnp.mean((token_single - centred_input) ** 2, axis=1, keepdims=True)
    inverse_deviation = lax.rsqrt(spread + EPSILON)
    xhat = (token_single - centred_input) * inverse_deviation
    normed = (xhat * input_norm_gain).astype(BF)

    first, second = normed[:rows], normed[rows:]
    keep = jnp.where(c == 0, first, second)
    give = jnp.where(c == 0, second, first)
    barrier = lax.optimization_barrier
    bits = [1 << b for b in range(n_dp.bit_length() - 1)]
    slab_o = part // n_dp
    slab_w = 3 * slab_o
    got = core_swap(give)
    w_own, gate_rows = unpack(nh, dim, proj_in, give)
    mirrored = sum(
        jnp.where((dp & b) != 0, bits[-1] // b, 0) for b in bits
    )
    w_slab = lax.dynamic_slice_in_dim(w_own, mirrored * slab_w, slab_w, 0)
    items = {0: jnp.where(is_home, keep, got)}
    crossed = z_swap(
        jnp.concatenate([jnp.where(is_home, got, keep), w_slab], axis=0), half
    )
    bit = 1
    while bit < half:
        for t in sorted(items):
            items[t ^ bit] = z_swap(items[t], bit)
        bit *= 2
    items, crossed = barrier((items, crossed))
    items[half], piece = crossed[:rows], crossed[rows:]
    bit = 1
    while bit < half:
        for t in [t for t in sorted(items) if t >= half]:
            items[t ^ bit] = z_swap(items[t], bit)
        bit *= 2

    def dp_double(x, bit):
        other = dp_swap(x, bit)
        up = (dp & bit) != 0
        return jnp.concatenate([jnp.where(up, other, x), jnp.where(up, x, other)], axis=0)

    for b in bits[:1:-1]:
        piece = dp_double(piece, b)
    items, piece = barrier((items, piece))
    for b in bits[1::-1]:
        piece = dp_double(piece, b)
    mine = [items[t] for t in range(n)]
    theirs = [core_swap(x) for x in mine]
    total = n * local_rows

    slabs = jnp.concatenate(
        [
            lax.dynamic_slice_in_dim(gate_rows, dp * slab_o, slab_o, 0),
            lax.dynamic_slice_in_dim(proj_out.reshape(part, width), dp * slab_o, slab_o, 0),
        ],
        axis=0,
    )
    everything = lax.all_gather(slabs, AXES).reshape(n_dp, n, 2, slab_o, width)

    w_qkv = jnp.where(c == 0, w_own, piece)

    own_lengths = lengths[0]
    hosted_lengths = jnp.where(is_home, own_lengths, core_swap(own_lengths))
    ends = jnp.cumsum(hosted_lengths)
    positions = jnp.arange(total, dtype=jnp.int32)
    starts = jnp.max(
        jnp.where(positions[:, None] >= ends[None, :], ends[None, :], 0), axis=1, keepdims=True
    ).astype(jnp.int32)
    block = jnp.arange(total // rows, dtype=jnp.int32)
    low = starts[::rows, 0] // rows
    shard = (block // 2) ^ z
    held = ((block & 1) ^ c) * n + shard
    sent = 2 * (shard ^ (c * half)) + (block & 1)
    tables = (low, held, sent)
    slopes = cross(bias_slope)

    attended, act, pre = attend(
        nh, dim, rows, tables, slopes, starts, w_qkv, mine + theirs
    )
    w_gate, w_out, pre_gate, d_gated = prepare(
        n, n_dp, slab_o, z, everything, normed, cotangent, attended
    )
    gathered = jnp.concatenate(mine + theirs, axis=0)
    arrived = [
        move(attended[r * local_rows : (r + 1) * local_rows], send_target(r)) for r in range(n)
    ]
    arrived, w_gate, w_out, pre_gate, d_gated = barrier(
        (arrived, w_gate, w_out, pre_gate, d_gated)
    )
    att_own = jnp.concatenate(arrived, axis=1).astype(F32)

    gate = jax.nn.silu(pre_gate).astype(BF).astype(F32)
    mean_o = jnp.mean(att_own, axis=1, keepdims=True)
    square_o = jnp.mean(att_own * att_own, axis=1, keepdims=True)
    inv_o = lax.rsqrt(square_o - mean_o * mean_o + EPSILON)
    normed_o = (att_own - mean_o) * inv_o
    gated = (normed_o * gate).astype(BF)
    d_norm_in = d_gated * gate
    first_g = jnp.mean(d_norm_in, axis=1, keepdims=True)
    second_g = jnp.mean(d_norm_in * normed_o, axis=1, keepdims=True)
    d_attended = (inv_o * (d_norm_in - first_g - normed_o * second_g)).astype(BF)
    mixed = (token_single + dot(gated, w_out)).astype(BF)
    d_gate = (d_gated * normed_o).astype(BF).astype(F32)
    d_pre_gate = (d_gate * silu_slope(pre_gate)).astype(BF)
    d_normed_gate = dot(d_pre_gate, w_gate)
    gate_part = dot(d_pre_gate, normed, TN)
    out_part = dot(gated, cotangent, TN)

    def add(x, y):
        return (x.astype(F32) + y.astype(F32)).astype(BF)

    order = bits[1:] + bits[:1]
    split = [2] * len(bits)
    forth, back = bits[1:], bits[:0:-1]

    def reduce_bit(x, b, axis):
        up = (dp & b) != 0
        low_half = lax.slice_in_dim(x, 0, 1, axis=axis)
        high_half = lax.slice_in_dim(x, 1, 2, axis=axis)
        return add(
            jnp.where(up, high_half, low_half),
            dp_swap(jnp.where(up, low_half, high_half), b),
        )

    def double_bit(x, b, axis):
        other = dp_swap(x, b)
        up = (dp & b) != 0
        return jnp.concatenate(
            [jnp.where(up, other, x), jnp.where(up, x, other)], axis=axis
        )

    both = jnp.stack([gate_part, out_part]).astype(BF)
    both = both.reshape([2, n] + split + [slab_o, width])
    d_attended, both = barrier((d_attended, both))
    both = reduce_bit(both, 1, 1 + len(bits))
    arrived = [
        move(d_attended[:, r * part : (r + 1) * part], back_target(r)) for r in range(n)
    ]
    d_att = jnp.concatenate(arrived, axis=0)
    pair = [both[0], both[1]]
    d_att, pair = lax.optimization_barrier((d_att, pair))
    def reduce_pair(pair, k, first_axis):
        return [
            reduce_bit(pair[0], forth[k], first_axis + order.index(forth[k])),
            reduce_bit(pair[1], back[k], first_axis + order.index(back[k])),
        ]

    both = reduce_pair(pair, 0, 1)

    d_pre, slope_rows = attend_back(
        nh, dim, rows, tables, slopes, starts, act, pre, d_att
    )

    def partial(first_block, last_block):
        return dot(d_pre[first_block * rows : last_block * rows], w_qkv).astype(BF)

    d_pre, both = barrier((d_pre, both))
    theirs = partial(n, 2 * n)
    got = core_swap(theirs)
    d_pre, theirs = barrier((d_pre, theirs))
    in_part = dot(d_pre, gathered, TN).astype(BF)
    mine = partial(0, n)
    for k in range(1, len(forth)):
        both = reduce_pair(both, k, 1)
    both = jnp.stack(both).reshape(2, n, slab_o, width)
    in_part, got, both = barrier((in_part, got, both))

    side = width // 2
    x = in_part.reshape(split + [slab_w, width])
    pair = reduce_pair([x[..., :side], x[..., side:]], 0, 0)
    home, away = add(mine[: half * rows], got[: half * rows]), add(
        mine[half * rows :], got[half * rows :]
    )
    bit = half // 2
    while bit >= 1:
        away = add(away[: bit * rows], z_swap(away[bit * rows :], bit))
        bit //= 2
    both = add(both[:, :half], z_swap(both[:, half:], half))
    for k in range(1, len(forth)):
        pair = reduce_pair(pair, k, 0)
    pair, away, home, both = barrier((pair, away, home, both))

    cuts = [away[k * rows // 4 : (k + 1) * rows // 4] for k in range(4)]
    moved = [z_swap(cuts[0], half)]
    bit = half // 2
    while bit >= 1:
        home = add(home[: bit * rows], z_swap(home[bit * rows :], bit))
        both = add(both[:, :bit], z_swap(both[:, bit:], bit))
        bit //= 2
    both = both.reshape(2 * slab_o, width)
    x = cross(jnp.concatenate(pair, axis=-1))
    x, moved, home, both, cuts = barrier((x, moved, home, both, cuts))

    moved.append(z_swap(cuts[1], half))
    x = reduce_bit(x, 1, len(bits) - 1)
    x, moved, cuts = barrier((x, moved, cuts))
    moved.append(z_swap(cuts[2], half))
    x = x.reshape(slab_w, width)
    place = sum(
        jnp.where((dp & b) != 0, 1 << (len(bits) - 1 - i), 0) for i, b in enumerate(order)
    )
    own = jnp.concatenate(
        [
            lax.dynamic_slice_in_dim(w_own, place * slab_w, slab_w, 0),
            lax.dynamic_slice_in_dim(gate_rows, place * slab_o, slab_o, 0),
        ],
        axis=0,
    )
    x = jnp.concatenate([x, both], axis=0)
    gain_part = jnp.sum(x[: slab_w + slab_o].astype(F32) * own.astype(F32), axis=0)
    own_slope = jnp.sum(slope_rows, axis=(1, 2))
    chunk = z ^ (c * half)
    slope_part = jnp.where(jnp.arange(n)[:, None] == chunk, own_slope[None, :], 0.0)
    slope_part = jnp.pad(slope_part.reshape(-1), (0, width - n * nh))
    small = jnp.stack([gain_part, slope_part])
    high = small.astype(BF)
    rest = (small - high.astype(F32)).astype(BF)
    x = jnp.concatenate([x, high, rest, jnp.zeros((12, width), BF)], axis=0)
    x = x.reshape([1] * len(bits) + list(x.shape))

    def double_pair(pair, k):
        return [
            double_bit(pair[0], back[k], order.index(back[k])),
            double_bit(pair[1], forth[k], order.index(forth[k])),
        ]

    pair = double_pair([x[..., :side], x[..., side:]], 0)
    pair, moved, cuts = barrier((pair, moved, cuts))
    moved.append(z_swap(cuts[3], half))
    for k in range(1, len(forth)):
        pair = double_pair(pair, k)
    pair, moved = barrier((pair, moved))
    away = jnp.concatenate(moved, axis=0)
    keep = jnp.where(is_home, home, away)
    got = core_swap(jnp.where(is_home, away, home))
    d_normed = jnp.concatenate(
        [jnp.where(c == 0, keep, got), jnp.where(c == 0, got, keep)], axis=0
    ).astype(F32) + d_normed_gate
    pair = [
        double_bit(y, 1, len(bits) - 1).reshape(n_dp, 5 * slab_o + 16, side) for y in pair
    ]
    grad_proj_in, grad_proj_out = assemble(nh, dim, n_dp, width, *pair)
    grad_proj_in = grad_proj_in.reshape(width, nh, 4, dim)
    grad_proj_out = grad_proj_out.reshape(nh, dim, width)

    small = jnp.concatenate([y[:, 5 * slab_o :] for y in pair], axis=-1).astype(F32)
    small = jnp.sum(small, axis=0)
    small = small[:2] + small[2:4]
    step = 1
    while step < n:
        small = small + z_swap(small, step)
        step *= 2
    norm_gain_gradient = small[0] / input_norm_gain
    grad_slope = lax.dynamic_slice_in_dim(small[1], z * nh, nh, 0)

    dh = d_normed * input_norm_gain
    token_gradient = cotangent.astype(F32) + inverse_deviation * (
        dh
        - jnp.mean(dh, axis=1, keepdims=True)
        - xhat * jnp.mean(dh * xhat, axis=1, keepdims=True)
    )
    return (mixed, token_gradient, norm_gain_gradient, grad_proj_in, grad_proj_out, grad_slope)


def solution(mesh):
    return jax.shard_map(
        functools.partial(body, mesh.shape["dp"], mesh.shape["head"]),
        mesh=mesh,
        in_specs=(
            P(("dp", "head"), None),
            P(),
            P(None, "head", None, None),
            P("head", None, None),
            P("head"),
            P("dp", None),
            P(("dp", "head"), None),
        ),
        out_specs=(
            P(("dp", "head"), None),
            P(("dp", "head"), None),
            P(),
            P(None, "head", None, None),
            P("head", None, None),
            P("head"),
        ),
        check_vma=False,
    )
```

profile of v0, /device:TPU:0, one launch (start us, length us, event | category | flops | bytes accessed | tf_op | source)
XLA Modules:
  0.0 358.0 jit_solution(16155298121563120330)
XLA Ops:
  12.0 3.3 shard_map.118
  21.7 4.0 %collective-permute-start.4 = (bf16[352,1024]{1,0:T(8,128)(2,1)S(1)}, bf16[352,1024]{1,0:T(8,128)(2,1)S(1)}, u32[]{:S(2)}, u32[]{:S(2)}) collective-permute-start(bf16[352,1024]{1,0:T(8,128)(2,1)S(1)} %pad_maximum_fusion.6), channel_id=1, source_target_pairs={{0,2},{1,3},{2,0},{3,1},{4,6},{5,7},{6,4},{7,5},{8,10},{9,11},{10,... | collective-permute-start | bytes 2162696 | tf_op jit(solution)/shard_map/ppermute | solution.py:332
  27.3 28.2 %collective-permute-done.3.refs_1_ = bf16[256,1024]{1,0:T(8,128)(2,1)S(1)} collective-permute-done((bf16[256,1024]{1,0:T(8,128)(2,1)S(1)}, bf16[256,1024]{1,0:T(8,128)(2,1)S(1)}, u32[]{:S(2)}, u32[]{:S(2)}) %collective-permute-start.3) | collective-permute-done | bytes 524320 | tf_op jit(solution)/shard_map/ppermute | solution.py:332
  56.3 4.2 %collective-permute-done.4 = bf16[352,1024]{1,0:T(8,128)(2,1)S(1)} collective-permute-done((bf16[352,1024]{1,0:T(8,128)(2,1)S(1)}, bf16[352,1024]{1,0:T(8,128)(2,1)S(1)}, u32[]{:S(2)}, u32[]{:S(2)}) %collective-permute-start.4) | collective-permute-done | bytes 720928 | tf_op jit(solution)/shard_map/ppermute | solution.py:332
  63.0 2.6 collective-permute-start.5
  67.0 14.5 %collective-permute-done.5.refs_3_ = bf16[256,1024]{1,0:T(8,128)(2,1)S(1)} collective-permute-done((bf16[256,1024]{1,0:T(8,128)(2,1)S(1)}, bf16[256,1024]{1,0:T(8,128)(2,1)S(1)}, u32[]{:S(2)}, u32[]{:S(2)}) %collective-permute-start.5) | collective-permute-done | bytes 524320 | tf_op jit(solution)/shard_map/ppermute | solution.py:332
  85.4 9.7 %collective-permute-done.7 = bf16[192,1024]{1,0:T(8,128)(2,1)} collective-permute-done((bf16[192,1024]{1,0:T(8,128)(2,1)S(1)}, bf16[192,1024]{1,0:T(8,128)(2,1)}, u32[]{:S(2)}, u32[]{:S(2)}) %collective-permute-start.7) | collective-permute-done | bytes 393248 | tf_op jit(solution)/shard_map/ppermute | solution.py:332
  110.0 17.6 %shard_map.119 = (bf16[2048,256]{1,0:T(8,128)(2,1)S(1)}, bf16[2048,768]{1,0:T(8,128)(2,1)S(1)}, bf16[2048,768]{1,0:T(8,128)(2,1)S(1)}) custom-call(s32[8]{0:T(128)S(1)} %and_select_fusion.1.low, s32[8]{0:T(128)S(1)} %multiply_add_fusion.1.held, s32[8]{0:T(128)S(1)} %multiply_add_fusion.sent, f32[2]{0:T(128)S(1)} %collective-permute-done.1.slopes, ...), custom_call_target="tpu_custom_call" | custom-call | flops 12884889600 | bytes 4194304 | tf_op jit(solution)/shard_map/pallas_call | solution.py:170
  135.1 4.9 %collective-permute-start.15 = (bf16[512,256]{1,0:T(8,128)(2,1)}, bf16[512,256]{1,0:T(8,128)(2,1)S(1)}, u32[]{:S(2)}, u32[]{:S(2)}) collective-permute-start(bf16[512,256]{1,0:T(8,128)(2,1)} %get-tuple-element.175), channel_id=1, source_target_pairs={{0,2},{1,3},{2,4},{3,5},{4,0},{5,1},{6,6},{7,7},{8,10},{9,11},{10,... | collective-permute-start | bytes 786440 | tf_op jit(solution)/shard_map/ppermute | solution.py:332
  143.7 2.4 shard_map.120
  147.8 4.0 %collective-permute-done.16 = bf16[512,256]{1,0:T(8,128)(2,1)} collective-permute-done((bf16[512,256]{1,0:T(8,128)(2,1)}, bf16[512,256]{1,0:T(8,128)(2,1)}, u32[]{:S(2)}, u32[]{:S(2)}) %collective-permute-start.16) | collective-permute-done | bytes 262176 | tf_op jit(solution)/shard_map/ppermute | solution.py:332
  153.2 2.8 fusion.25
  156.1 2.7 convolution_convert_fusion
  165.1 5.0 %collective-permute-start.21 = (bf16[2,4,2,2,1,32,1024]{6,5,1,3,2,4,0:T(8,128)(2,1)}, bf16[2,4,2,2,1,32,1024]{6,5,1,3,2,4,0:T(8,128)(2,1)}, u32[]{:S(2)}, u32[]{:S(2)}) collective-permute-start(bf16[2,4,2,2,1,32,1024]{6,5,1,3,2,4,0:T(8,128)(2,1)} %broadcast_select_fusion), channel_id=1, source_target_pairs={{0,4},{1,5},{2,6},{3,7},{4,0},{5,1},{6,2},{7,3},{8,12},{9,13},{10,... | collective-permute-start | bytes 6291464 | tf_op jit(solution)/shard_map/ppermute | solution.py:332
  171.8 3.9 %collective-permute-start.20 = (bf16[512,256]{1,0:T(8,128)(2,1)S(1)}, bf16[512,256]{1,0:T(8,128)(2,1)S(1)}, u32[]{:S(2)}, u32[]{:S(2)}) collective-permute-start(bf16[512,256]{1,0:T(8,128)(2,1)S(1)} %get-tuple-element.171), channel_id=1, source_target_pairs={{0,5},{1,4},{2,1},{3,0},{4,3},{5,2},{6,7},{7,6},{8,13},{9,12},{10,... | collective-permute-start | bytes 786440 | tf_op jit(solution)/shard_map/ppermute | solution.py:332
  181.5 12.8 %collective-permute-done.19 = bf16[512,256]{1,0:T(8,128)(2,1)S(1)} collective-permute-done((bf16[512,256]{1,0:T(8,128)(2,1)S(1)}, bf16[512,256]{1,0:T(8,128)(2,1)S(1)}, u32[]{:S(2)}, u32[]{:S(2)}) %collective-permute-start.19) | collective-permute-done | bytes 262176 | tf_op jit(solution)/shard_map/ppermute | solution.py:332
  194.4 3.2 add_convert_fusion
  199.7 26.0 %shard_map.121 = (bf16[2048,768]{1,0:T(8,128)(2,1)S(1)}, f32[2,8,256]{2,1,0:T(8,128)S(1)}) custom-call(s32[8]{0:T(128)S(1)} %and_select_fusion.1.low, s32[8]{0:T(128)S(1)} %multiply_add_fusion.1.held, s32[8]{0:T(128)S(1)} %multiply_add_fusion.sent, f32[2]{0:T(128)S(1)} %collective-permute-done.1.slopes, s32[2048,1]{1,0:T(8,128)S(1)} %copy-done.6, ...), custom_call_target="tpu_custom_call" | custom-call | flops 32212224000 | bytes 10485760 | tf_op jit(solution)/shard_map/pallas_call | solution.py:292
  229.2 3.4 convolution_convert_fusion.3
  232.5 7.3 %collective-permute-start.24 = (bf16[1024,1024]{1,0:T(8,128)(2,1)S(1)}, bf16[1024,1024]{1,0:T(8,128)(2,1)S(1)}, u32[]{:S(2)}, u32[]{:S(2)}) collective-permute-start(bf16[1024,1024]{1,0:T(8,128)(2,1)S(1)} %convolution_convert_fusion.3), channel_id=1, source_target_pairs={{0,4},{1,5},{2,6},{3,7},{4,0},{5,1},{6,2},{7,3},{8,12},{9,13},{10,... | collective-permute-start | bytes 6291464 | tf_op jit(solution)/shard_map/ppermute | solution.py:332
  239.9 2.7 collective-permute-start.26
  242.6 3.5 convolution_convert_fusion.4
  255.1 9.0 %collective-permute-done.32 = bf16[2,2,32,1024]{3,2,0,1:T(8,128)(2,1)S(1)} collective-permute-done((bf16[2,2,32,1024]{3,2,0,1:T(8,128)(2,1)S(1)}, bf16[2,2,32,1024]{3,2,0,1:T(8,128)(2,1)S(1)}, u32[]{:S(2)}, u32[]{:S(2)}) %collective-permute-start.32) | collective-permute-done | bytes 262176 | tf_op jit(solution)/shard_map/ppermute | solution.py:332
  267.9 3.5 collective-permute-done.31
  277.3 18.3 %collective-permute-done.36 = bf16[2,1,32,1024]{3,2,0,1:T(8,128)(2,1)S(1)} collective-permute-done((bf16[2,1,32,1024]{3,2,0,1:T(8,128)(2,1)S(1)}, bf16[2,1,32,1024]{3,2,0,1:T(8,128)(2,1)S(1)}, u32[]{:S(2)}, u32[]{:S(2)}) %collective-permute-start.36) | collective-permute-done | bytes 131104 | tf_op jit(solution)/shard_map/ppermute | solution.py:332
  298.2 7.4 %collective-permute-done.38 = bf16[64,1024]{1,0:T(8,128)(2,1)S(1)} collective-permute-done((bf16[64,1024]{1,0:T(8,128)(2,1)S(1)}, bf16[64,1024]{1,0:T(8,128)(2,1)S(1)}, u32[]{:S(2)}, u32[]{:S(2)}) %collective-permute-start.38) | collective-permute-done | bytes 131104 | tf_op jit(solution)/shard_map/ppermute | solution.py:332
  308.3 4.7 %collective-permute-done.40 = bf16[1,1,1,176,512]{4,3,2,1,0:T(8,128)(2,1)S(1)} collective-permute-done((bf16[1,1,1,176,512]{4,3,2,1,0:T(8,128)(2,1)S(1)}, bf16[1,1,1,176,512]{4,3,2,1,0:T(8,128)(2,1)S(1)}, u32[]{:S(2)}, u32[]{:S(2)}) %collective-permute-start.40) | collective-permute-done | bytes 180256 | tf_op jit(solution)/shard_map/ppermute | solution.py:332
  318.5 8.3 %collective-permute-done.42 = bf16[1,2,1,176,512]{4,3,2,1,0:T(8,128)(2,1)S(1)} collective-permute-done((bf16[1,2,1,176,512]{4,3,2,1,0:T(8,128)(2,1)S(1)}, bf16[1,2,1,176,512]{4,3,2,1,0:T(8,128)(2,1)S(1)}, u32[]{:S(2)}, u32[]{:S(2)}) %collective-permute-start.42) | collective-permute-done | bytes 360480 | tf_op jit(solution)/shard_map/ppermute | solution.py:332
  330.5 3.9 %fusion.12 = bf16[512,1024]{1,0:T(8,128)(2,1)} fusion(bf16[512,1024]{1,0:T(8,128)(2,1)S(1)} %copy-done.37, bf16[1024,1024]{1,0:T(8,128)(2,1)S(1)} %copy-done.29, bf16[512,1024]{1,0:T(8,128)(2,1)} %copy-done.40, f32[512]{0:T(512)S(1)} %copy-done.66, f32[512]{0:T(512)S(1)} %copy-done.64, bf16[512,256]{1,0:T(8,128)(2,1)} %collective-permute-done.16, ...), kind=kOutput, calls=%fused_computation.22 | convolution fusion | flops 1082130432 | bytes 6295552 | tf_op jit(solution)/shard_map/dot_general | solution.py:20
  338.5 3.6 %collective-permute-done.48 = f32[2,1024]{1,0:T(2,128)S(1)} collective-permute-done((f32[2,1024]{1,0:T(2,128)S(1)}, f32[2,1024]{1,0:T(2,128)S(1)}, u32[]{:S(2)}, u32[]{:S(2)}) %collective-permute-start.48) | collective-permute-done | bytes 8224 | tf_op jit(solution)/shard_map/ppermute | solution.py:332
  342.6 2.2 fusion.9
  344.8 4.7 %shard_map.122 = (f32[1024,8,128]{2,1,0:T(8,128)}, f32[256,1024]{1,0:T(8,128)}) custom-call(bf16[8,176,512]{2,1,0:T(8,128)(2,1)S(1)} %bitcast.57, bf16[8,176,512]{2,1,0:T(8,128)(2,1)S(1)} %bitcast.55), custom_call_target="tpu_custom_call" | custom-call | bytes 8388608 | tf_op jit(solution)/shard_map/pallas_call | solution.py:273
  (344 shorter events, 107.7 us)
Async XLA Ops:
  7.2 133.1 %all-gather.3.cloned.1.call-start = ((), (), s32[]{:S(2)}) async-start(), calls=%async_computation | async-start | bytes 4325376 | tf_op jit(solution)/shard_map/all_gather | solution.py:418
  21.7 38.7 %collective-permute-start.4 = (bf16[352,1024]{1,0:T(8,128)(2,1)S(1)}, bf16[352,1024]{1,0:T(8,128)(2,1)S(1)}, u32[]{:S(2)}, u32[]{:S(2)}) collective-permute-start(bf16[352,1024]{1,0:T(8,128)(2,1)S(1)} %pad_maximum_fusion.6), channel_id=1, source_target_pairs={{0,2},{1,3},{2,0},{3,1},{4,6},{5,7},{6,4},{7,5},{8,10},{9,11},{10,... | collective-permute-start | bytes 2162696 | tf_op jit(solution)/shard_map/ppermute | solution.py:332
  25.8 29.7 %collective-permute-start.3 = (bf16[256,1024]{1,0:T(8,128)(2,1)S(1)}, bf16[256,1024]{1,0:T(8,128)(2,1)S(1)}, u32[]{:S(2)}, u32[]{:S(2)}) collective-permute-start(bf16[256,1024]{1,0:T(8,128)(2,1)S(1)} %get-tuple-element.81.refs_0_), channel_id=1, source_target_pairs={{0,1},{1,0},{2,3},{3,2},{4,5},{5,4},{6,7},{7,6},{8,9},{9,8},{10,11... | collective-permute-start | bytes 1572872 | tf_op jit(solution)/shard_map/ppermute | solution.py:332
  63.0 18.4 %collective-permute-start.5 = (bf16[256,1024]{1,0:T(8,128)(2,1)S(1)}, bf16[256,1024]{1,0:T(8,128)(2,1)S(1)}, u32[]{:S(2)}, u32[]{:S(2)}) collective-permute-start(bf16[256,1024]{1,0:T(8,128)(2,1)S(1)} %slice.195.refs_2_), channel_id=1, source_target_pairs={{0,1},{1,0},{2,3},{3,2},{4,5},{5,4},{6,7},{7,6},{8,9},{9,8},{10,11... | collective-permute-start | bytes 1572872 | tf_op jit(solution)/shard_map/ppermute | solution.py:332
  82.3 12.8 %collective-permute-start.7 = (bf16[192,1024]{1,0:T(8,128)(2,1)S(1)}, bf16[192,1024]{1,0:T(8,128)(2,1)}, u32[]{:S(2)}, u32[]{:S(2)}) collective-permute-start(bf16[192,1024]{1,0:T(8,128)(2,1)S(1)} %pad_maximum_fusion.9), channel_id=1, source_target_pairs={{0,8},{1,9},{2,10},{3,11},{4,12},{5,13},{6,14},{7,15},{8,0},{9,1},... | collective-permute-start | bytes 1179656 | tf_op jit(solution)/shard_map/ppermute | solution.py:332
  83.6 13.7 %collective-permute-start = (s32[16]{0:T(128)}, s32[16]{0:T(128)}, u32[]{:S(2)}, u32[]{:S(2)}) collective-permute-start(s32[16]{0:T(128)} %bitcast), channel_id=1, source_target_pairs={{0,4},{1,5},{2,6},{3,7},{4,0},{5,1},{6,2},{7,3},{8,12},{9,13},{10,... | collective-permute-start | bytes 200 | tf_op jit(solution)/shard_map/ppermute | solution.py:332
  83.6 25.4 %collective-permute-start.1 = (f32[2]{0:T(128)}, f32[2]{0:T(128)S(1)}, u32[]{:S(2)}, u32[]{:S(2)}) collective-permute-start(f32[2]{0:T(128)} %param.11), channel_id=1, source_target_pairs={{0,0},{1,1},{2,2},{3,3},{4,6},{5,7},{6,4},{7,5},{8,8},{9,9},{10,10... | collective-permute-start | bytes 32 | tf_op jit(solution)/shard_map/ppermute | solution.py:332
  97.3 9.2 %collective-permute-start.8 = (bf16[384,1024]{1,0:T(8,128)(2,1)}, bf16[384,1024]{1,0:T(8,128)(2,1)}, u32[]{:S(2)}, u32[]{:S(2)}) collective-permute-start(bf16[384,1024]{1,0:T(8,128)(2,1)} %pad_maximum_fusion.5), channel_id=1, source_target_pairs={{0,4},{1,5},{2,6},{3,7},{4,0},{5,1},{6,2},{7,3},{8,12},{9,13},{10,... | collective-permute-start | bytes 2359304 | tf_op jit(solution)/shard_map/ppermute | solution.py:332
  132.0 14.2 %collective-permute-start.13 = (bf16[512,256]{1,0:T(8,128)(2,1)}, bf16[512,256]{1,0:T(8,128)(2,1)S(1)}, u32[]{:S(2)}, u32[]{:S(2)}) collective-permute-start(bf16[512,256]{1,0:T(8,128)(2,1)} %get-tuple-element.177), channel_id=1, source_target_pairs={{0,0},{1,1},{2,6},{3,7},{4,2},{5,3},{6,4},{7,5},{8,8},{9,9},{10,14... | collective-permute-start | bytes 786440 | tf_op jit(solution)/shard_map/ppermute | solution.py:332
  133.6 12.6 %collective-permute-start.14 = (bf16[512,256]{1,0:T(8,128)(2,1)}, bf16[512,256]{1,0:T(8,128)(2,1)S(1)}, u32[]{:S(2)}, u32[]{:S(2)}) collective-permute-start(bf16[512,256]{1,0:T(8,128)(2,1)} %get-tuple-element.176), channel_id=1, source_target_pairs={{0,1},{1,0},{2,7},{3,6},{4,3},{5,2},{6,5},{7,4},{8,9},{9,8},{10,15... | collective-permute-start | bytes 786440 | tf_op jit(solution)/shard_map/ppermute | solution.py:332
  135.1 12.7 %collective-permute-start.15 = (bf16[512,256]{1,0:T(8,128)(2,1)}, bf16[512,256]{1,0:T(8,128)(2,1)S(1)}, u32[]{:S(2)}, u32[]{:S(2)}) collective-permute-start(bf16[512,256]{1,0:T(8,128)(2,1)} %get-tuple-element.175), channel_id=1, source_target_pairs={{0,2},{1,3},{2,4},{3,5},{4,0},{5,1},{6,6},{7,7},{8,10},{9,11},{10,... | collective-permute-start | bytes 786440 | tf_op jit(solution)/shard_map/ppermute | solution.py:332
  140.0 11.8 %collective-permute-start.16 = (bf16[512,256]{1,0:T(8,128)(2,1)}, bf16[512,256]{1,0:T(8,128)(2,1)}, u32[]{:S(2)}, u32[]{:S(2)}) collective-permute-start(bf16[512,256]{1,0:T(8,128)(2,1)} %get-tuple-element.174), channel_id=1, source_target_pairs={{0,3},{1,2},{2,5},{3,4},{4,1},{5,0},{6,7},{7,6},{8,11},{9,10},{10,... | collective-permute-start | bytes 786440 | tf_op jit(solution)/shard_map/ppermute | solution.py:332
  165.1 29.3 %collective-permute-start.21 = (bf16[2,4,2,2,1,32,1024]{6,5,1,3,2,4,0:T(8,128)(2,1)}, bf16[2,4,2,2,1,32,1024]{6,5,1,3,2,4,0:T(8,128)(2,1)}, u32[]{:S(2)}, u32[]{:S(2)}) collective-permute-start(bf16[2,4,2,2,1,32,1024]{6,5,1,3,2,4,0:T(8,128)(2,1)} %broadcast_select_fusion), channel_id=1, source_target_pairs={{0,4},{1,5},{2,6},{3,7},{4,0},{5,1},{6,2},{7,3},{8,12},{9,13},{10,... | collective-permute-start | bytes 6291464 | tf_op jit(solution)/shard_map/ppermute | solution.py:332
  171.8 9.8 %collective-permute-start.20 = (bf16[512,256]{1,0:T(8,128)(2,1)S(1)}, bf16[512,256]{1,0:T(8,128)(2,1)S(1)}, u32[]{:S(2)}, u32[]{:S(2)}) collective-permute-start(bf16[512,256]{1,0:T(8,128)(2,1)S(1)} %get-tuple-element.171), channel_id=1, source_target_pairs={{0,5},{1,4},{2,1},{3,0},{4,3},{5,2},{6,7},{7,6},{8,13},{9,12},{10,... | collective-permute-start | bytes 786440 | tf_op jit(solution)/shard_map/ppermute | solution.py:332
  175.7 18.6 %collective-permute-start.19 = (bf16[512,256]{1,0:T(8,128)(2,1)S(1)}, bf16[512,256]{1,0:T(8,128)(2,1)S(1)}, u32[]{:S(2)}, u32[]{:S(2)}) collective-permute-start(bf16[512,256]{1,0:T(8,128)(2,1)S(1)} %get-tuple-element.172), channel_id=1, source_target_pairs={{0,4},{1,5},{2,0},{3,1},{4,2},{5,3},{6,6},{7,7},{8,12},{9,13},{10,... | collective-permute-start | bytes 786440 | tf_op jit(solution)/shard_map/ppermute | solution.py:332
  177.6 16.7 %collective-permute-start.18 = (bf16[512,256]{1,0:T(8,128)(2,1)S(1)}, bf16[512,256]{1,0:T(8,128)(2,1)S(1)}, u32[]{:S(2)}, u32[]{:S(2)}) collective-permute-start(bf16[512,256]{1,0:T(8,128)(2,1)S(1)} %get-tuple-element.173), channel_id=1, source_target_pairs={{0,1},{1,0},{2,5},{3,4},{4,7},{5,6},{6,3},{7,2},{8,9},{9,8},{10,13... | collective-permute-start | bytes 786440 | tf_op jit(solution)/shard_map/ppermute | solution.py:332
  178.6 15.7 %collective-permute-start.17 = (bf16[512,256]{1,0:T(8,128)(2,1)S(1)}, bf16[512,256]{1,0:T(8,128)(2,1)S(1)}, u32[]{:S(2)}, u32[]{:S(2)}) collective-permute-start(bf16[512,256]{1,0:T(8,128)(2,1)S(1)} %get-tuple-element.170), channel_id=1, source_target_pairs={{0,0},{1,1},{2,4},{3,5},{4,6},{5,7},{6,2},{7,3},{8,8},{9,9},{10,12... | collective-permute-start | bytes 786440 | tf_op jit(solution)/shard_map/ppermute | solution.py:332
  198.8 28.6 %collective-permute-start.22 = (bf16[4,1,2,1,32,1024]{5,4,0,2,1,3:T(8,128)(2,1)}, bf16[4,1,2,1,32,1024]{5,4,0,2,1,3:T(8,128)(2,1)}, u32[]{:S(2)}, u32[]{:S(2)}) collective-permute-start(bf16[4,1,2,1,32,1024]{5,4,0,2,1,3:T(8,128)(2,1)} %broadcast_select_fusion.8), channel_id=1, source_target_pairs={{0,8},{1,9},{2,10},{3,11},{4,12},{5,13},{6,14},{7,15},{8,0},{9,1},... | collective-permute-start | bytes 1572872 | tf_op jit(solution)/shard_map/ppermute | solution.py:332
  199.7 29.2 %collective-permute-start.23 = (bf16[4,2,1,1,32,1024]{5,4,0,3,2,1:T(8,128)(2,1)}, bf16[4,2,1,1,32,1024]{5,4,0,3,2,1:T(8,128)(2,1)S(1)}, u32[]{:S(2)}, u32[]{:S(2)}) collective-permute-start(bf16[4,2,1,1,32,1024]{5,4,0,3,2,1:T(8,128)(2,1)} %broadcast_select_fusion.7), channel_id=1, source_target_pairs={{0,16},{1,17},{2,18},{3,19},{4,20},{5,21},{6,22},{7,23},{8,24},{9,... | collective-permute-start | bytes 1572872 | tf_op jit(solution)/shard_map/ppermute | solution.py:332
  232.5 18.2 %collective-permute-start.24 = (bf16[1024,1024]{1,0:T(8,128)(2,1)S(1)}, bf16[1024,1024]{1,0:T(8,128)(2,1)S(1)}, u32[]{:S(2)}, u32[]{:S(2)}) collective-permute-start(bf16[1024,1024]{1,0:T(8,128)(2,1)S(1)} %convolution_convert_fusion.3), channel_id=1, source_target_pairs={{0,4},{1,5},{2,6},{3,7},{4,0},{5,1},{6,2},{7,3},{8,12},{9,13},{10,... | collective-permute-start | bytes 6291464 | tf_op jit(solution)/shard_map/ppermute | solution.py:332
  239.9 9.1 %collective-permute-start.26 = (bf16[4,1,1,1,32,1024]{5,4,0,3,2,1:T(8,128)(2,1)S(1)}, bf16[4,1,1,1,32,1024]{5,4,0,3,2,1:T(8,128)(2,1)S(1)}, u32[]{:S(2)}, u32[]{:S(2)}) collective-permute-start(bf16[4,1,1,1,32,1024]{5,4,0,3,2,1:T(8,128)(2,1)S(1)} %broadcast_select_fusion.25), channel_id=1, source_target_pairs={{0,8},{1,9},{2,10},{3,11},{4,12},{5,13},{6,14},{7,15},{8,0},{9,1},... | collective-permute-start | bytes 786440 | tf_op jit(solution)/shard_map/ppermute | solution.py:332
  250.9 13.3 %collective-permute-start.27 = (bf16[1,2,2,96,512]{4,3,2,1,0:T(8,128)(2,1)S(1)}, bf16[1,2,2,96,512]{4,3,2,1,0:T(8,128)(2,1)S(1)}, u32[]{:S(2)}, u32[]{:S(2)}) collective-permute-start(bf16[1,2,2,96,512]{4,3,2,1,0:T(8,128)(2,1)S(1)} %broadcast_select_fusion.18), channel_id=1, source_target_pairs={{0,8},{1,9},{2,10},{3,11},{4,12},{5,13},{6,14},{7,15},{8,0},{9,1},... | collective-permute-start | bytes 1179656 | tf_op jit(solution)/shard_map/ppermute | solution.py:332
  251.3 14.9 %collective-permute-start.29 = (bf16[2,1,2,96,512]{4,3,2,1,0:T(8,128)(2,1)S(1)}, bf16[2,1,2,96,512]{4,3,2,1,0:T(8,128)(2,1)S(1)}, u32[]{:S(2)}, u32[]{:S(2)}) collective-permute-start(bf16[2,1,2,96,512]{4,3,2,1,0:T(8,128)(2,1)S(1)} %broadcast_select_fusion.17), channel_id=1, source_target_pairs={{0,16},{1,17},{2,18},{3,19},{4,20},{5,21},{6,22},{7,23},{8,24},{9,... | collective-permute-start | bytes 1179656 | tf_op jit(solution)/shard_map/ppermute | solution.py:332
  251.6 12.5 %collective-permute-start.32 = (bf16[2,2,32,1024]{3,2,0,1:T(8,128)(2,1)S(1)}, bf16[2,2,32,1024]{3,2,0,1:T(8,128)(2,1)S(1)}, u32[]{:S(2)}, u32[]{:S(2)}) collective-permute-start(bf16[2,2,32,1024]{3,2,0,1:T(8,128)(2,1)S(1)} %slice.234), channel_id=1, source_target_pairs={{0,2},{1,3},{2,0},{3,1},{4,6},{5,7},{6,4},{7,5},{8,10},{9,11},{10,... | collective-permute-start | bytes 786440 | tf_op jit(solution)/shard_map/ppermute | solution.py:332
  253.4 18.0 %collective-permute-start.31 = (bf16[256,1024]{1,0:T(8,128)(2,1)S(1)}, bf16[256,1024]{1,0:T(8,128)(2,1)S(1)}, u32[]{:S(2)}, u32[]{:S(2)}) collective-permute-start(bf16[256,1024]{1,0:T(8,128)(2,1)S(1)} %slice.268), channel_id=1, source_target_pairs={{0,1},{1,0},{2,3},{3,2},{4,5},{5,4},{6,7},{7,6},{8,9},{9,8},{10,11... | collective-permute-start | bytes 1572872 | tf_op jit(solution)/shard_map/ppermute | solution.py:332
  273.1 22.5 %collective-permute-start.35 = (bf16[256,1024]{1,0:T(8,128)(2,1)S(1)}, bf16[256,1024]{1,0:T(8,128)(2,1)S(1)}, u32[]{:S(2)}, u32[]{:S(2)}) collective-permute-start(bf16[256,1024]{1,0:T(8,128)(2,1)S(1)} %slice.237), channel_id=1, source_target_pairs={{0,1},{1,0},{2,3},{3,2},{4,5},{5,4},{6,7},{7,6},{8,9},{9,8},{10,11... | collective-permute-start | bytes 1572872 | tf_op jit(solution)/shard_map/ppermute | solution.py:332
  273.2 23.4 %collective-permute-start.33 = (bf16[1,1,2,96,1024]{4,3,2,1,0:T(8,128)(2,1)S(1)}, bf16[1,1,2,96,1024]{4,3,2,1,0:T(8,128)(2,1)S(1)}, u32[]{:S(2)}, u32[]{:S(2)}) collective-permute-start(bf16[1,1,2,96,1024]{4,3,2,1,0:T(8,128)(2,1)S(1)} %pad_maximum_fusion.10), channel_id=1, source_target_pairs={{0,0},{1,1},{2,2},{3,3},{4,6},{5,7},{6,4},{7,5},{8,8},{9,9},{10,10... | collective-permute-start | bytes 1179656 | tf_op jit(solution)/shard_map/ppermute | solution.py:332
  274.0 21.6 %collective-permute-start.36 = (bf16[2,1,32,1024]{3,2,0,1:T(8,128)(2,1)S(1)}, bf16[2,1,32,1024]{3,2,0,1:T(8,128)(2,1)S(1)}, u32[]{:S(2)}, u32[]{:S(2)}) collective-permute-start(bf16[2,1,32,1024]{3,2,0,1:T(8,128)(2,1)S(1)} %slice.239), channel_id=1, source_target_pairs={{0,1},{1,0},{2,3},{3,2},{4,5},{5,4},{6,7},{7,6},{8,9},{9,8},{10,11... | collective-permute-start | bytes 393224 | tf_op jit(solution)/shard_map/ppermute | solution.py:332
  276.7 19.9 %collective-permute-start.34 = (bf16[64,1024]{1,0:T(8,128)(2,1)S(1)}, bf16[64,1024]{1,0:T(8,128)(2,1)S(1)}, u32[]{:S(2)}, u32[]{:S(2)}) collective-permute-start(bf16[64,1024]{1,0:T(8,128)(2,1)S(1)} %get-tuple-element.195), channel_id=1, source_target_pairs={{0,2},{1,3},{2,0},{3,1},{4,6},{5,7},{6,4},{7,5},{8,10},{9,11},{10,... | collective-permute-start | bytes 393224 | tf_op jit(solution)/shard_map/ppermute | solution.py:332
  316.5 10.3 %collective-permute-start.42 = (bf16[1,2,1,176,512]{4,3,2,1,0:T(8,128)(2,1)S(1)}, bf16[1,2,1,176,512]{4,3,2,1,0:T(8,128)(2,1)S(1)}, u32[]{:S(2)}, u32[]{:S(2)}) collective-permute-start(bf16[1,2,1,176,512]{4,3,2,1,0:T(8,128)(2,1)S(1)} %pad_maximum_fusion.11), channel_id=1, source_target_pairs={{0,8},{1,9},{2,10},{3,11},{4,12},{5,13},{6,14},{7,15},{8,0},{9,1},... | collective-permute-start | bytes 1081352 | tf_op jit(solution)/shard_map/ppermute | solution.py:332
  316.9 10.1 %collective-permute-start.43 = (bf16[2,1,1,176,512]{4,3,2,1,0:T(8,128)(2,1)S(1)}, bf16[2,1,1,176,512]{4,3,2,1,0:T(8,128)(2,1)S(1)}, u32[]{:S(2)}, u32[]{:S(2)}) collective-permute-start(bf16[2,1,1,176,512]{4,3,2,1,0:T(8,128)(2,1)S(1)} %pad_maximum_fusion.12), channel_id=1, source_target_pairs={{0,16},{1,17},{2,18},{3,19},{4,20},{5,21},{6,22},{7,23},{8,24},{9,... | collective-permute-start | bytes 1081352 | tf_op jit(solution)/shard_map/ppermute | solution.py:332
  318.5 10.3 %collective-permute-start.44 = (bf16[64,1024]{1,0:T(8,128)(2,1)}, bf16[64,1024]{1,0:T(8,128)(2,1)S(1)}, u32[]{:S(2)}, u32[]{:S(2)}) collective-permute-start(bf16[64,1024]{1,0:T(8,128)(2,1)} %get-tuple-element.136), channel_id=1, source_target_pairs={{0,2},{1,3},{2,0},{3,1},{4,6},{5,7},{6,4},{7,5},{8,10},{9,11},{10,... | collective-permute-start | bytes 393224 | tf_op jit(solution)/shard_map/ppermute | solution.py:332
  (89 other events, 556.6 us)
Sparse Core Ops, SparseCore 0:
  18.5 79.6 all-gather.2
where the time goes:
time: 363 us; the launch traced here: 358 us
  waiting for transfers between devices  143 us (39%)
  starting transfers between devices  60.2 us (17%)
  Pallas kernels  54 us (15%)
  other arithmetic  40.8 us (11%)
  local copies, waits for them, and re-layouts  25.4 us (7%)
  matrix products  18.1 us (5%)
  between operations  16.1 us (4%)
    ppermute x50, waiting for transfers between devices, move(): return lax.ppermute(x, AXES, pairs)  143 us
    ppermute x50, starting transfers between devices, move(): return lax.ppermute(x, AXES, pairs)  60.1 us
    pallas_call x1, Pallas kernels, attend_back(): pl.pallas_call(functools.partial(backward_kernel, nh, dim, rows, blocks),...  26 us
    dot_general x7, matrix products, dot(): return lax.dot_general(a, b, dims, preferred_element_type=F32)  18.1 us
    pallas_call x1, Pallas kernels, attend(): pl.pallas_call(functools.partial(forward_kernel, nh, dim, rows, blocks),...  17.6 us
    unnamed x150, local copies, waits for them, and re-layouts  14.9 us
    convert_element_type x13, other arithmetic, add(): return (x.astype(F32) + y.astype(F32)).astype(BF)  7.86 us
  transfers between devices with their start and end apart: 51, of which 26 were waited for; matrix products, arithmetic and copies ran while one was open for 11% of the time, Pallas kernels for 14%

commit v1 on v0

--- a/solution.py
+++ b/solution.py
@@ -58,12 +58,16 @@
     nh, dim, rows, blocks, low, held, sent, slopes, starts_ref, w_ref, *refs
 ):
     pieces = refs[:blocks]
-    out_ref, act_ref, pre_ref, dist, acc = refs[blocks:]
+    out_ref, act_hbm, pre_hbm, dist, acc, act_ref, pre_ref, sems = refs[blocks:]
     for b in range(blocks):
         pre = dot(pieces[b][...], w_ref[...], NT)
         half = 0.5 * pre
         pre_ref[b * rows : (b + 1) * rows, :] = pre.astype(BF)
         act_ref[b * rows : (b + 1) * rows, :] = (half + half * jnp.tanh(half)).astype(BF)
+    act_copy = pltpu.make_async_copy(act_ref, act_hbm, sems.at[0])
+    pre_copy = pltpu.make_async_copy(pre_ref, pre_hbm, sems.at[1])
+    act_copy.start()
+    pre_copy.start()
     fill_distance(dist, blocks, rows)
     scale = dim ** (-0.5)
     part = nh * dim
@@ -91,6 +95,8 @@
         return carry
 
     lax.fori_loop(0, blocks, query_block, 0)
+    act_copy.wait()
+    pre_copy.wait()
 
 
 def backward_kernel(
@@ -171,10 +177,13 @@
         functools.partial(forward_kernel, nh, dim, rows, blocks),
         out_shape=(jax.ShapeDtypeStruct((total, nh * dim), BF), wide, wide),
         in_specs=[smem] * 4 + [vmem] * (2 + blocks),
-        out_specs=(vmem,) * 3,
+        out_specs=(vmem,) + (pl.BlockSpec(memory_space=pl.ANY),) * 2,
         scratch_shapes=[
             pltpu.VMEM((blocks, rows, rows), F32),
             pltpu.VMEM((rows, nh * dim), F32),
+            pltpu.VMEM(wide.shape, BF),
+            pltpu.VMEM(wide.shape, BF),
+            pltpu.SemaphoreType.DMA((2,)),
         ],
         compiler_params=pltpu.CompilerParams(vmem_limit_bytes=40 * 2**20),
         cost_estimate=attention_cost(nh, dim, total, 2),
@@ -248,6 +257,73 @@
             flops=20 * rows * width * columns, bytes_accessed=16 * 2**20, transcendentals=0
         ),
     )(z.reshape(1), everything, normed, cotangent, after)
+
+
+def gate_kernel(n, step, pre_gate_ref, d_gated_ref, normed_ref, cot_ref, *refs):
+    pieces, d_att = refs[:n], refs[n : 2 * n]
+    both_ref, gated_ref, d_pre_gate_ref, dn_ref = refs[2 * n :]
+    rows, width = pre_gate_ref.shape
+    part = width // n
+
+    def some_rows(r, carry):
+        at = pl.ds(pl.multiple_of(r * step, step), step)
+        att = [ref[at, :].astype(F32) for ref in pieces]
+        mean = sum(jnp.sum(x, axis=1, keepdims=True) for x in att) / width
+        square = sum(jnp.sum(x * x, axis=1, keepdims=True) for x in att) / width
+        inv = lax.rsqrt(square - mean * mean + EPSILON)
+        first = jnp.zeros((step, 1), F32)
+        second = jnp.zeros((step, 1), F32)
+        for t in range(n):
+            columns = slice(t * part, (t + 1) * part)
+            normed_o = (att[t] - mean) * inv
+            pre = pre_gate_ref[at, columns]
+            d_gated = d_gated_ref[at, columns]
+            sigma = 0.5 + 0.5 * jnp.tanh(0.5 * pre)
+            gate = (pre * sigma).astype(BF).astype(F32)
+            gated_ref[at, columns] = (normed_o * gate).astype(BF)
+            dn = d_gated * gate
+            first += jnp.sum(dn, axis=1, keepdims=True)
+            second += jnp.sum(dn * normed_o, axis=1, keepdims=True)
+            d_gate = (d_gated * normed_o).astype(BF).astype(F32)
+            slope = sigma * (1.0 + pre * (1.0 - sigma))
+            d_pre_gate_ref[at, columns] = (d_gate * slope).astype(BF)
+            dn_ref[:, columns] = dn
+        first, second = first / width, second / width
+        for t in range(n):
+            columns = slice(t * part, (t + 1) * part)
+            normed_o = (att[t] - mean) * inv
+            dn = dn_ref[:, columns]
+            d_att[t][at, :] = (inv * (dn - first - normed_o * second)).astype(BF)
+        return carry
+
+    lax.fori_loop(0, rows // step, some_rows, 0)
+    for t in range(n):
+        columns = slice(t * part, (t + 1) * part)
+        both_ref[0, columns, :] = dot(d_pre_gate_ref[:, columns], normed_ref[...], TN).astype(BF)
+        both_ref[1, columns, :] = dot(gated_ref[:, columns], cot_ref[...], TN).astype(BF)
+
+
+def gate_and_norm(n, pre_gate, d_gated, normed, cotangent, pieces):
+    rows, width = normed.shape
+    columns = pre_gate.shape[1]
+    vmem = pl.BlockSpec(memory_space=pltpu.VMEM)
+    outs = pl.pallas_call(
+        functools.partial(gate_kernel, n, 64),
+        out_shape=[jax.ShapeDtypeStruct(x.shape, BF) for x in pieces]
+        + [
+            jax.ShapeDtypeStruct((2, columns, width), BF),
+            jax.ShapeDtypeStruct((rows, columns), BF),
+            jax.ShapeDtypeStruct((rows, columns), BF),
+        ],
+        in_specs=[vmem] * (4 + n),
+        out_specs=[vmem] * (n + 3),
+        scratch_shapes=[pltpu.VMEM((64, columns), F32)],
+        compiler_params=pltpu.CompilerParams(vmem_limit_bytes=32 * 2**20),
+        cost_estimate=pl.CostEstimate(
+            flops=8 * rows * width * columns, bytes_accessed=16 * 2**20, transcendentals=0
+        ),
+    )(pre_gate, d_gated, normed, cotangent, *pieces)
+    return list(outs[:n]), outs[n], outs[n + 1], outs[n + 2]
 
 
 def assemble_kernel(nh, dim, n_dp, first_ref, second_ref, in_ref, out_ref, rows_ref):
@@ -386,41 +462,9 @@
         for t in sorted(items):
             items[t ^ bit] = z_swap(items[t], bit)
         bit *= 2
-    items, crossed = barrier((items, crossed))
-    items[half], piece = crossed[:rows], crossed[rows:]
-    bit = 1
-    while bit < half:
-        for t in [t for t in sorted(items) if t >= half]:
-            items[t ^ bit] = z_swap(items[t], bit)
-        bit *= 2
-
-    def dp_double(x, bit):
-        other = dp_swap(x, bit)
-        up = (dp & bit) != 0
-        return jnp.concatenate([jnp.where(up, other, x), jnp.where(up, x, other)], axis=0)
-
-    for b in bits[:1:-1]:
-        piece = dp_double(piece, b)
-    items, piece = barrier((items, piece))
-    for b in bits[1::-1]:
-        piece = dp_double(piece, b)
-    mine = [items[t] for t in range(n)]
-    theirs = [core_swap(x) for x in mine]
-    total = n * local_rows
-
-    slabs = jnp.concatenate(
-        [
-            lax.dynamic_slice_in_dim(gate_rows, dp * slab_o, slab_o, 0),
-            lax.dynamic_slice_in_dim(proj_out.reshape(part, width), dp * slab_o, slab_o, 0),
-        ],
-        axis=0,
-    )
-    everything = lax.all_gather(slabs, AXES).reshape(n_dp, n, 2, slab_o, width)
-
-    w_qkv = jnp.where(c == 0, w_own, piece)
-
     own_lengths = lengths[0]
     hosted_lengths = jnp.where(is_home, own_lengths, core_swap(own_lengths))
+    total = n * local_rows
     ends = jnp.cumsum(hosted_lengths)
     positions = jnp.arange(total, dtype=jnp.int32)
     starts = jnp.max(
@@ -434,6 +478,48 @@
     tables = (low, held, sent)
     slopes = cross(bias_slope)
 
+    items, crossed, tables, starts, slopes = barrier((items, crossed, tables, starts, slopes))
+    piece = crossed[rows:]
+
+    def dp_double(x, bit):
+        other = dp_swap(x, bit)
+        up = (dp & bit) != 0
+        return jnp.concatenate([jnp.where(up, other, x), jnp.where(up, x, other)], axis=0)
+
+    def spread(x):
+        found = {half: x}
+        bit = 1
+        while bit < half:
+            for t in sorted(found):
+                found[t ^ bit] = z_swap(found[t], bit)
+            bit *= 2
+        return found
+
+    middle = rows // 2
+    upper = spread(crossed[:middle])
+    for b in bits[:1:-1]:
+        piece = dp_double(piece, b)
+    upper, piece, lower = barrier((upper, piece, crossed[middle:rows]))
+    lower = spread(lower)
+    piece = dp_double(piece, bits[1])
+    items, upper, lower, piece = barrier((items, upper, lower, piece))
+    piece = dp_double(piece, bits[0])
+    for t in upper:
+        items[t] = jnp.concatenate([upper[t], lower[t]], axis=0)
+    mine = [items[t] for t in range(n)]
+    theirs = [core_swap(x) for x in mine]
+
+    slabs = jnp.concatenate(
+        [
+            lax.dynamic_slice_in_dim(gate_rows, dp * slab_o, slab_o, 0),
+            lax.dynamic_slice_in_dim(proj_out.reshape(part, width), dp * slab_o, slab_o, 0),
+        ],
+        axis=0,
+    )
+    everything = lax.all_gather(slabs, AXES).reshape(n_dp, n, 2, slab_o, width)
+
+    w_qkv = jnp.where(c == 0, w_own, piece)
+
     attended, act, pre = attend(
         nh, dim, rows, tables, slopes, starts, w_qkv, mine + theirs
     )
@@ -447,24 +533,9 @@
     arrived, w_gate, w_out, pre_gate, d_gated = barrier(
         (arrived, w_gate, w_out, pre_gate, d_gated)
     )
-    att_own = jnp.concatenate(arrived, axis=1).astype(F32)
-
-    gate = jax.nn.silu(pre_gate).astype(BF).astype(F32)
-    mean_o = jnp.mean(att_own, axis=1, keepdims=True)
-    square_o = jnp.mean(att_own * att_own, axis=1, keepdims=True)
-    inv_o = lax.rsqrt(square_o - mean_o * mean_o + EPSILON)
-    normed_o = (att_own - mean_o) * inv_o
-    gated = (normed_o * gate).astype(BF)
-    d_norm_in = d_gated * gate
-    first_g = jnp.mean(d_norm_in, axis=1, keepdims=True)
-    second_g = jnp.mean(d_norm_in * normed_o, axis=1, keepdims=True)
-    d_attended = (inv_o * (d_norm_in - first_g - normed_o * second_g)).astype(BF)
-    mixed = (token_single + dot(gated, w_out)).astype(BF)
-    d_gate = (d_gated * normed_o).astype(BF).astype(F32)
-    d_pre_gate = (d_gate * silu_slope(pre_gate)).astype(BF)
-    d_normed_gate = dot(d_pre_gate, w_gate)
-    gate_part = dot(d_pre_gate, normed, TN)
-    out_part = dot(gated, cotangent, TN)
+    d_attended, both, gated, d_pre_gate = gate_and_norm(
+        n, pre_gate, d_gated, normed, cotangent, arrived
+    )
 
     def add(x, y):
         return (x.astype(F32) + y.astype(F32)).astype(BF)
@@ -489,16 +560,13 @@
             [jnp.where(up, other, x), jnp.where(up, x, other)], axis=axis
         )
 
-    both = jnp.stack([gate_part, out_part]).astype(BF)
     both = both.reshape([2, n] + split + [slab_o, width])
-    d_attended, both = barrier((d_attended, both))
     both = reduce_bit(both, 1, 1 + len(bits))
     arrived = [
-        move(d_attended[:, r * part : (r + 1) * part], back_target(r)) for r in range(n)
+        move(d_attended[r], back_target(r)) for r in range(n)
     ]
     d_att = jnp.concatenate(arrived, axis=0)
     pair = [both[0], both[1]]
-    d_att, pair = lax.optimization_barrier((d_att, pair))
     def reduce_pair(pair, k, first_axis):
         return [
             reduce_bit(pair[0], forth[k], first_axis + order.index(forth[k])),
@@ -506,6 +574,11 @@
         ]
 
     both = reduce_pair(pair, 0, 1)
+    mixed = (token_single + dot(gated, w_out)).astype(BF)
+    d_normed_gate = dot(d_pre_gate, w_gate)
+    d_att, both, mixed, d_normed_gate = barrier((d_att, both, mixed, d_normed_gate))
+    for k in range(1, len(forth)):
+        both = reduce_pair(both, k, 1)
 
     d_pre, slope_rows = attend_back(
         nh, dim, rows, tables, slopes, starts, act, pre, d_att
@@ -520,9 +593,8 @@
     d_pre, theirs = barrier((d_pre, theirs))
     in_part = dot(d_pre, gathered, TN).astype(BF)
     mine = partial(0, n)
-    for k in range(1, len(forth)):
-        both = reduce_pair(both, k, 1)
     both = jnp.stack(both).reshape(2, n, slab_o, width)
+    both = add(both[:, :half], z_swap(both[:, half:], half))
     in_part, got, both = barrier((in_part, got, both))
 
     side = width // 2
@@ -535,25 +607,33 @@
     while bit >= 1:
         away = add(away[: bit * rows], z_swap(away[bit * rows :], bit))
         bit //= 2
-    both = add(both[:, :half], z_swap(both[:, half:], half))
+    bit = half // 2
+    while bit >= 1:
+        both = add(both[:, :bit], z_swap(both[:, bit:], bit))
+        bit //= 2
+    both = both.reshape(2 * slab_o, width)
     for k in range(1, len(forth)):
         pair = reduce_pair(pair, k, 0)
     pair, away, home, both = barrier((pair, away, home, both))
 
     cuts = [away[k * rows // 4 : (k + 1) * rows // 4] for k in range(4)]
     moved = [z_swap(cuts[0], half)]
-    bit = half // 2
-    while bit >= 1:
-        home = add(home[: bit * rows], z_swap(home[bit * rows :], bit))
-        both = add(both[:, :bit], z_swap(both[:, bit:], bit))
-        bit //= 2
-    both = both.reshape(2 * slab_o, width)
     x = cross(jnp.concatenate(pair, axis=-1))
     x, moved, home, both, cuts = barrier((x, moved, home, both, cuts))
 
     moved.append(z_swap(cuts[1], half))
     x = reduce_bit(x, 1, len(bits) - 1)
-    x, moved, cuts = barrier((x, moved, cuts))
+    bit = half // 2
+    while bit > 1:
+        home = add(home[: bit * rows], z_swap(home[bit * rows :], bit))
+        bit //= 2
+    homes = [home[:middle]]
+    if bit:
+        homes[0] = add(homes[0], z_swap(home[rows : rows + middle], 1))
+    x, moved, cuts, homes, home = barrier((x, moved, cuts, homes, home))
+    homes.append(home[middle:rows])
+    if bit:
+        homes[1] = add(homes[1], z_swap(home[rows + middle :], 1))
     moved.append(z_swap(cuts[2], half))
     x = x.reshape(slab_w, width)
     place = sum(
@@ -585,7 +665,8 @@
         ]
 
     pair = double_pair([x[..., :side], x[..., side:]], 0)
-    pair, moved, cuts = barrier((pair, moved, cuts))
+    pair, moved, cuts, homes = barrier((pair, moved, cuts, homes))
+    home = jnp.concatenate(homes, axis=0)
     moved.append(z_swap(cuts[3], half))
     for k in range(1, len(forth)):
         pair = double_pair(pair, k)

time: 363 us -> 345 us (0.950)
  waiting for transfers between devices: 143 us -> 125 us
  starting transfers between devices: 60.2 us -> 74.3 us
  other arithmetic: 40.8 us -> 28.3 us
  Pallas kernels: 54 us -> 61.8 us
  matrix products: 18.1 us -> 12 us
    ppermute x50 -> x52, waiting for transfers between devices: 143 us -> 125 us  [move(): return lax.ppermute(x, AXES, pairs)]
    ppermute x50 -> x52, starting transfers between devices: 60.1 us -> 74.2 us  [move(): return lax.ppermute(x, AXES, pairs)]
    pallas_call x0 -> x1, Pallas kernels: none -> 6.5 us  [gate_and_norm(): pl.pallas_call(functools.partial(gate_kernel, n, 64), out_shape=[jax.Shap...]
    dot_general x7 -> x5, matrix products: 18.1 us -> 12 us  [dot(): return lax.dot_general(a, b, dims, preferred_element_type=F32)]
    convert_element_type x13 -> x16, other arithmetic: 7.86 us -> 6.3 us  [add(): return (x.astype(F32) + y.astype(F32)).astype(BF)]
    unnamed x150 -> x100, local copies, waits for them, and re-layouts: 14.9 us -> 14.9 us
  transfers between devices with their start and end apart: 51 -> 53, of which waited for: 26 -> 23; matrix products, arithmetic and copies ran while one was open for 11% -> 11% of each run, Pallas kernels for 14% -> 15%
where the time goes in v1:
time: 345 us; the launch traced here: 341 us
  waiting for transfers between devices  125 us (36%)
  starting transfers between devices  74.3 us (22%)
  Pallas kernels  61.8 us (18%)
  other arithmetic  28.3 us (8%)
  local copies, waits for them, and re-layouts  24 us (7%)
  between operations  15.5 us (4%)
  matrix products  12 us (3%)
    ppermute x52, waiting for transfers between devices, move(): return lax.ppermute(x, AXES, pairs)  125 us
    ppermute x52, starting transfers between devices, move(): return lax.ppermute(x, AXES, pairs)  74.2 us
    pallas_call x1, Pallas kernels, attend_back(): pl.pallas_call(functools.partial(backward_kernel, nh, dim, rows, blocks),...  26 us
    pallas_call x1, Pallas kernels, attend(): pl.pallas_call(functools.partial(forward_kernel, nh, dim, rows, blocks),...  18.9 us
    unnamed x100, local copies, waits for them, and re-layouts  14.9 us
    dot_general x5, matrix products, dot(): return lax.dot_general(a, b, dims, preferred_element_type=F32)  12 us
  transfers between devices with their start and end apart: 53, of which 23 were waited for; matrix products, arithmetic and copies ran while one was open for 11% of the time, Pallas kernels for 15%

profile of v1, /device:TPU:0, one launch (start us, length us, event | category | flops | bytes accessed | tf_op | source)
XLA Modules:
  0.0 341.3 jit_solution(6011900022693631870)
XLA Ops:
  12.5 3.3 shard_map.118
  22.2 4.0 %collective-permute-start.2 = (bf16[352,1024]{1,0:T(8,128)(2,1)}, bf16[352,1024]{1,0:T(8,128)(2,1)}, u32[]{:S(2)}, u32[]{:S(2)}) collective-permute-start(bf16[352,1024]{1,0:T(8,128)(2,1)} %pad_maximum_fusion.4), channel_id=1, source_target_pairs={{0,2},{1,3},{2,0},{3,1},{4,6},{5,7},{6,4},{7,5},{8,10},{9,11},{10,... | collective-permute-start | bytes 2162696 | tf_op jit(solution)/shard_map/ppermute | solution.py:408
  30.6 25.5 %collective-permute-done.1.refs_1_ = bf16[256,1024]{1,0:T(8,128)(2,1)} collective-permute-done((bf16[256,1024]{1,0:T(8,128)(2,1)S(1)}, bf16[256,1024]{1,0:T(8,128)(2,1)}, u32[]{:S(2)}, u32[]{:S(2)}) %collective-permute-start.1) | collective-permute-done | bytes 524320 | tf_op jit(solution)/shard_map/ppermute | solution.py:408
  56.1 5.1 %collective-permute-done.2 = bf16[352,1024]{1,0:T(8,128)(2,1)} collective-permute-done((bf16[352,1024]{1,0:T(8,128)(2,1)}, bf16[352,1024]{1,0:T(8,128)(2,1)}, u32[]{:S(2)}, u32[]{:S(2)}) %collective-permute-start.2) | collective-permute-done | bytes 720928 | tf_op jit(solution)/shard_map/ppermute | solution.py:408
  64.9 2.7 collective-permute-start.5
  69.6 5.5 %collective-permute-done.5 = bf16[128,1024]{1,0:T(8,128)(2,1)S(1)} collective-permute-done((bf16[128,1024]{1,0:T(8,128)(2,1)S(1)}, bf16[128,1024]{1,0:T(8,128)(2,1)S(1)}, u32[]{:S(2)}, u32[]{:S(2)}) %collective-permute-start.5) | collective-permute-done | bytes 262176 | tf_op jit(solution)/shard_map/ppermute | solution.py:408
  77.4 15.7 %collective-permute-done.8 = bf16[192,1024]{1,0:T(8,128)(2,1)S(1)} collective-permute-done((bf16[192,1024]{1,0:T(8,128)(2,1)S(1)}, bf16[192,1024]{1,0:T(8,128)(2,1)S(1)}, u32[]{:S(2)}, u32[]{:S(2)}) %collective-permute-start.8) | collective-permute-done | bytes 393248 | tf_op jit(solution)/shard_map/ppermute | solution.py:408
  103.4 18.9 %shard_map.119 = (bf16[2048,256]{1,0:T(8,128)(2,1)S(1)}, bf16[2048,768]{1,0:T(8,128)(2,1)S(1)}, bf16[2048,768]{1,0:T(8,128)(2,1)S(1)}) custom-call(s32[8]{0:T(128)S(1)} %get-tuple-element.99.low, s32[8]{0:T(128)S(1)} %multiply_add_fusion.1.held, s32[8]{0:T(128)S(1)} %get-tuple-element.101.sent, f32[2]{0:T(128)S(1)} %collective-permute-done.4.slopes, ...), custom_call_target="tpu_custom_call" | custom-call | flops 12884889600 | bytes 4194304 | tf_op jit(solution)/shard_map/pallas_call | solution.py:176
  126.7 2.6 collective-permute-start.17
  132.7 3.7 %collective-permute-start.14 = (bf16[512,256]{1,0:T(8,128)(2,1)}, bf16[512,256]{1,0:T(8,128)(2,1)}, u32[]{:S(2)}, u32[]{:S(2)}) collective-permute-start(bf16[512,256]{1,0:T(8,128)(2,1)} %get-tuple-element.211), channel_id=1, source_target_pairs={{0,0},{1,1},{2,6},{3,7},{4,2},{5,3},{6,4},{7,5},{8,8},{9,9},{10,14... | collective-permute-start | bytes 786440 | tf_op jit(solution)/shard_map/ppermute | solution.py:408
  141.0 3.9 %collective-permute-done.15.refs_1_ = bf16[512,256]{1,0:T(8,128)(2,1)} collective-permute-done((bf16[512,256]{1,0:T(8,128)(2,1)}, bf16[512,256]{1,0:T(8,128)(2,1)}, u32[]{:S(2)}, u32[]{:S(2)}) %collective-permute-start.15) | collective-permute-done | bytes 262176 | tf_op jit(solution)/shard_map/ppermute | solution.py:408
  144.9 6.5 %shard_map.121 = (bf16[512,256]{1,0:T(8,128)(2,1)S(1)}, bf16[512,256]{1,0:T(8,128)(2,1)S(1)}, bf16[512,256]{1,0:T(8,128)(2,1)S(1)}, bf16[512,256]{1,0:T(8,128)(2...) custom-call(f32[512,1024]{1,0:T(8,128)S(1)} %get-tuple-element.124.pre_gat, ...), custom_call_target="tpu_custom_call" | custom-call | flops 4294967296 | bytes 16777216 | tf_op jit(solution)/shard_map/pallas_call | solution.py:310
  151.7 7.8 %collective-permute-start.22 = (bf16[2,4,2,2,1,32,1024]{6,5,4,3,2,1,0:T(8,128)(2,1)S(1)}, bf16[2,4,2,2,1,32,1024]{6,5,4,3,2,1,0:T(8,128)(2,1)S(1)}, u32[]{:S(2)}, u32[]{:S(2)}) collective-permute-start(bf16[2,4,2,2,1,32,1024]{6,5,4,3,2,1,0:T(8,128)(2,1)S(1)} %broadcast_select_fusion), channel_id=1, source_target_pairs={{0,4},{1,5},{2,6},{3,7},{4,0},{5,1},{6,2},{7,3},{8,12},{9,13},{10,... | collective-permute-start | bytes 6291464 | tf_op jit(solution)/shard_map/ppermute | solution.py:408
  160.6 6.1 %collective-permute-start.20 = (bf16[512,256]{1,0:T(8,128)(2,1)S(1)}, bf16[512,256]{1,0:T(8,128)(2,1)S(1)}, u32[]{:S(2)}, u32[]{:S(2)}) collective-permute-start(bf16[512,256]{1,0:T(8,128)(2,1)S(1)} %get-tuple-element.132), channel_id=1, source_target_pairs={{0,4},{1,5},{2,0},{3,1},{4,2},{5,3},{6,6},{7,7},{8,12},{9,13},{10,... | collective-permute-start | bytes 786440 | tf_op jit(solution)/shard_map/ppermute | solution.py:408
  172.4 2.5 collective-permute-start.23
  174.9 2.6 fusion.24
  177.5 7.6 %collective-permute-done.20 = bf16[512,256]{1,0:T(8,128)(2,1)S(1)} collective-permute-done((bf16[512,256]{1,0:T(8,128)(2,1)S(1)}, bf16[512,256]{1,0:T(8,128)(2,1)S(1)}, u32[]{:S(2)}, u32[]{:S(2)}) %collective-permute-start.20) | collective-permute-done | bytes 262176 | tf_op jit(solution)/shard_map/ppermute | solution.py:408
  190.2 26.0 %shard_map.122 = (bf16[2048,768]{1,0:T(8,128)(2,1)S(1)}, f32[2,8,256]{2,1,0:T(8,128)S(1)}) custom-call(s32[8]{0:T(128)S(1)} %get-tuple-element.99.low, s32[8]{0:T(128)S(1)} %multiply_add_fusion.1.held, s32[8]{0:T(128)S(1)} %get-tuple-element.101.sent, f32[2]{0:T(128)S(1)} %collective-permute-done.4.slopes, s32[2048,1]{1,0:T(8,128)S(1)} %copy-done.3, ...), custom_call_target="tpu_custom_call" | custom-call | flops 32212224000 | bytes 10485760 | tf_op jit(solution)/shard_map/pallas_call | solution.py:368
  220.9 2.6 collective-permute-start.28
  223.5 3.5 %convolution_convert_fusion.2 = bf16[768,1024]{1,0:T(8,128)(2,1)S(1)} fusion(bf16[2048,768]{1,0:T(8,128)(2,1)S(1)} %get-tuple-element.147, bf16[2048,1024]{1,0:T(8,128)(2,1)S(1)} %constant_dynamic-update-slice_fusion.4), kind=kOutput, calls=%fused_computation.22 | convolution fusion | flops 3222011904 | bytes 8912896 | tf_op jit(solution)/shard_map/dot_general | solution.py:20
  228.8 6.6 %collective-permute-done.28 = bf16[2,2,32,1024]{3,2,1,0:T(8,128)(2,1)S(1)} collective-permute-done((bf16[2,2,32,1024]{3,2,1,0:T(8,128)(2,1)S(1)}, bf16[2,2,32,1024]{3,2,1,0:T(8,128)(2,1)S(1)}, u32[]{:S(2)}, u32[]{:S(2)}) %collective-permute-start.28) | collective-permute-done | bytes 262176 | tf_op jit(solution)/shard_map/ppermute | solution.py:408
  241.6 3.9 %collective-permute-done.29 = bf16[1,2,2,96,512]{4,3,2,1,0:T(8,128)(2,1)S(1)} collective-permute-done((bf16[1,2,2,96,512]{4,3,2,1,0:T(8,128)(2,1)S(1)}, bf16[1,2,2,96,512]{4,3,2,1,0:T(8,128)(2,1)S(1)}, u32[]{:S(2)}, u32[]{:S(2)}) %collective-permute-start.29) | collective-permute-done | bytes 393248 | tf_op jit(solution)/shard_map/ppermute | solution.py:408
  245.7 2.8 collective-permute-start.30
  249.1 3.7 %collective-permute-done.33 = bf16[256,1024]{1,0:T(8,128)(2,1)S(1)} collective-permute-done((bf16[256,1024]{1,0:T(8,128)(2,1)S(1)}, bf16[256,1024]{1,0:T(8,128)(2,1)S(1)}, u32[]{:S(2)}, u32[]{:S(2)}) %collective-permute-start.33) | collective-permute-done | bytes 524320 | tf_op jit(solution)/shard_map/ppermute | solution.py:408
  257.9 11.9 %collective-permute-done.36 = bf16[64,1024]{1,0:T(8,128)(2,1)S(1)} collective-permute-done((bf16[64,1024]{1,0:T(8,128)(2,1)S(1)}, bf16[64,1024]{1,0:T(8,128)(2,1)S(1)}, u32[]{:S(2)}, u32[]{:S(2)}) %collective-permute-start.36) | collective-permute-done | bytes 131104 | tf_op jit(solution)/shard_map/ppermute | solution.py:408
  269.8 3.1 collective-permute-start.37
  275.9 8.7 %collective-permute-done.39 = bf16[128,1024]{1,0:T(8,128)(2,1)S(1)} collective-permute-done((bf16[128,1024]{1,0:T(8,128)(2,1)S(1)}, bf16[128,1024]{1,0:T(8,128)(2,1)S(1)}, u32[]{:S(2)}, u32[]{:S(2)}) %collective-permute-start.39) | collective-permute-done | bytes 262176 | tf_op jit(solution)/shard_map/ppermute | solution.py:408
  289.6 3.1 collective-permute-done.41
  293.4 5.8 %collective-permute-done.43 = bf16[128,1024]{1,0:T(8,128)(2,1)S(1)} collective-permute-done((bf16[128,1024]{1,0:T(8,128)(2,1)S(1)}, bf16[128,1024]{1,0:T(8,128)(2,1)S(1)}, u32[]{:S(2)}, u32[]{:S(2)}) %collective-permute-start.43) | collective-permute-done | bytes 262176 | tf_op jit(solution)/shard_map/ppermute | solution.py:408
  302.2 6.3 %collective-permute-done.44 = bf16[1,2,1,176,512]{4,3,2,1,0:T(8,128)(2,1)S(1)} collective-permute-done((bf16[1,2,1,176,512]{4,3,2,1,0:T(8,128)(2,1)S(1)}, bf16[1,2,1,176,512]{4,3,2,1,0:T(8,128)(2,1)S(1)}, u32[]{:S(2)}, u32[]{:S(2)}) %collective-permute-start.44) | collective-permute-done | bytes 360480 | tf_op jit(solution)/shard_map/ppermute | solution.py:408
  323.3 2.7 collective-permute-start.51
  328.2 4.7 %shard_map.123 = (f32[1024,8,128]{2,1,0:T(8,128)}, f32[256,1024]{1,0:T(8,128)}) custom-call(bf16[8,176,512]{2,1,0:T(8,128)(2,1)S(1)} %bitcast.51, bf16[8,176,512]{2,1,0:T(8,128)(2,1)S(1)} %bitcast.53), custom_call_target="tpu_custom_call" | custom-call | bytes 8388608 | tf_op jit(solution)/shard_map/pallas_call | solution.py:349
  (291 shorter events, 106.4 us)
Async XLA Ops:
  7.2 129.3 %all-gather.3.cloned.1.call-start = ((), (), s32[]{:S(2)}) async-start(), calls=%async_computation | async-start | bytes 4325376 | tf_op jit(solution)/shard_map/all_gather | solution.py:519
  22.2 39.0 %collective-permute-start.2 = (bf16[352,1024]{1,0:T(8,128)(2,1)}, bf16[352,1024]{1,0:T(8,128)(2,1)}, u32[]{:S(2)}, u32[]{:S(2)}) collective-permute-start(bf16[352,1024]{1,0:T(8,128)(2,1)} %pad_maximum_fusion.4), channel_id=1, source_target_pairs={{0,2},{1,3},{2,0},{3,1},{4,6},{5,7},{6,4},{7,5},{8,10},{9,11},{10,... | collective-permute-start | bytes 2162696 | tf_op jit(solution)/shard_map/ppermute | solution.py:408
  28.5 27.6 %collective-permute-start.1 = (bf16[256,1024]{1,0:T(8,128)(2,1)S(1)}, bf16[256,1024]{1,0:T(8,128)(2,1)}, u32[]{:S(2)}, u32[]{:S(2)}) collective-permute-start(bf16[256,1024]{1,0:T(8,128)(2,1)S(1)} %get-tuple-element.112.refs_0_), channel_id=1, source_target_pairs={{0,1},{1,0},{2,3},{3,2},{4,5},{5,4},{6,7},{7,6},{8,9},{9,8},{10,11... | collective-permute-start | bytes 1572872 | tf_op jit(solution)/shard_map/ppermute | solution.py:408
  64.9 10.2 %collective-permute-start.5 = (bf16[128,1024]{1,0:T(8,128)(2,1)S(1)}, bf16[128,1024]{1,0:T(8,128)(2,1)S(1)}, u32[]{:S(2)}, u32[]{:S(2)}) collective-permute-start(bf16[128,1024]{1,0:T(8,128)(2,1)S(1)} %get-tuple-element.114), channel_id=1, source_target_pairs={{0,1},{1,0},{2,3},{3,2},{4,5},{5,4},{6,7},{7,6},{8,9},{9,8},{10,11... | collective-permute-start | bytes 786440 | tf_op jit(solution)/shard_map/ppermute | solution.py:408
  75.1 18.0 %collective-permute-start.8 = (bf16[192,1024]{1,0:T(8,128)(2,1)S(1)}, bf16[192,1024]{1,0:T(8,128)(2,1)S(1)}, u32[]{:S(2)}, u32[]{:S(2)}) collective-permute-start(bf16[192,1024]{1,0:T(8,128)(2,1)S(1)} %pad_maximum_fusion.7), channel_id=1, source_target_pairs={{0,8},{1,9},{2,10},{3,11},{4,12},{5,13},{6,14},{7,15},{8,0},{9,1},... | collective-permute-start | bytes 1179656 | tf_op jit(solution)/shard_map/ppermute | solution.py:408
  76.6 17.5 %collective-permute-start.7 = (bf16[128,1024]{1,0:T(8,128)(2,1)S(1)}, bf16[128,1024]{1,0:T(8,128)(2,1)S(1)}, u32[]{:S(2)}, u32[]{:S(2)}) collective-permute-start(bf16[128,1024]{1,0:T(8,128)(2,1)S(1)} %get-tuple-element.115), channel_id=1, source_target_pairs={{0,1},{1,0},{2,3},{3,2},{4,5},{5,4},{6,7},{7,6},{8,9},{9,8},{10,11... | collective-permute-start | bytes 786440 | tf_op jit(solution)/shard_map/ppermute | solution.py:408
  126.7 14.3 %collective-permute-start.17 = (bf16[512,256]{1,0:T(8,128)(2,1)}, bf16[512,256]{1,0:T(8,128)(2,1)S(1)}, u32[]{:S(2)}, u32[]{:S(2)}) collective-permute-start(bf16[512,256]{1,0:T(8,128)(2,1)} %get-tuple-element.208), channel_id=1, source_target_pairs={{0,3},{1,2},{2,5},{3,4},{4,1},{5,0},{6,7},{7,6},{8,11},{9,10},{10,... | collective-permute-start | bytes 786440 | tf_op jit(solution)/shard_map/ppermute | solution.py:408
  129.3 11.7 %collective-permute-start.16 = (bf16[512,256]{1,0:T(8,128)(2,1)}, bf16[512,256]{1,0:T(8,128)(2,1)}, u32[]{:S(2)}, u32[]{:S(2)}) collective-permute-start(bf16[512,256]{1,0:T(8,128)(2,1)} %get-tuple-element.209), channel_id=1, source_target_pairs={{0,2},{1,3},{2,4},{3,5},{4,0},{5,1},{6,6},{7,7},{8,10},{9,11},{10,... | collective-permute-start | bytes 786440 | tf_op jit(solution)/shard_map/ppermute | solution.py:408
  131.2 13.7 %collective-permute-start.15 = (bf16[512,256]{1,0:T(8,128)(2,1)}, bf16[512,256]{1,0:T(8,128)(2,1)}, u32[]{:S(2)}, u32[]{:S(2)}) collective-permute-start(bf16[512,256]{1,0:T(8,128)(2,1)} %get-tuple-element.210), channel_id=1, source_target_pairs={{0,1},{1,0},{2,7},{3,6},{4,3},{5,2},{6,5},{7,4},{8,9},{9,8},{10,15... | collective-permute-start | bytes 786440 | tf_op jit(solution)/shard_map/ppermute | solution.py:408
  132.7 12.2 %collective-permute-start.14 = (bf16[512,256]{1,0:T(8,128)(2,1)}, bf16[512,256]{1,0:T(8,128)(2,1)}, u32[]{:S(2)}, u32[]{:S(2)}) collective-permute-start(bf16[512,256]{1,0:T(8,128)(2,1)} %get-tuple-element.211), channel_id=1, source_target_pairs={{0,0},{1,1},{2,6},{3,7},{4,2},{5,3},{6,4},{7,5},{8,8},{9,9},{10,14... | collective-permute-start | bytes 786440 | tf_op jit(solution)/shard_map/ppermute | solution.py:408
  151.7 17.7 %collective-permute-start.22 = (bf16[2,4,2,2,1,32,1024]{6,5,4,3,2,1,0:T(8,128)(2,1)S(1)}, bf16[2,4,2,2,1,32,1024]{6,5,4,3,2,1,0:T(8,128)(2,1)S(1)}, u32[]{:S(2)}, u32[]{:S(2)}) collective-permute-start(bf16[2,4,2,2,1,32,1024]{6,5,4,3,2,1,0:T(8,128)(2,1)S(1)} %broadcast_select_fusion), channel_id=1, source_target_pairs={{0,4},{1,5},{2,6},{3,7},{4,0},{5,1},{6,2},{7,3},{8,12},{9,13},{10,... | collective-permute-start | bytes 6291464 | tf_op jit(solution)/shard_map/ppermute | solution.py:408
  159.5 12.9 %collective-permute-start.18 = (bf16[512,256]{1,0:T(8,128)(2,1)S(1)}, bf16[512,256]{1,0:T(8,128)(2,1)S(1)}, u32[]{:S(2)}, u32[]{:S(2)}) collective-permute-start(bf16[512,256]{1,0:T(8,128)(2,1)S(1)} %get-tuple-element.130), channel_id=1, source_target_pairs={{0,0},{1,1},{2,4},{3,5},{4,6},{5,7},{6,2},{7,3},{8,8},{9,9},{10,12... | collective-permute-start | bytes 786440 | tf_op jit(solution)/shard_map/ppermute | solution.py:408
  160.1 17.4 %collective-permute-start.19 = (bf16[512,256]{1,0:T(8,128)(2,1)S(1)}, bf16[512,256]{1,0:T(8,128)(2,1)S(1)}, u32[]{:S(2)}, u32[]{:S(2)}) collective-permute-start(bf16[512,256]{1,0:T(8,128)(2,1)S(1)} %get-tuple-element.131), channel_id=1, source_target_pairs={{0,1},{1,0},{2,5},{3,4},{4,7},{5,6},{6,3},{7,2},{8,9},{9,8},{10,13... | collective-permute-start | bytes 786440 | tf_op jit(solution)/shard_map/ppermute | solution.py:408
  160.6 24.5 %collective-permute-start.20 = (bf16[512,256]{1,0:T(8,128)(2,1)S(1)}, bf16[512,256]{1,0:T(8,128)(2,1)S(1)}, u32[]{:S(2)}, u32[]{:S(2)}) collective-permute-start(bf16[512,256]{1,0:T(8,128)(2,1)S(1)} %get-tuple-element.132), channel_id=1, source_target_pairs={{0,4},{1,5},{2,0},{3,1},{4,2},{5,3},{6,6},{7,7},{8,12},{9,13},{10,... | collective-permute-start | bytes 786440 | tf_op jit(solution)/shard_map/ppermute | solution.py:408
  166.7 18.4 %collective-permute-start.21 = (bf16[512,256]{1,0:T(8,128)(2,1)S(1)}, bf16[512,256]{1,0:T(8,128)(2,1)S(1)}, u32[]{:S(2)}, u32[]{:S(2)}) collective-permute-start(bf16[512,256]{1,0:T(8,128)(2,1)S(1)} %get-tuple-element.133), channel_id=1, source_target_pairs={{0,5},{1,4},{2,1},{3,0},{4,3},{5,2},{6,7},{7,6},{8,13},{9,12},{10,... | collective-permute-start | bytes 786440 | tf_op jit(solution)/shard_map/ppermute | solution.py:408
  171.5 14.6 %collective-permute-start.24 = (bf16[4,2,1,1,32,1024]{5,4,2,1,0,3:T(8,128)(2,1)S(1)}, bf16[4,2,1,1,32,1024]{5,4,2,1,0,3:T(8,128)(2,1)S(1)}, u32[]{:S(2)}, u32[]{:S(2)}) collective-permute-start(bf16[4,2,1,1,32,1024]{5,4,2,1,0,3:T(8,128)(2,1)S(1)} %broadcast_select_fusion.7), channel_id=1, source_target_pairs={{0,16},{1,17},{2,18},{3,19},{4,20},{5,21},{6,22},{7,23},{8,24},{9,... | collective-permute-start | bytes 1572872 | tf_op jit(solution)/shard_map/ppermute | solution.py:408
  172.4 15.2 %collective-permute-start.23 = (bf16[4,1,2,1,32,1024]{5,4,0,3,2,1:T(8,128)(2,1)S(1)}, bf16[4,1,2,1,32,1024]{5,4,0,3,2,1:T(8,128)(2,1)S(1)}, u32[]{:S(2)}, u32[]{:S(2)}) collective-permute-start(bf16[4,1,2,1,32,1024]{5,4,0,3,2,1:T(8,128)(2,1)S(1)} %broadcast_select_fusion.8), channel_id=1, source_target_pairs={{0,8},{1,9},{2,10},{3,11},{4,12},{5,13},{6,14},{7,15},{8,0},{9,1},... | collective-permute-start | bytes 1572872 | tf_op jit(solution)/shard_map/ppermute | solution.py:408
  188.0 28.3 %collective-permute-start.26 = (bf16[4,1,1,1,32,1024]{5,4,2,1,0,3:T(8,128)(2,1)S(1)}, bf16[4,1,1,1,32,1024]{5,4,2,1,0,3:T(8,128)(2,1)S(1)}, u32[]{:S(2)}, u32[]{:S(2)}) collective-permute-start(bf16[4,1,1,1,32,1024]{5,4,2,1,0,3:T(8,128)(2,1)S(1)} %broadcast_select_fusion.25), channel_id=1, source_target_pairs={{0,8},{1,9},{2,10},{3,11},{4,12},{5,13},{6,14},{7,15},{8,0},{9,1},... | collective-permute-start | bytes 786440 | tf_op jit(solution)/shard_map/ppermute | solution.py:408
  189.9 26.4 %collective-permute-start.25 = (bf16[4,1,1,1,32,1024]{5,4,0,3,2,1:T(8,128)(2,1)S(1)}, bf16[4,1,1,1,32,1024]{5,4,0,3,2,1:T(8,128)(2,1)S(1)}, u32[]{:S(2)}, u32[]{:S(2)}) collective-permute-start(bf16[4,1,1,1,32,1024]{5,4,0,3,2,1:T(8,128)(2,1)S(1)} %broadcast_select_fusion.26), channel_id=1, source_target_pairs={{0,16},{1,17},{2,18},{3,19},{4,20},{5,21},{6,22},{7,23},{8,24},{9,... | collective-permute-start | bytes 786440 | tf_op jit(solution)/shard_map/ppermute | solution.py:408
  219.4 16.0 %collective-permute-start.27 = (bf16[1024,1024]{1,0:T(8,128)(2,1)S(1)}, bf16[1024,1024]{1,0:T(8,128)(2,1)S(1)}, u32[]{:S(2)}, u32[]{:S(2)}) collective-permute-start(bf16[1024,1024]{1,0:T(8,128)(2,1)S(1)} %convolution_convert_fusion.1), channel_id=1, source_target_pairs={{0,4},{1,5},{2,6},{3,7},{4,0},{5,1},{6,2},{7,3},{8,12},{9,13},{10,... | collective-permute-start | bytes 6291464 | tf_op jit(solution)/shard_map/ppermute | solution.py:408
  220.9 14.4 %collective-permute-start.28 = (bf16[2,2,32,1024]{3,2,1,0:T(8,128)(2,1)S(1)}, bf16[2,2,32,1024]{3,2,1,0:T(8,128)(2,1)S(1)}, u32[]{:S(2)}, u32[]{:S(2)}) collective-permute-start(bf16[2,2,32,1024]{3,2,1,0:T(8,128)(2,1)S(1)} %slice.261), channel_id=1, source_target_pairs={{0,2},{1,3},{2,0},{3,1},{4,6},{5,7},{6,4},{7,5},{8,10},{9,11},{10,... | collective-permute-start | bytes 786440 | tf_op jit(solution)/shard_map/ppermute | solution.py:408
  235.7 9.8 %collective-permute-start.29 = (bf16[1,2,2,96,512]{4,3,2,1,0:T(8,128)(2,1)S(1)}, bf16[1,2,2,96,512]{4,3,2,1,0:T(8,128)(2,1)S(1)}, u32[]{:S(2)}, u32[]{:S(2)}) collective-permute-start(bf16[1,2,2,96,512]{4,3,2,1,0:T(8,128)(2,1)S(1)} %broadcast_select_fusion.18), channel_id=1, source_target_pairs={{0,8},{1,9},{2,10},{3,11},{4,12},{5,13},{6,14},{7,15},{8,0},{9,1},... | collective-permute-start | bytes 1179656 | tf_op jit(solution)/shard_map/ppermute | solution.py:408
  235.7 12.8 %collective-permute-start.31 = (bf16[2,1,2,96,512]{4,3,2,1,0:T(8,128)(2,1)S(1)}, bf16[2,1,2,96,512]{4,3,2,1,0:T(8,128)(2,1)S(1)}, u32[]{:S(2)}, u32[]{:S(2)}) collective-permute-start(bf16[2,1,2,96,512]{4,3,2,1,0:T(8,128)(2,1)S(1)} %broadcast_select_fusion.17), channel_id=1, source_target_pairs={{0,16},{1,17},{2,18},{3,19},{4,20},{5,21},{6,22},{7,23},{8,24},{9,... | collective-permute-start | bytes 1179656 | tf_op jit(solution)/shard_map/ppermute | solution.py:408
  239.5 13.4 %collective-permute-start.33 = (bf16[256,1024]{1,0:T(8,128)(2,1)S(1)}, bf16[256,1024]{1,0:T(8,128)(2,1)S(1)}, u32[]{:S(2)}, u32[]{:S(2)}) collective-permute-start(bf16[256,1024]{1,0:T(8,128)(2,1)S(1)} %slice.272), channel_id=1, source_target_pairs={{0,1},{1,0},{2,3},{3,2},{4,5},{5,4},{6,7},{7,6},{8,9},{9,8},{10,11... | collective-permute-start | bytes 1572872 | tf_op jit(solution)/shard_map/ppermute | solution.py:408
  255.4 14.4 %collective-permute-start.35 = (bf16[1,1,2,96,1024]{4,3,2,1,0:T(8,128)(2,1)}, bf16[1,1,2,96,1024]{4,3,2,1,0:T(8,128)(2,1)S(1)}, u32[]{:S(2)}, u32[]{:S(2)}) collective-permute-start(bf16[1,1,2,96,1024]{4,3,2,1,0:T(8,128)(2,1)} %pad_maximum_fusion.8), channel_id=1, source_target_pairs={{0,0},{1,1},{2,2},{3,3},{4,6},{5,7},{6,4},{7,5},{8,8},{9,9},{10,10... | collective-permute-start | bytes 1179656 | tf_op jit(solution)/shard_map/ppermute | solution.py:408
  257.8 12.0 %collective-permute-start.36 = (bf16[64,1024]{1,0:T(8,128)(2,1)S(1)}, bf16[64,1024]{1,0:T(8,128)(2,1)S(1)}, u32[]{:S(2)}, u32[]{:S(2)}) collective-permute-start(bf16[64,1024]{1,0:T(8,128)(2,1)S(1)} %get-tuple-element.231), channel_id=1, source_target_pairs={{0,2},{1,3},{2,0},{3,1},{4,6},{5,7},{6,4},{7,5},{8,10},{9,11},{10,... | collective-permute-start | bytes 393224 | tf_op jit(solution)/shard_map/ppermute | solution.py:408
  273.0 11.6 %collective-permute-start.39 = (bf16[128,1024]{1,0:T(8,128)(2,1)S(1)}, bf16[128,1024]{1,0:T(8,128)(2,1)S(1)}, u32[]{:S(2)}, u32[]{:S(2)}) collective-permute-start(bf16[128,1024]{1,0:T(8,128)(2,1)S(1)} %slice.238), channel_id=1, source_target_pairs={{0,1},{1,0},{2,3},{3,2},{4,5},{5,4},{6,7},{7,6},{8,9},{9,8},{10,11... | collective-permute-start | bytes 786440 | tf_op jit(solution)/shard_map/ppermute | solution.py:408
  273.2 11.5 %collective-permute-start.38 = (bf16[64,1024]{1,0:T(8,128)(2,1)}, bf16[64,1024]{1,0:T(8,128)(2,1)S(1)}, u32[]{:S(2)}, u32[]{:S(2)}) collective-permute-start(bf16[64,1024]{1,0:T(8,128)(2,1)} %get-tuple-element.160), channel_id=1, source_target_pairs={{0,2},{1,3},{2,0},{3,1},{4,6},{5,7},{6,4},{7,5},{8,10},{9,11},{10,... | collective-permute-start | bytes 393224 | tf_op jit(solution)/shard_map/ppermute | solution.py:408
  287.9 11.4 %collective-permute-start.42 = (bf16[64,1024]{1,0:T(8,128)(2,1)}, bf16[64,1024]{1,0:T(8,128)(2,1)S(1)}, u32[]{:S(2)}, u32[]{:S(2)}) collective-permute-start(bf16[64,1024]{1,0:T(8,128)(2,1)} %get-tuple-element.169), channel_id=1, source_target_pairs={{0,2},{1,3},{2,0},{3,1},{4,6},{5,7},{6,4},{7,5},{8,10},{9,11},{10,... | collective-permute-start | bytes 393224 | tf_op jit(solution)/shard_map/ppermute | solution.py:408
  289.0 10.2 %collective-permute-start.43 = (bf16[128,1024]{1,0:T(8,128)(2,1)S(1)}, bf16[128,1024]{1,0:T(8,128)(2,1)S(1)}, u32[]{:S(2)}, u32[]{:S(2)}) collective-permute-start(bf16[128,1024]{1,0:T(8,128)(2,1)S(1)} %slice.243), channel_id=1, source_target_pairs={{0,1},{1,0},{2,3},{3,2},{4,5},{5,4},{6,7},{7,6},{8,9},{9,8},{10,11... | collective-permute-start | bytes 786440 | tf_op jit(solution)/shard_map/ppermute | solution.py:408
  300.8 10.9 %collective-permute-start.46 = (bf16[64,1024]{1,0:T(8,128)(2,1)S(1)}, bf16[64,1024]{1,0:T(8,128)(2,1)S(1)}, u32[]{:S(2)}, u32[]{:S(2)}) collective-permute-start(bf16[64,1024]{1,0:T(8,128)(2,1)S(1)} %copy-done.37), channel_id=1, source_target_pairs={{0,2},{1,3},{2,0},{3,1},{4,6},{5,7},{6,4},{7,5},{8,10},{9,11},{10,... | collective-permute-start | bytes 393224 | tf_op jit(solution)/shard_map/ppermute | solution.py:408
  323.3 9.7 %collective-permute-start.51 = (f32[2,1024]{1,0:T(2,128)S(1)}, f32[2,1024]{1,0:T(2,128)S(1)}, u32[]{:S(2)}, u32[]{:S(2)}) collective-permute-start(f32[2,1024]{1,0:T(2,128)S(1)} %fusion.33), channel_id=1, source_target_pairs={{0,2},{1,3},{2,0},{3,1},{4,6},{5,7},{6,4},{7,5},{8,10},{9,11},{10,... | collective-permute-start | bytes 24584 | tf_op jit(solution)/shard_map/ppermute | solution.py:408
  (64 other events, 402.1 us)
Sparse Core Ops, SparseCore 0:
  18.1 83.9 all-gather.2

commit v2 on v1

--- a/solution.py
+++ b/solution.py
@@ -177,7 +177,7 @@
         functools.partial(forward_kernel, nh, dim, rows, blocks),
         out_shape=(jax.ShapeDtypeStruct((total, nh * dim), BF), wide, wide),
         in_specs=[smem] * 4 + [vmem] * (2 + blocks),
-        out_specs=(vmem,) + (pl.BlockSpec(memory_space=pl.ANY),) * 2,
+        out_specs=(vmem,) + (pl.BlockSpec(memory_space=pltpu.HBM),) * 2,
         scratch_shapes=[
             pltpu.VMEM((blocks, rows, rows), F32),
             pltpu.VMEM((rows, nh * dim), F32),
@@ -356,7 +356,9 @@
         out_specs=(vmem,) * 2,
         scratch_shapes=[pltpu.VMEM((4 * nh * dim, width), F32)],
         compiler_params=pltpu.CompilerParams(vmem_limit_bytes=40 * 2**20),
-        cost_estimate=pl.CostEstimate(flops=0, bytes_accessed=8 * 2**20, transcendentals=0),
+        cost_estimate=pl.CostEstimate(
+            flops=10**10, bytes_accessed=8 * 2**20, transcendentals=0
+        ),
     )(first, second)
 
 
@@ -454,9 +456,8 @@
     )
     w_slab = lax.dynamic_slice_in_dim(w_own, mirrored * slab_w, slab_w, 0)
     items = {0: jnp.where(is_home, keep, got)}
-    crossed = z_swap(
-        jnp.concatenate([jnp.where(is_home, got, keep), w_slab], axis=0), half
-    )
+    crossed = z_swap(jnp.where(is_home, got, keep), half)
+    piece = z_swap(w_slab, half)
     bit = 1
     while bit < half:
         for t in sorted(items):
@@ -478,13 +479,27 @@
     tables = (low, held, sent)
     slopes = cross(bias_slope)
 
-    items, crossed, tables, starts, slopes = barrier((items, crossed, tables, starts, slopes))
-    piece = crossed[rows:]
-
-    def dp_double(x, bit):
+    items, crossed, piece, tables, starts, slopes = barrier(
+        (items, crossed, piece, tables, starts, slopes)
+    )
+
+    def dp_double(x, bit, axis):
         other = dp_swap(x, bit)
         up = (dp & bit) != 0
-        return jnp.concatenate([jnp.where(up, other, x), jnp.where(up, x, other)], axis=0)
+        return jnp.concatenate(
+            [jnp.where(up, other, x), jnp.where(up, x, other)], axis=axis
+        )
+
+    side = width // 2
+    pair = [piece[:, :side], piece[:, side:]]
+    pair = [x.reshape([1] * len(bits) + [slab_w, side]) for x in pair]
+
+    def weights_step(pair, k):
+        there, here = bits[:0:-1], bits[1:]
+        return [
+            dp_double(pair[0], there[k], bits.index(there[k])),
+            dp_double(pair[1], here[k], bits.index(here[k])),
+        ]
 
     def spread(x):
         found = {half: x}
@@ -497,13 +512,14 @@
 
     middle = rows // 2
     upper = spread(crossed[:middle])
-    for b in bits[:1:-1]:
-        piece = dp_double(piece, b)
-    upper, piece, lower = barrier((upper, piece, crossed[middle:rows]))
+    for k in range(len(bits) - 2):
+        pair = weights_step(pair, k)
+    upper, pair, lower = barrier((upper, pair, crossed[middle:rows]))
     lower = spread(lower)
-    piece = dp_double(piece, bits[1])
-    items, upper, lower, piece = barrier((items, upper, lower, piece))
-    piece = dp_double(piece, bits[0])
+    pair = weights_step(pair, len(bits) - 2)
+    items, upper, lower, pair = barrier((items, upper, lower, pair))
+    piece = dp_double(jnp.concatenate(pair, axis=-1), bits[0], 0)
+    piece = piece.reshape(3 * part, width)
     for t in upper:
         items[t] = jnp.concatenate([upper[t], lower[t]], axis=0)
     mine = [items[t] for t in range(n)]
@@ -526,6 +542,7 @@
     w_gate, w_out, pre_gate, d_gated = prepare(
         n, n_dp, slab_o, z, everything, normed, cotangent, attended
     )
+    mine, theirs, attended = barrier((mine, theirs, attended))
     gathered = jnp.concatenate(mine + theirs, axis=0)
     arrived = [
         move(attended[r * local_rows : (r + 1) * local_rows], send_target(r)) for r in range(n)
@@ -687,10 +704,7 @@
     small = jnp.concatenate([y[:, 5 * slab_o :] for y in pair], axis=-1).astype(F32)
     small = jnp.sum(small, axis=0)
     small = small[:2] + small[2:4]
-    step = 1
-    while step < n:
-        small = small + z_swap(small, step)
-        step *= 2
+    small = small + sum(z_swap(small, t) for t in range(1, n))
     norm_gain_gradient = small[0] / input_norm_gain
     grad_slope = lax.dynamic_slice_in_dim(small[1], z * nh, nh, 0)
 

time: 345 us -> 341 us (0.988)
  starting transfers between devices: 74.3 us -> 87.1 us
  waiting for transfers between devices: 125 us -> 116 us
  Pallas kernels: 61.8 us -> 55.5 us
  other arithmetic: 28.3 us -> 23.2 us
    ppermute x52 -> x56, starting transfers between devices: 74.2 us -> 87 us  [move(): return lax.ppermute(x, AXES, pairs)]
    ppermute x52 -> x56, waiting for transfers between devices: 125 us -> 116 us  [move(): return lax.ppermute(x, AXES, pairs)]
    pallas_call x1, Pallas kernels: 26 us -> 22.3 us  [attend_back(): pl.pallas_call(functools.partial(backward_kernel, nh, dim, rows, blocks),...]
    unnamed x100 -> x105, local copies, waits for them, and re-layouts: 14.9 us -> 17.2 us
  transfers between devices with their start and end apart: 53 -> 57, of which waited for: 23 -> 27; matrix products, arithmetic and copies ran while one was open for 11% -> 11% of each run, Pallas kernels for 15% -> 14%
where the time goes in v2:
time: 341 us; the launch traced here: 336 us
  waiting for transfers between devices  116 us (34%)
  starting transfers between devices  87.1 us (26%)
  Pallas kernels  55.5 us (16%)
  local copies, waits for them, and re-layouts  26.6 us (8%)
  other arithmetic  23.2 us (7%)
  between operations  15.6 us (5%)
  matrix products  12 us (4%)
    ppermute x56, waiting for transfers between devices, move(): return lax.ppermute(x, AXES, pairs)  116 us
    ppermute x56, starting transfers between devices, move(): return lax.ppermute(x, AXES, pairs)  87 us
    pallas_call x1, Pallas kernels, attend_back(): pl.pallas_call(functools.partial(backward_kernel, nh, dim, rows, blocks),...  22.3 us
    unnamed x105, local copies, waits for them, and re-layouts  17.2 us
    pallas_call x1, Pallas kernels, attend(): pl.pallas_call(functools.partial(forward_kernel, nh, dim, rows, blocks),...  16.5 us
    dot_general x5, matrix products, dot(): return lax.dot_general(a, b, dims, preferred_element_type=F32)  12 us
  transfers between devices with their start and end apart: 57, of which 27 were waited for; matrix products, arithmetic and copies ran while one was open for 11% of the time, Pallas kernels for 14%

profile of v2, /device:TPU:0, one launch (start us, length us, event | category | flops | bytes accessed | tf_op | source)
XLA Modules:
  0.0 336.0 jit_solution(2615963525798032159)
XLA Ops:
  12.1 3.3 shard_map.118
  19.8 3.6 %collective-permute-start.3 = (bf16[96,1024]{1,0:T(8,128)(2,1)}, bf16[96,1024]{1,0:T(8,128)(2,1)S(1)}, u32[]{:S(2)}, u32[]{:S(2)}) collective-permute-start(bf16[96,1024]{1,0:T(8,128)(2,1)} %get-tuple-element.223), channel_id=1, source_target_pairs={{0,2},{1,3},{2,0},{3,1},{4,6},{5,7},{6,4},{7,5},{8,10},{9,11},{10,... | collective-permute-start | bytes 589832 | tf_op jit(solution)/shard_map/ppermute | solution.py:410
  29.2 4.3 %collective-permute-done.3 = bf16[96,1024]{1,0:T(8,128)(2,1)S(1)} collective-permute-done((bf16[96,1024]{1,0:T(8,128)(2,1)}, bf16[96,1024]{1,0:T(8,128)(2,1)S(1)}, u32[]{:S(2)}, u32[]{:S(2)}) %collective-permute-start.3) | collective-permute-done | bytes 196640 | tf_op jit(solution)/shard_map/ppermute | solution.py:410
  33.5 22.0 %collective-permute-done.1.refs_1_ = bf16[256,1024]{1,0:T(8,128)(2,1)} collective-permute-done((bf16[256,1024]{1,0:T(8,128)(2,1)S(1)}, bf16[256,1024]{1,0:T(8,128)(2,1)}, u32[]{:S(2)}, u32[]{:S(2)}) %collective-permute-start.1) | collective-permute-done | bytes 524320 | tf_op jit(solution)/shard_map/ppermute | solution.py:410
  55.5 3.3 collective-permute-done.2
  67.2 8.7 %collective-permute-done.6 = bf16[128,1024]{1,0:T(8,128)(2,1)S(1)} collective-permute-done((bf16[128,1024]{1,0:T(8,128)(2,1)S(1)}, bf16[128,1024]{1,0:T(8,128)(2,1)S(1)}, u32[]{:S(2)}, u32[]{:S(2)}) %collective-permute-start.6) | collective-permute-done | bytes 262176 | tf_op jit(solution)/shard_map/ppermute | solution.py:410
  76.6 5.7 %collective-permute-done.11 = bf16[1,2,1,96,512]{4,3,2,1,0:T(8,128)(2,1)S(1)} collective-permute-done((bf16[1,2,1,96,512]{4,3,2,1,0:T(8,128)(2,1)S(1)}, bf16[1,2,1,96,512]{4,3,2,1,0:T(8,128)(2,1)S(1)}, u32[]{:S(2)}, u32[]{:S(2)}) %collective-permute-start.11) | collective-permute-done | bytes 196640 | tf_op jit(solution)/shard_map/ppermute | solution.py:410
  94.0 16.5 %shard_map.119 = (bf16[2048,256]{1,0:T(8,128)(2,1)S(1)}, bf16[2048,768]{1,0:T(8,128)(2,1)S(1)}, bf16[2048,768]{1,0:T(8,128)(2,1)S(1)}) custom-call(s32[8]{0:T(128)S(1)} %get-tuple-element.126.low, s32[8]{0:T(128)S(1)} %multiply_add_fusion.1.held, s32[8]{0:T(128)S(1)} %get-tuple-element.128.sent, f32[2]{0:T(128)S(1)} %collective-permute-done.5.slopes, ...), custom_call_target="tpu_custom_call" | custom-call | flops 12884889600 | bytes 4194304 | tf_op jit(solution)/shard_map/pallas_call | solution.py:176
  116.8 15.9 %collective-permute-start.19 = (bf16[512,256]{1,0:T(8,128)(2,1)}, bf16[512,256]{1,0:T(8,128)(2,1)S(1)}, u32[]{:S(2)}, u32[]{:S(2)}) collective-permute-start(bf16[512,256]{1,0:T(8,128)(2,1)} %get-tuple-element.233), channel_id=1, source_target_pairs={{0,2},{1,3},{2,4},{3,5},{4,0},{5,1},{6,6},{7,7},{8,10},{9,11},{10,... | collective-permute-start | bytes 786440 | tf_op jit(solution)/shard_map/ppermute | solution.py:410
  143.3 6.3 %shard_map.121 = (bf16[512,256]{1,0:T(8,128)(2,1)S(1)}, bf16[512,256]{1,0:T(8,128)(2,1)S(1)}, bf16[512,256]{1,0:T(8,128)(2,1)S(1)}, bf16[512,256]{1,0:T(8,128)(2...) custom-call(f32[512,1024]{1,0:T(8,128)S(1)} %get-tuple-element.140.pre_gat, ...), custom_call_target="tpu_custom_call" | custom-call | flops 4294967296 | bytes 16777216 | tf_op jit(solution)/shard_map/pallas_call | solution.py:310
  149.9 6.0 %collective-permute-start.25 = (bf16[2,4,2,2,1,32,1024]{6,5,4,3,2,1,0:T(8,128)(2,1)S(1)}, bf16[2,4,2,2,1,32,1024]{6,5,4,3,2,1,0:T(8,128)(2,1)S(1)}, u32[]{:S(2)}, u32[]{:S(2)}) collective-permute-start(bf16[2,4,2,2,1,32,1024]{6,5,4,3,2,1,0:T(8,128)(2,1)S(1)} %broadcast_select_fusion), channel_id=1, source_target_pairs={{0,4},{1,5},{2,6},{3,7},{4,0},{5,1},{6,2},{7,3},{8,12},{9,13},{10,... | collective-permute-start | bytes 6291464 | tf_op jit(solution)/shard_map/ppermute | solution.py:410
  157.9 4.1 %collective-permute-start.22 = (bf16[512,256]{1,0:T(8,128)(2,1)S(1)}, bf16[512,256]{1,0:T(8,128)(2,1)S(1)}, u32[]{:S(2)}, u32[]{:S(2)}) collective-permute-start(bf16[512,256]{1,0:T(8,128)(2,1)S(1)} %get-tuple-element.147), channel_id=1, source_target_pairs={{0,1},{1,0},{2,5},{3,4},{4,7},{5,6},{6,3},{7,2},{8,9},{9,8},{10,13... | collective-permute-start | bytes 786440 | tf_op jit(solution)/shard_map/ppermute | solution.py:410
  161.9 5.2 %collective-permute-start.23 = (bf16[512,256]{1,0:T(8,128)(2,1)S(1)}, bf16[512,256]{1,0:T(8,128)(2,1)S(1)}, u32[]{:S(2)}, u32[]{:S(2)}) collective-permute-start(bf16[512,256]{1,0:T(8,128)(2,1)S(1)} %get-tuple-element.148), channel_id=1, source_target_pairs={{0,4},{1,5},{2,0},{3,1},{4,2},{5,3},{6,6},{7,7},{8,12},{9,13},{10,... | collective-permute-start | bytes 786440 | tf_op jit(solution)/shard_map/ppermute | solution.py:410
  167.1 3.7 %collective-permute-start.24 = (bf16[512,256]{1,0:T(8,128)(2,1)S(1)}, bf16[512,256]{1,0:T(8,128)(2,1)S(1)}, u32[]{:S(2)}, u32[]{:S(2)}) collective-permute-start(bf16[512,256]{1,0:T(8,128)(2,1)S(1)} %get-tuple-element.149), channel_id=1, source_target_pairs={{0,5},{1,4},{2,1},{3,0},{4,3},{5,2},{6,7},{7,6},{8,13},{9,12},{10,... | collective-permute-start | bytes 786440 | tf_op jit(solution)/shard_map/ppermute | solution.py:410
  177.4 2.6 fusion.24
  180.0 6.2 %collective-permute-done.23 = bf16[512,256]{1,0:T(8,128)(2,1)S(1)} collective-permute-done((bf16[512,256]{1,0:T(8,128)(2,1)S(1)}, bf16[512,256]{1,0:T(8,128)(2,1)S(1)}, u32[]{:S(2)}, u32[]{:S(2)}) %collective-permute-start.23) | collective-permute-done | bytes 262176 | tf_op jit(solution)/shard_map/ppermute | solution.py:410
  186.3 2.8 collective-permute-done.27
  193.2 22.3 %shard_map.122 = (bf16[2048,768]{1,0:T(8,128)(2,1)S(1)}, f32[2,8,256]{2,1,0:T(8,128)S(1)}) custom-call(s32[8]{0:T(128)S(1)} %get-tuple-element.126.low, s32[8]{0:T(128)S(1)} %multiply_add_fusion.1.held, s32[8]{0:T(128)S(1)} %get-tuple-element.128.sent, f32[2]{0:T(128)S(1)} %collective-permute-done.5.slopes, s32[2048,1]{1,0:T(8,128)S(1)} %copy-done.9, ...), custom_call_target="tpu_custom_call" | custom-call | flops 32212224000 | bytes 10485760 | tf_op jit(solution)/shard_map/pallas_call | solution.py:370
  222.3 3.5 %convolution_convert_fusion.2 = bf16[768,1024]{1,0:T(8,128)(2,1)S(1)} fusion(bf16[2048,768]{1,0:T(8,128)(2,1)S(1)} %get-tuple-element.163, bf16[2048,1024]{1,0:T(8,128)(2,1)S(1)} %constant_dynamic-update-slice_fusion.6), kind=kOutput, calls=%fused_computation.22 | convolution fusion | flops 3222011904 | bytes 8912896 | tf_op jit(solution)/shard_map/dot_general | solution.py:20
  227.6 6.3 %collective-permute-done.31 = bf16[2,2,32,1024]{3,2,1,0:T(8,128)(2,1)S(1)} collective-permute-done((bf16[2,2,32,1024]{3,2,1,0:T(8,128)(2,1)S(1)}, bf16[2,2,32,1024]{3,2,1,0:T(8,128)(2,1)S(1)}, u32[]{:S(2)}, u32[]{:S(2)}) %collective-permute-start.31) | collective-permute-done | bytes 262176 | tf_op jit(solution)/shard_map/ppermute | solution.py:410
  237.3 4.6 %collective-permute-start.34 = (bf16[2,1,2,96,512]{4,3,2,1,0:T(8,128)(2,1)S(1)}, bf16[2,1,2,96,512]{4,3,2,1,0:T(8,128)(2,1)S(1)}, u32[]{:S(2)}, u32[]{:S(2)}) collective-permute-start(bf16[2,1,2,96,512]{4,3,2,1,0:T(8,128)(2,1)S(1)} %broadcast_select_fusion.17), channel_id=1, source_target_pairs={{0,16},{1,17},{2,18},{3,19},{4,20},{5,21},{6,22},{7,23},{8,24},{9,... | collective-permute-start | bytes 1179656 | tf_op jit(solution)/shard_map/ppermute | solution.py:410
  242.5 7.8 %collective-permute-done.34 = bf16[2,1,2,96,512]{4,3,2,1,0:T(8,128)(2,1)S(1)} collective-permute-done((bf16[2,1,2,96,512]{4,3,2,1,0:T(8,128)(2,1)S(1)}, bf16[2,1,2,96,512]{4,3,2,1,0:T(8,128)(2,1)S(1)}, u32[]{:S(2)}, u32[]{:S(2)}) %collective-permute-start.34) | collective-permute-done | bytes 393248 | tf_op jit(solution)/shard_map/ppermute | solution.py:410
  253.6 2.7 collective-permute-done.35
  260.1 10.8 %collective-permute-done.39 = bf16[64,1024]{1,0:T(8,128)(2,1)S(1)} collective-permute-done((bf16[64,1024]{1,0:T(8,128)(2,1)S(1)}, bf16[64,1024]{1,0:T(8,128)(2,1)S(1)}, u32[]{:S(2)}, u32[]{:S(2)}) %collective-permute-start.39) | collective-permute-done | bytes 131104 | tf_op jit(solution)/shard_map/ppermute | solution.py:410
  271.6 4.0 %collective-permute-start.40 = (bf16[1,1,1,96,1024]{4,3,2,1,0:T(8,128)(2,1)S(1)}, bf16[1,1,1,96,1024]{4,3,2,1,0:T(8,128)(2,1)S(1)}, u32[]{:S(2)}, u32[]{:S(2)}) collective-permute-start(bf16[1,1,1,96,1024]{4,3,2,1,0:T(8,128)(2,1)S(1)} %broadcast_select_fusion.26), channel_id=1, source_target_pairs={{0,4},{1,5},{2,6},{3,7},{4,0},{5,1},{6,2},{7,3},{8,12},{9,13},{10,... | collective-permute-start | bytes 589832 | tf_op jit(solution)/shard_map/ppermute | solution.py:410
  278.0 6.9 %collective-permute-done.41 = bf16[64,1024]{1,0:T(8,128)(2,1)S(1)} collective-permute-done((bf16[64,1024]{1,0:T(8,128)(2,1)S(1)}, bf16[64,1024]{1,0:T(8,128)(2,1)S(1)}, u32[]{:S(2)}, u32[]{:S(2)}) %collective-permute-start.41) | collective-permute-done | bytes 131104 | tf_op jit(solution)/shard_map/ppermute | solution.py:410
  292.5 5.0 %collective-permute-done.46 = bf16[128,1024]{1,0:T(8,128)(2,1)S(1)} collective-permute-done((bf16[128,1024]{1,0:T(8,128)(2,1)S(1)}, bf16[128,1024]{1,0:T(8,128)(2,1)S(1)}, u32[]{:S(2)}, u32[]{:S(2)}) %collective-permute-start.46) | collective-permute-done | bytes 262176 | tf_op jit(solution)/shard_map/ppermute | solution.py:410
  300.7 6.3 %collective-permute-done.48 = bf16[2,1,1,176,512]{4,3,2,1,0:T(8,128)(2,1)S(1)} collective-permute-done((bf16[2,1,1,176,512]{4,3,2,1,0:T(8,128)(2,1)S(1)}, bf16[2,1,1,176,512]{4,3,2,1,0:T(8,128)(2,1)S(1)}, u32[]{:S(2)}, u32[]{:S(2)}) %collective-permute-start.48) | collective-permute-done | bytes 360480 | tf_op jit(solution)/shard_map/ppermute | solution.py:410
  309.4 2.5 collective-permute-done.50
  313.1 2.5 fusion.18
  318.6 4.3 %collective-permute-start.55 = (f32[2,1024]{1,0:T(2,128)S(1)}, f32[2,1024]{1,0:T(2,128)S(1)}, u32[]{:S(2)}, u32[]{:S(2)}) collective-permute-start(f32[2,1024]{1,0:T(2,128)S(1)} %slice_add_fusion), channel_id=1, source_target_pairs={{0,3},{1,2},{2,1},{3,0},{4,7},{5,6},{6,5},{7,4},{8,11},{9,10},{10,... | collective-permute-start | bytes 24584 | tf_op jit(solution)/shard_map/ppermute | solution.py:410
  322.9 4.7 %shard_map.123 = (f32[1024,8,128]{2,1,0:T(8,128)}, f32[256,1024]{1,0:T(8,128)}) custom-call(bf16[8,176,512]{2,1,0:T(8,128)(2,1)S(1)} %bitcast.66, bf16[8,176,512]{2,1,0:T(8,128)(2,1)S(1)} %bitcast.68), custom_call_target="tpu_custom_call" | custom-call | flops 10000000000 | bytes 8388608 | tf_op jit(solution)/shard_map/pallas_call | solution.py:349
  (310 shorter events, 105.9 us)
Async XLA Ops:
  7.2 127.8 %all-gather.3.cloned.1.call-start = ((), (), s32[]{:S(2)}) async-start(), calls=%async_computation | async-start | bytes 4325376 | tf_op jit(solution)/shard_map/all_gather | solution.py:535
  19.8 13.7 %collective-permute-start.3 = (bf16[96,1024]{1,0:T(8,128)(2,1)}, bf16[96,1024]{1,0:T(8,128)(2,1)S(1)}, u32[]{:S(2)}, u32[]{:S(2)}) collective-permute-start(bf16[96,1024]{1,0:T(8,128)(2,1)} %get-tuple-element.223), channel_id=1, source_target_pairs={{0,2},{1,3},{2,0},{3,1},{4,6},{5,7},{6,4},{7,5},{8,10},{9,11},{10,... | collective-permute-start | bytes 589832 | tf_op jit(solution)/shard_map/ppermute | solution.py:410
  26.8 28.7 %collective-permute-start.1 = (bf16[256,1024]{1,0:T(8,128)(2,1)S(1)}, bf16[256,1024]{1,0:T(8,128)(2,1)}, u32[]{:S(2)}, u32[]{:S(2)}) collective-permute-start(bf16[256,1024]{1,0:T(8,128)(2,1)S(1)} %get-tuple-element.164.refs_0_), channel_id=1, source_target_pairs={{0,1},{1,0},{2,3},{3,2},{4,5},{5,4},{6,7},{7,6},{8,9},{9,8},{10,11... | collective-permute-start | bytes 1572872 | tf_op jit(solution)/shard_map/ppermute | solution.py:410
  28.4 30.4 %collective-permute-start.2 = (bf16[256,1024]{1,0:T(8,128)(2,1)}, bf16[256,1024]{1,0:T(8,128)(2,1)}, u32[]{:S(2)}, u32[]{:S(2)}) collective-permute-start(bf16[256,1024]{1,0:T(8,128)(2,1)} %get-tuple-element.226), channel_id=1, source_target_pairs={{0,2},{1,3},{2,0},{3,1},{4,6},{5,7},{6,4},{7,5},{8,10},{9,11},{10,... | collective-permute-start | bytes 1572872 | tf_op jit(solution)/shard_map/ppermute | solution.py:410
  63.0 12.9 %collective-permute-start.6 = (bf16[128,1024]{1,0:T(8,128)(2,1)S(1)}, bf16[128,1024]{1,0:T(8,128)(2,1)S(1)}, u32[]{:S(2)}, u32[]{:S(2)}) collective-permute-start(bf16[128,1024]{1,0:T(8,128)(2,1)S(1)} %get-tuple-element.122), channel_id=1, source_target_pairs={{0,1},{1,0},{2,3},{3,2},{4,5},{5,4},{6,7},{7,6},{8,9},{9,8},{10,11... | collective-permute-start | bytes 786440 | tf_op jit(solution)/shard_map/ppermute | solution.py:410
  114.9 25.9 %collective-permute-start.17 = (bf16[512,256]{1,0:T(8,128)(2,1)}, bf16[512,256]{1,0:T(8,128)(2,1)S(1)}, u32[]{:S(2)}, u32[]{:S(2)}) collective-permute-start(bf16[512,256]{1,0:T(8,128)(2,1)} %get-tuple-element.235), channel_id=1, source_target_pairs={{0,0},{1,1},{2,6},{3,7},{4,2},{5,3},{6,4},{7,5},{8,8},{9,9},{10,14... | collective-permute-start | bytes 786440 | tf_op jit(solution)/shard_map/ppermute | solution.py:410
  116.5 24.4 %collective-permute-start.18 = (bf16[512,256]{1,0:T(8,128)(2,1)}, bf16[512,256]{1,0:T(8,128)(2,1)S(1)}, u32[]{:S(2)}, u32[]{:S(2)}) collective-permute-start(bf16[512,256]{1,0:T(8,128)(2,1)} %get-tuple-element.234), channel_id=1, source_target_pairs={{0,1},{1,0},{2,7},{3,6},{4,3},{5,2},{6,5},{7,4},{8,9},{9,8},{10,15... | collective-permute-start | bytes 786440 | tf_op jit(solution)/shard_map/ppermute | solution.py:410
  116.8 24.0 %collective-permute-start.19 = (bf16[512,256]{1,0:T(8,128)(2,1)}, bf16[512,256]{1,0:T(8,128)(2,1)S(1)}, u32[]{:S(2)}, u32[]{:S(2)}) collective-permute-start(bf16[512,256]{1,0:T(8,128)(2,1)} %get-tuple-element.233), channel_id=1, source_target_pairs={{0,2},{1,3},{2,4},{3,5},{4,0},{5,1},{6,6},{7,7},{8,10},{9,11},{10,... | collective-permute-start | bytes 786440 | tf_op jit(solution)/shard_map/ppermute | solution.py:410
  132.7 10.6 %collective-permute-start.20 = (bf16[512,256]{1,0:T(8,128)(2,1)}, bf16[512,256]{1,0:T(8,128)(2,1)}, u32[]{:S(2)}, u32[]{:S(2)}) collective-permute-start(bf16[512,256]{1,0:T(8,128)(2,1)} %get-tuple-element.232), channel_id=1, source_target_pairs={{0,3},{1,2},{2,5},{3,4},{4,1},{5,0},{6,7},{7,6},{8,11},{9,10},{10,... | collective-permute-start | bytes 786440 | tf_op jit(solution)/shard_map/ppermute | solution.py:410
  149.9 23.2 %collective-permute-start.25 = (bf16[2,4,2,2,1,32,1024]{6,5,4,3,2,1,0:T(8,128)(2,1)S(1)}, bf16[2,4,2,2,1,32,1024]{6,5,4,3,2,1,0:T(8,128)(2,1)S(1)}, u32[]{:S(2)}, u32[]{:S(2)}) collective-permute-start(bf16[2,4,2,2,1,32,1024]{6,5,4,3,2,1,0:T(8,128)(2,1)S(1)} %broadcast_select_fusion), channel_id=1, source_target_pairs={{0,4},{1,5},{2,6},{3,7},{4,0},{5,1},{6,2},{7,3},{8,12},{9,13},{10,... | collective-permute-start | bytes 6291464 | tf_op jit(solution)/shard_map/ppermute | solution.py:410
  157.2 20.2 %collective-permute-start.21 = (bf16[512,256]{1,0:T(8,128)(2,1)S(1)}, bf16[512,256]{1,0:T(8,128)(2,1)S(1)}, u32[]{:S(2)}, u32[]{:S(2)}) collective-permute-start(bf16[512,256]{1,0:T(8,128)(2,1)S(1)} %get-tuple-element.146), channel_id=1, source_target_pairs={{0,0},{1,1},{2,4},{3,5},{4,6},{5,7},{6,2},{7,3},{8,8},{9,9},{10,12... | collective-permute-start | bytes 786440 | tf_op jit(solution)/shard_map/ppermute | solution.py:410
  157.9 22.2 %collective-permute-start.22 = (bf16[512,256]{1,0:T(8,128)(2,1)S(1)}, bf16[512,256]{1,0:T(8,128)(2,1)S(1)}, u32[]{:S(2)}, u32[]{:S(2)}) collective-permute-start(bf16[512,256]{1,0:T(8,128)(2,1)S(1)} %get-tuple-element.147), channel_id=1, source_target_pairs={{0,1},{1,0},{2,5},{3,4},{4,7},{5,6},{6,3},{7,2},{8,9},{9,8},{10,13... | collective-permute-start | bytes 786440 | tf_op jit(solution)/shard_map/ppermute | solution.py:410
  161.9 24.3 %collective-permute-start.23 = (bf16[512,256]{1,0:T(8,128)(2,1)S(1)}, bf16[512,256]{1,0:T(8,128)(2,1)S(1)}, u32[]{:S(2)}, u32[]{:S(2)}) collective-permute-start(bf16[512,256]{1,0:T(8,128)(2,1)S(1)} %get-tuple-element.148), channel_id=1, source_target_pairs={{0,4},{1,5},{2,0},{3,1},{4,2},{5,3},{6,6},{7,7},{8,12},{9,13},{10,... | collective-permute-start | bytes 786440 | tf_op jit(solution)/shard_map/ppermute | solution.py:410
  167.1 19.1 %collective-permute-start.24 = (bf16[512,256]{1,0:T(8,128)(2,1)S(1)}, bf16[512,256]{1,0:T(8,128)(2,1)S(1)}, u32[]{:S(2)}, u32[]{:S(2)}) collective-permute-start(bf16[512,256]{1,0:T(8,128)(2,1)S(1)} %get-tuple-element.149), channel_id=1, source_target_pairs={{0,5},{1,4},{2,1},{3,0},{4,3},{5,2},{6,7},{7,6},{8,13},{9,12},{10,... | collective-permute-start | bytes 786440 | tf_op jit(solution)/shard_map/ppermute | solution.py:410
  175.1 14.1 %collective-permute-start.27 = (bf16[4,2,1,1,32,1024]{5,4,2,1,0,3:T(8,128)(2,1)S(1)}, bf16[4,2,1,1,32,1024]{5,4,2,1,0,3:T(8,128)(2,1)S(1)}, u32[]{:S(2)}, u32[]{:S(2)}) collective-permute-start(bf16[4,2,1,1,32,1024]{5,4,2,1,0,3:T(8,128)(2,1)S(1)} %broadcast_select_fusion.7), channel_id=1, source_target_pairs={{0,16},{1,17},{2,18},{3,19},{4,20},{5,21},{6,22},{7,23},{8,24},{9,... | collective-permute-start | bytes 1572872 | tf_op jit(solution)/shard_map/ppermute | solution.py:410
  177.4 13.5 %collective-permute-start.26 = (bf16[4,1,2,1,32,1024]{5,4,0,3,2,1:T(8,128)(2,1)S(1)}, bf16[4,1,2,1,32,1024]{5,4,0,3,2,1:T(8,128)(2,1)S(1)}, u32[]{:S(2)}, u32[]{:S(2)}) collective-permute-start(bf16[4,1,2,1,32,1024]{5,4,0,3,2,1:T(8,128)(2,1)S(1)} %broadcast_select_fusion.8), channel_id=1, source_target_pairs={{0,8},{1,9},{2,10},{3,11},{4,12},{5,13},{6,14},{7,15},{8,0},{9,1},... | collective-permute-start | bytes 1572872 | tf_op jit(solution)/shard_map/ppermute | solution.py:410
  191.1 24.4 %collective-permute-start.29 = (bf16[4,1,1,1,32,1024]{5,4,2,1,0,3:T(8,128)(2,1)S(1)}, bf16[4,1,1,1,32,1024]{5,4,2,1,0,3:T(8,128)(2,1)S(1)}, u32[]{:S(2)}, u32[]{:S(2)}) collective-permute-start(bf16[4,1,1,1,32,1024]{5,4,2,1,0,3:T(8,128)(2,1)S(1)} %broadcast_select_fusion.23), channel_id=1, source_target_pairs={{0,8},{1,9},{2,10},{3,11},{4,12},{5,13},{6,14},{7,15},{8,0},{9,1},... | collective-permute-start | bytes 786440 | tf_op jit(solution)/shard_map/ppermute | solution.py:410
  191.5 24.1 %collective-permute-start.28 = (bf16[4,1,1,1,32,1024]{5,4,0,3,2,1:T(8,128)(2,1)S(1)}, bf16[4,1,1,1,32,1024]{5,4,0,3,2,1:T(8,128)(2,1)S(1)}, u32[]{:S(2)}, u32[]{:S(2)}) collective-permute-start(bf16[4,1,1,1,32,1024]{5,4,0,3,2,1:T(8,128)(2,1)S(1)} %broadcast_select_fusion.24), channel_id=1, source_target_pairs={{0,16},{1,17},{2,18},{3,19},{4,20},{5,21},{6,22},{7,23},{8,24},{9,... | collective-permute-start | bytes 786440 | tf_op jit(solution)/shard_map/ppermute | solution.py:410
  218.7 15.3 %collective-permute-start.30 = (bf16[1024,1024]{1,0:T(8,128)(2,1)S(1)}, bf16[1024,1024]{1,0:T(8,128)(2,1)S(1)}, u32[]{:S(2)}, u32[]{:S(2)}) collective-permute-start(bf16[1024,1024]{1,0:T(8,128)(2,1)S(1)} %convolution_convert_fusion.1), channel_id=1, source_target_pairs={{0,4},{1,5},{2,6},{3,7},{4,0},{5,1},{6,2},{7,3},{8,12},{9,13},{10,... | collective-permute-start | bytes 6291464 | tf_op jit(solution)/shard_map/ppermute | solution.py:410
  220.2 13.7 %collective-permute-start.31 = (bf16[2,2,32,1024]{3,2,1,0:T(8,128)(2,1)S(1)}, bf16[2,2,32,1024]{3,2,1,0:T(8,128)(2,1)S(1)}, u32[]{:S(2)}, u32[]{:S(2)}) collective-permute-start(bf16[2,2,32,1024]{3,2,1,0:T(8,128)(2,1)S(1)} %slice.265), channel_id=1, source_target_pairs={{0,2},{1,3},{2,0},{3,1},{4,6},{5,7},{6,4},{7,5},{8,10},{9,11},{10,... | collective-permute-start | bytes 786440 | tf_op jit(solution)/shard_map/ppermute | solution.py:410
  235.1 18.3 %collective-permute-start.36 = (bf16[256,1024]{1,0:T(8,128)(2,1)S(1)}, bf16[256,1024]{1,0:T(8,128)(2,1)S(1)}, u32[]{:S(2)}, u32[]{:S(2)}) collective-permute-start(bf16[256,1024]{1,0:T(8,128)(2,1)S(1)} %slice.276), channel_id=1, source_target_pairs={{0,1},{1,0},{2,3},{3,2},{4,5},{5,4},{6,7},{7,6},{8,9},{9,8},{10,11... | collective-permute-start | bytes 1572872 | tf_op jit(solution)/shard_map/ppermute | solution.py:410
  237.3 13.1 %collective-permute-start.34 = (bf16[2,1,2,96,512]{4,3,2,1,0:T(8,128)(2,1)S(1)}, bf16[2,1,2,96,512]{4,3,2,1,0:T(8,128)(2,1)S(1)}, u32[]{:S(2)}, u32[]{:S(2)}) collective-permute-start(bf16[2,1,2,96,512]{4,3,2,1,0:T(8,128)(2,1)S(1)} %broadcast_select_fusion.17), channel_id=1, source_target_pairs={{0,16},{1,17},{2,18},{3,19},{4,20},{5,21},{6,22},{7,23},{8,24},{9,... | collective-permute-start | bytes 1179656 | tf_op jit(solution)/shard_map/ppermute | solution.py:410
  241.9 10.4 %collective-permute-start.32 = (bf16[1,2,2,96,512]{4,3,2,1,0:T(8,128)(2,1)S(1)}, bf16[1,2,2,96,512]{4,3,2,1,0:T(8,128)(2,1)S(1)}, u32[]{:S(2)}, u32[]{:S(2)}) collective-permute-start(bf16[1,2,2,96,512]{4,3,2,1,0:T(8,128)(2,1)S(1)} %broadcast_select_fusion.18), channel_id=1, source_target_pairs={{0,8},{1,9},{2,10},{3,11},{4,12},{5,13},{6,14},{7,15},{8,0},{9,1},... | collective-permute-start | bytes 1179656 | tf_op jit(solution)/shard_map/ppermute | solution.py:410
  258.4 12.5 %collective-permute-start.38 = (bf16[1,1,2,96,1024]{4,3,2,1,0:T(8,128)(2,1)S(1)}, bf16[1,1,2,96,1024]{4,3,2,1,0:T(8,128)(2,1)S(1)}, u32[]{:S(2)}, u32[]{:S(2)}) collective-permute-start(bf16[1,1,2,96,1024]{4,3,2,1,0:T(8,128)(2,1)S(1)} %pad_maximum_fusion.8), channel_id=1, source_target_pairs={{0,0},{1,1},{2,2},{3,3},{4,6},{5,7},{6,4},{7,5},{8,8},{9,9},{10,10... | collective-permute-start | bytes 1179656 | tf_op jit(solution)/shard_map/ppermute | solution.py:410
  260.0 10.9 %collective-permute-start.39 = (bf16[64,1024]{1,0:T(8,128)(2,1)S(1)}, bf16[64,1024]{1,0:T(8,128)(2,1)S(1)}, u32[]{:S(2)}, u32[]{:S(2)}) collective-permute-start(bf16[64,1024]{1,0:T(8,128)(2,1)S(1)} %get-tuple-element.249), channel_id=1, source_target_pairs={{0,2},{1,3},{2,0},{3,1},{4,6},{5,7},{6,4},{7,5},{8,10},{9,11},{10,... | collective-permute-start | bytes 393224 | tf_op jit(solution)/shard_map/ppermute | solution.py:410
  275.7 9.2 %collective-permute-start.41 = (bf16[64,1024]{1,0:T(8,128)(2,1)S(1)}, bf16[64,1024]{1,0:T(8,128)(2,1)S(1)}, u32[]{:S(2)}, u32[]{:S(2)}) collective-permute-start(bf16[64,1024]{1,0:T(8,128)(2,1)S(1)} %get-tuple-element.184), channel_id=1, source_target_pairs={{0,2},{1,3},{2,0},{3,1},{4,6},{5,7},{6,4},{7,5},{8,10},{9,11},{10,... | collective-permute-start | bytes 393224 | tf_op jit(solution)/shard_map/ppermute | solution.py:410
  287.8 9.7 %collective-permute-start.46 = (bf16[128,1024]{1,0:T(8,128)(2,1)S(1)}, bf16[128,1024]{1,0:T(8,128)(2,1)S(1)}, u32[]{:S(2)}, u32[]{:S(2)}) collective-permute-start(bf16[128,1024]{1,0:T(8,128)(2,1)S(1)} %slice.247), channel_id=1, source_target_pairs={{0,1},{1,0},{2,3},{3,2},{4,5},{5,4},{6,7},{7,6},{8,9},{9,8},{10,11... | collective-permute-start | bytes 786440 | tf_op jit(solution)/shard_map/ppermute | solution.py:410
  287.9 9.7 %collective-permute-start.45 = (bf16[64,1024]{1,0:T(8,128)(2,1)S(1)}, bf16[64,1024]{1,0:T(8,128)(2,1)S(1)}, u32[]{:S(2)}, u32[]{:S(2)}) collective-permute-start(bf16[64,1024]{1,0:T(8,128)(2,1)S(1)} %get-tuple-element.193), channel_id=1, source_target_pairs={{0,2},{1,3},{2,0},{3,1},{4,6},{5,7},{6,4},{7,5},{8,10},{9,11},{10,... | collective-permute-start | bytes 393224 | tf_op jit(solution)/shard_map/ppermute | solution.py:410
  297.6 9.4 %collective-permute-start.48 = (bf16[2,1,1,176,512]{4,3,2,1,0:T(8,128)(2,1)S(1)}, bf16[2,1,1,176,512]{4,3,2,1,0:T(8,128)(2,1)S(1)}, u32[]{:S(2)}, u32[]{:S(2)}) collective-permute-start(bf16[2,1,1,176,512]{4,3,2,1,0:T(8,128)(2,1)S(1)} %pad_maximum_fusion.10), channel_id=1, source_target_pairs={{0,16},{1,17},{2,18},{3,19},{4,20},{5,21},{6,22},{7,23},{8,24},{9,... | collective-permute-start | bytes 1081352 | tf_op jit(solution)/shard_map/ppermute | solution.py:410
  318.4 9.2 %collective-permute-start.53 = (f32[2,1024]{1,0:T(2,128)S(1)}, f32[2,1024]{1,0:T(2,128)S(1)}, u32[]{:S(2)}, u32[]{:S(2)}) collective-permute-start(f32[2,1024]{1,0:T(2,128)S(1)} %slice_add_fusion), channel_id=1, source_target_pairs={{0,1},{1,0},{2,3},{3,2},{4,5},{5,4},{6,7},{7,6},{8,9},{9,8},{10,11... | collective-permute-start | bytes 24584 | tf_op jit(solution)/shard_map/ppermute | solution.py:410
  318.5 9.1 %collective-permute-start.54 = (f32[2,1024]{1,0:T(2,128)S(1)}, f32[2,1024]{1,0:T(2,128)S(1)}, u32[]{:S(2)}, u32[]{:S(2)}) collective-permute-start(f32[2,1024]{1,0:T(2,128)S(1)} %slice_add_fusion), channel_id=1, source_target_pairs={{0,2},{1,3},{2,0},{3,1},{4,6},{5,7},{6,4},{7,5},{8,10},{9,11},{10,... | collective-permute-start | bytes 24584 | tf_op jit(solution)/shard_map/ppermute | solution.py:410
  318.6 9.0 %collective-permute-start.55 = (f32[2,1024]{1,0:T(2,128)S(1)}, f32[2,1024]{1,0:T(2,128)S(1)}, u32[]{:S(2)}, u32[]{:S(2)}) collective-permute-start(f32[2,1024]{1,0:T(2,128)S(1)} %slice_add_fusion), channel_id=1, source_target_pairs={{0,3},{1,2},{2,1},{3,0},{4,7},{5,6},{6,5},{7,4},{8,11},{9,10},{10,... | collective-permute-start | bytes 24584 | tf_op jit(solution)/shard_map/ppermute | solution.py:410
  (70 other events, 461.6 us)
Sparse Core Ops, SparseCore 0:
  18.7 82.0 all-gather.2

commit v3 on v2

--- a/solution.py
+++ b/solution.py
@@ -30,9 +30,9 @@
     return sigma * (1.0 + values * (1.0 - sigma))
 
 
-def fill_distance(dist, blocks, rows):
-    row = lax.broadcasted_iota(jnp.int32, (rows, rows), 0)
-    column = lax.broadcasted_iota(jnp.int32, (rows, rows), 1)
+def fill_distance(dist, blocks, rows, query_axis):
+    row = lax.broadcasted_iota(jnp.int32, (rows, rows), query_axis)
+    column = lax.broadcasted_iota(jnp.int32, (rows, rows), 1 - query_axis)
 
     def one(step, carry):
         offset = jnp.maximum(step * rows + row - column, 0).astype(F32)
@@ -68,7 +68,7 @@
     pre_copy = pltpu.make_async_copy(pre_ref, pre_hbm, sems.at[1])
     act_copy.start()
     pre_copy.start()
-    fill_distance(dist, blocks, rows)
+    fill_distance(dist, blocks, rows, 0)
     scale = dim ** (-0.5)
     part = nh * dim
 
@@ -103,7 +103,7 @@
     nh, dim, rows, blocks, low, held, sent, slopes, starts_ref, act_ref, pre_ref, datt_ref,
     out_ref, slope_ref, dist, dq, dk, dv, gs
 ):
-    fill_distance(dist, blocks, rows)
+    fill_distance(dist, blocks, rows, 1)
     scale = dim ** (-0.5)
     part = nh * dim
     dk[...] = jnp.zeros_like(dk)
@@ -118,7 +118,9 @@
         mine = held[i]
 
         def key_block(j, inner):
-            visible = visible_pairs(starts_ref, i, j, rows)
+            key = lax.broadcasted_iota(jnp.int32, (rows, rows), 0) + j * rows
+            query = lax.broadcasted_iota(jnp.int32, (rows, rows), 1) + i * rows
+            visible = (key >= starts_ref[i]) & (key <= query)
             distance = dist[i - j]
             theirs = held[j]
             for h in range(nh):
@@ -127,16 +129,16 @@
                 k = act_ref[at(theirs), 2 * part + h * dim : 2 * part + (h + 1) * dim]
                 v = act_ref[at(theirs), cols]
                 da = datt_ref[at(sent[i]), cols]
-                u = half_score(q, k, slopes[h], distance, visible, scale)
+                u = half_score(k, q, slopes[h], distance, visible, scale)
                 t = jnp.tanh(u)
                 w = u + u * t
-                ds = dot(da, v, NT) * ((1.0 + t) + w * (1.0 - t))
+                ds = dot(v, da, NT) * ((1.0 + t) + w * (1.0 - t))
                 gs[h] += jnp.sum((ds * distance).reshape(rows // 8, 8, rows), axis=0)
                 wb = w.astype(BF)
                 db = ds.astype(BF)
-                dv[at(theirs), cols] += dot(wb, da, TN)
-                dk[at(theirs), cols] += dot(db, q, TN)
-                dq[:, cols] += dot(db, k)
+                dv[at(theirs), cols] += dot(wb, da)
+                dk[at(theirs), cols] += dot(db, q)
+                dq[:, cols] += dot(db, k, TN)
             return inner
 
         lax.fori_loop(low[i], i + 1, key_block, 0)
@@ -384,7 +386,7 @@
         ],
         compiler_params=pltpu.CompilerParams(vmem_limit_bytes=48 * 2**20),
         cost_estimate=attention_cost(nh, dim, total, 5),
-    )(*tables, slopes, starts, act, pre, d_attended)
+    )(*tables, slopes, starts.reshape(blocks, 1, rows), act, pre, d_attended)
 
 
 def body(

time: 341 us -> 339 us (level)
  starting transfers between devices: 87.1 us -> 79.5 us
  Pallas kernels: 55.5 us -> 59.7 us
    ppermute x56, starting transfers between devices: 87 us -> 79.5 us  [move(): return lax.ppermute(x, AXES, pairs)]
    unnamed x105 -> x99, local copies, waits for them, and re-layouts: 17.2 us -> 16.9 us
  transfers between devices with their start and end apart: 57 -> 57, of which waited for: 27 -> 29; matrix products, arithmetic and copies ran while one was open for 11% -> 11% of each run, Pallas kernels for 14% -> 15%
where the time goes in v3:
time: 339 us; the launch traced here: 335 us
  waiting for transfers between devices  119 us (35%)
  starting transfers between devices  79.5 us (23%)
  Pallas kernels  59.7 us (18%)
  local copies, waits for them, and re-layouts  26.4 us (8%)
  other arithmetic  23.1 us (7%)
  between operations  15.6 us (5%)
  matrix products  11.9 us (4%)
    ppermute x56, waiting for transfers between devices, move(): return lax.ppermute(x, AXES, pairs)  119 us
    ppermute x56, starting transfers between devices, move(): return lax.ppermute(x, AXES, pairs)  79.5 us
    pallas_call x1, Pallas kernels, attend_back(): pl.pallas_call(functools.partial(backward_kernel, nh, dim, rows, blocks),...  24.2 us
    pallas_call x1, Pallas kernels, attend(): pl.pallas_call(functools.partial(forward_kernel, nh, dim, rows, blocks),...  18.8 us
    unnamed x99, local copies, waits for them, and re-layouts  16.9 us
    dot_general x5, matrix products, dot(): return lax.dot_general(a, b, dims, preferred_element_type=F32)  11.9 us
  transfers between devices with their start and end apart: 57, of which 29 were waited for; matrix products, arithmetic and copies ran while one was open for 11% of the time, Pallas kernels for 15%

profile of v3, /device:TPU:0, one launch (start us, length us, event | category | flops | bytes accessed | tf_op | source)
XLA Modules:
  0.0 335.1 jit_solution(815355305737644050)
XLA Ops:
  12.1 3.3 shard_map.118
  19.9 3.6 %collective-permute-start.3 = (bf16[96,1024]{1,0:T(8,128)(2,1)}, bf16[96,1024]{1,0:T(8,128)(2,1)S(1)}, u32[]{:S(2)}, u32[]{:S(2)}) collective-permute-start(bf16[96,1024]{1,0:T(8,128)(2,1)} %get-tuple-element.223), channel_id=1, source_target_pairs={{0,2},{1,3},{2,0},{3,1},{4,6},{5,7},{6,4},{7,5},{8,10},{9,11},{10,... | collective-permute-start | bytes 589832 | tf_op jit(solution)/shard_map/ppermute | solution.py:412
  29.2 4.3 %collective-permute-done.3 = bf16[96,1024]{1,0:T(8,128)(2,1)S(1)} collective-permute-done((bf16[96,1024]{1,0:T(8,128)(2,1)}, bf16[96,1024]{1,0:T(8,128)(2,1)S(1)}, u32[]{:S(2)}, u32[]{:S(2)}) %collective-permute-start.3) | collective-permute-done | bytes 196640 | tf_op jit(solution)/shard_map/ppermute | solution.py:412
  33.5 22.0 %collective-permute-done.1.refs_1_ = bf16[256,1024]{1,0:T(8,128)(2,1)} collective-permute-done((bf16[256,1024]{1,0:T(8,128)(2,1)S(1)}, bf16[256,1024]{1,0:T(8,128)(2,1)}, u32[]{:S(2)}, u32[]{:S(2)}) %collective-permute-start.1) | collective-permute-done | bytes 524320 | tf_op jit(solution)/shard_map/ppermute | solution.py:412
  55.5 3.3 collective-permute-done.2
  67.2 8.7 %collective-permute-done.6 = bf16[128,1024]{1,0:T(8,128)(2,1)S(1)} collective-permute-done((bf16[128,1024]{1,0:T(8,128)(2,1)S(1)}, bf16[128,1024]{1,0:T(8,128)(2,1)S(1)}, u32[]{:S(2)}, u32[]{:S(2)}) %collective-permute-start.6) | collective-permute-done | bytes 262176 | tf_op jit(solution)/shard_map/ppermute | solution.py:412
  76.6 5.7 %collective-permute-done.11 = bf16[1,2,1,96,512]{4,3,2,1,0:T(8,128)(2,1)S(1)} collective-permute-done((bf16[1,2,1,96,512]{4,3,2,1,0:T(8,128)(2,1)S(1)}, bf16[1,2,1,96,512]{4,3,2,1,0:T(8,128)(2,1)S(1)}, u32[]{:S(2)}, u32[]{:S(2)}) %collective-permute-start.11) | collective-permute-done | bytes 196640 | tf_op jit(solution)/shard_map/ppermute | solution.py:412
  94.1 18.8 %shard_map.119 = (bf16[2048,256]{1,0:T(8,128)(2,1)S(1)}, bf16[2048,768]{1,0:T(8,128)(2,1)S(1)}, bf16[2048,768]{1,0:T(8,128)(2,1)S(1)}) custom-call(s32[8]{0:T(128)S(1)} %get-tuple-element.126.low, s32[8]{0:T(128)S(1)} %multiply_add_fusion.1.held, s32[8]{0:T(128)S(1)} %get-tuple-element.128.sent, f32[2]{0:T(128)S(1)} %collective-permute-done.5.slopes, ...), custom_call_target="tpu_custom_call" | custom-call | flops 12884889600 | bytes 4194304 | tf_op jit(solution)/shard_map/pallas_call | solution.py:178
  119.2 13.6 %collective-permute-start.19 = (bf16[512,256]{1,0:T(8,128)(2,1)}, bf16[512,256]{1,0:T(8,128)(2,1)S(1)}, u32[]{:S(2)}, u32[]{:S(2)}) collective-permute-start(bf16[512,256]{1,0:T(8,128)(2,1)} %get-tuple-element.233), channel_id=1, source_target_pairs={{0,2},{1,3},{2,4},{3,5},{4,0},{5,1},{6,6},{7,7},{8,10},{9,11},{10,... | collective-permute-start | bytes 786440 | tf_op jit(solution)/shard_map/ppermute | solution.py:412
  143.3 6.3 %shard_map.121 = (bf16[512,256]{1,0:T(8,128)(2,1)S(1)}, bf16[512,256]{1,0:T(8,128)(2,1)S(1)}, bf16[512,256]{1,0:T(8,128)(2,1)S(1)}, bf16[512,256]{1,0:T(8,128)(2...) custom-call(f32[512,1024]{1,0:T(8,128)S(1)} %get-tuple-element.140.pre_gat, ...), custom_call_target="tpu_custom_call" | custom-call | flops 4294967296 | bytes 16777216 | tf_op jit(solution)/shard_map/pallas_call | solution.py:312
  149.9 6.1 %collective-permute-start.25 = (bf16[2,4,2,2,1,32,1024]{6,5,4,3,2,1,0:T(8,128)(2,1)S(1)}, bf16[2,4,2,2,1,32,1024]{6,5,4,3,2,1,0:T(8,128)(2,1)S(1)}, u32[]{:S(2)}, u32[]{:S(2)}) collective-permute-start(bf16[2,4,2,2,1,32,1024]{6,5,4,3,2,1,0:T(8,128)(2,1)S(1)} %broadcast_select_fusion), channel_id=1, source_target_pairs={{0,4},{1,5},{2,6},{3,7},{4,0},{5,1},{6,2},{7,3},{8,12},{9,13},{10,... | collective-permute-start | bytes 6291464 | tf_op jit(solution)/shard_map/ppermute | solution.py:412
  157.9 4.1 %collective-permute-start.22 = (bf16[512,256]{1,0:T(8,128)(2,1)S(1)}, bf16[512,256]{1,0:T(8,128)(2,1)S(1)}, u32[]{:S(2)}, u32[]{:S(2)}) collective-permute-start(bf16[512,256]{1,0:T(8,128)(2,1)S(1)} %get-tuple-element.147), channel_id=1, source_target_pairs={{0,1},{1,0},{2,5},{3,4},{4,7},{5,6},{6,3},{7,2},{8,9},{9,8},{10,13... | collective-permute-start | bytes 786440 | tf_op jit(solution)/shard_map/ppermute | solution.py:412
  162.0 5.2 %collective-permute-start.23 = (bf16[512,256]{1,0:T(8,128)(2,1)S(1)}, bf16[512,256]{1,0:T(8,128)(2,1)S(1)}, u32[]{:S(2)}, u32[]{:S(2)}) collective-permute-start(bf16[512,256]{1,0:T(8,128)(2,1)S(1)} %get-tuple-element.148), channel_id=1, source_target_pairs={{0,4},{1,5},{2,0},{3,1},{4,2},{5,3},{6,6},{7,7},{8,12},{9,13},{10,... | collective-permute-start | bytes 786440 | tf_op jit(solution)/shard_map/ppermute | solution.py:412
  167.1 3.7 %collective-permute-start.24 = (bf16[512,256]{1,0:T(8,128)(2,1)S(1)}, bf16[512,256]{1,0:T(8,128)(2,1)S(1)}, u32[]{:S(2)}, u32[]{:S(2)}) collective-permute-start(bf16[512,256]{1,0:T(8,128)(2,1)S(1)} %get-tuple-element.149), channel_id=1, source_target_pairs={{0,5},{1,4},{2,1},{3,0},{4,3},{5,2},{6,7},{7,6},{8,13},{9,12},{10,... | collective-permute-start | bytes 786440 | tf_op jit(solution)/shard_map/ppermute | solution.py:412
  174.9 2.7 collective-permute-start.27
  177.9 2.6 fusion.24
  180.5 5.8 %collective-permute-done.23 = bf16[512,256]{1,0:T(8,128)(2,1)S(1)} collective-permute-done((bf16[512,256]{1,0:T(8,128)(2,1)S(1)}, bf16[512,256]{1,0:T(8,128)(2,1)S(1)}, u32[]{:S(2)}, u32[]{:S(2)}) %collective-permute-start.23) | collective-permute-done | bytes 262176 | tf_op jit(solution)/shard_map/ppermute | solution.py:412
  186.3 3.2 collective-permute-done.27
  193.0 24.2 %shard_map.122 = (bf16[2048,768]{1,0:T(8,128)(2,1)S(1)}, f32[2,8,256]{2,1,0:T(8,128)S(1)}) custom-call(s32[8]{0:T(128)S(1)} %get-tuple-element.126.low, s32[8]{0:T(128)S(1)} %multiply_add_fusion.1.held, s32[8]{0:T(128)S(1)} %get-tuple-element.128.sent, f32[2]{0:T(128)S(1)} %collective-permute-done.5.slopes, s32[8,1,256]{2,1,0:T(1,128)S(1)} %bitcast.72, ...), custom_call_target="tpu_custom_call" | custom-call | flops 32212224000 | bytes 10485760 | tf_op jit(solution)/shard_map/pallas_call | solution.py:372
  221.9 3.5 %convolution_convert_fusion.2 = bf16[768,1024]{1,0:T(8,128)(2,1)S(1)} fusion(bf16[2048,768]{1,0:T(8,128)(2,1)S(1)} %get-tuple-element.163, bf16[2048,1024]{1,0:T(8,128)(2,1)S(1)} %constant_dynamic-update-slice_fusion.6), kind=kOutput, calls=%fused_computation.22 | convolution fusion | flops 3222011904 | bytes 8912896 | tf_op jit(solution)/shard_map/dot_general | solution.py:20
  227.1 8.5 %collective-permute-done.31 = bf16[2,2,32,1024]{3,2,1,0:T(8,128)(2,1)S(1)} collective-permute-done((bf16[2,2,32,1024]{3,2,1,0:T(8,128)(2,1)S(1)}, bf16[2,2,32,1024]{3,2,1,0:T(8,128)(2,1)S(1)}, u32[]{:S(2)}, u32[]{:S(2)}) %collective-permute-start.31) | collective-permute-done | bytes 262176 | tf_op jit(solution)/shard_map/ppermute | solution.py:412
  242.2 7.3 %collective-permute-done.34 = bf16[2,1,2,96,512]{4,3,2,1,0:T(8,128)(2,1)S(1)} collective-permute-done((bf16[2,1,2,96,512]{4,3,2,1,0:T(8,128)(2,1)S(1)}, bf16[2,1,2,96,512]{4,3,2,1,0:T(8,128)(2,1)S(1)}, u32[]{:S(2)}, u32[]{:S(2)}) %collective-permute-start.34) | collective-permute-done | bytes 393248 | tf_op jit(solution)/shard_map/ppermute | solution.py:412
  252.6 2.8 collective-permute-done.35
  258.5 11.1 %collective-permute-done.39 = bf16[64,1024]{1,0:T(8,128)(2,1)S(1)} collective-permute-done((bf16[64,1024]{1,0:T(8,128)(2,1)S(1)}, bf16[64,1024]{1,0:T(8,128)(2,1)S(1)}, u32[]{:S(2)}, u32[]{:S(2)}) %collective-permute-start.39) | collective-permute-done | bytes 131104 | tf_op jit(solution)/shard_map/ppermute | solution.py:412
  270.3 4.0 %collective-permute-start.40 = (bf16[1,1,1,96,1024]{4,3,2,1,0:T(8,128)(2,1)S(1)}, bf16[1,1,1,96,1024]{4,3,2,1,0:T(8,128)(2,1)S(1)}, u32[]{:S(2)}, u32[]{:S(2)}) collective-permute-start(bf16[1,1,1,96,1024]{4,3,2,1,0:T(8,128)(2,1)S(1)} %broadcast_select_fusion.26), channel_id=1, source_target_pairs={{0,4},{1,5},{2,6},{3,7},{4,0},{5,1},{6,2},{7,3},{8,12},{9,13},{10,... | collective-permute-start | bytes 589832 | tf_op jit(solution)/shard_map/ppermute | solution.py:412
  276.7 6.9 %collective-permute-done.41 = bf16[64,1024]{1,0:T(8,128)(2,1)S(1)} collective-permute-done((bf16[64,1024]{1,0:T(8,128)(2,1)S(1)}, bf16[64,1024]{1,0:T(8,128)(2,1)S(1)}, u32[]{:S(2)}, u32[]{:S(2)}) %collective-permute-start.41) | collective-permute-done | bytes 131104 | tf_op jit(solution)/shard_map/ppermute | solution.py:412
  291.2 5.4 %collective-permute-done.46 = bf16[128,1024]{1,0:T(8,128)(2,1)S(1)} collective-permute-done((bf16[128,1024]{1,0:T(8,128)(2,1)S(1)}, bf16[128,1024]{1,0:T(8,128)(2,1)S(1)}, u32[]{:S(2)}, u32[]{:S(2)}) %collective-permute-start.46) | collective-permute-done | bytes 262176 | tf_op jit(solution)/shard_map/ppermute | solution.py:412
  299.4 6.6 %collective-permute-done.48 = bf16[2,1,1,176,512]{4,3,2,1,0:T(8,128)(2,1)S(1)} collective-permute-done((bf16[2,1,1,176,512]{4,3,2,1,0:T(8,128)(2,1)S(1)}, bf16[2,1,1,176,512]{4,3,2,1,0:T(8,128)(2,1)S(1)}, u32[]{:S(2)}, u32[]{:S(2)}) %collective-permute-start.48) | collective-permute-done | bytes 360480 | tf_op jit(solution)/shard_map/ppermute | solution.py:412
  308.5 2.5 collective-permute-done.50
  312.1 2.5 fusion.18
  317.7 4.3 %collective-permute-start.55 = (f32[2,1024]{1,0:T(2,128)S(1)}, f32[2,1024]{1,0:T(2,128)S(1)}, u32[]{:S(2)}, u32[]{:S(2)}) collective-permute-start(f32[2,1024]{1,0:T(2,128)S(1)} %slice_add_fusion), channel_id=1, source_target_pairs={{0,3},{1,2},{2,1},{3,0},{4,7},{5,6},{6,5},{7,4},{8,11},{9,10},{10,... | collective-permute-start | bytes 24584 | tf_op jit(solution)/shard_map/ppermute | solution.py:412
  322.0 4.7 %shard_map.123 = (f32[1024,8,128]{2,1,0:T(8,128)}, f32[256,1024]{1,0:T(8,128)}) custom-call(bf16[8,176,512]{2,1,0:T(8,128)(2,1)S(1)} %bitcast.67, bf16[8,176,512]{2,1,0:T(8,128)(2,1)S(1)} %bitcast.69), custom_call_target="tpu_custom_call" | custom-call | flops 10000000000 | bytes 8388608 | tf_op jit(solution)/shard_map/pallas_call | solution.py:351
  (304 shorter events, 102.2 us)
Async XLA Ops:
  7.2 127.9 %all-gather.3.cloned.1.call-start = ((), (), s32[]{:S(2)}) async-start(), calls=%async_computation | async-start | bytes 4325376 | tf_op jit(solution)/shard_map/all_gather | solution.py:537
  19.9 13.7 %collective-permute-start.3 = (bf16[96,1024]{1,0:T(8,128)(2,1)}, bf16[96,1024]{1,0:T(8,128)(2,1)S(1)}, u32[]{:S(2)}, u32[]{:S(2)}) collective-permute-start(bf16[96,1024]{1,0:T(8,128)(2,1)} %get-tuple-element.223), channel_id=1, source_target_pairs={{0,2},{1,3},{2,0},{3,1},{4,6},{5,7},{6,4},{7,5},{8,10},{9,11},{10,... | collective-permute-start | bytes 589832 | tf_op jit(solution)/shard_map/ppermute | solution.py:412
  26.8 28.7 %collective-permute-start.1 = (bf16[256,1024]{1,0:T(8,128)(2,1)S(1)}, bf16[256,1024]{1,0:T(8,128)(2,1)}, u32[]{:S(2)}, u32[]{:S(2)}) collective-permute-start(bf16[256,1024]{1,0:T(8,128)(2,1)S(1)} %get-tuple-element.164.refs_0_), channel_id=1, source_target_pairs={{0,1},{1,0},{2,3},{3,2},{4,5},{5,4},{6,7},{7,6},{8,9},{9,8},{10,11... | collective-permute-start | bytes 1572872 | tf_op jit(solution)/shard_map/ppermute | solution.py:412
  28.4 30.4 %collective-permute-start.2 = (bf16[256,1024]{1,0:T(8,128)(2,1)}, bf16[256,1024]{1,0:T(8,128)(2,1)}, u32[]{:S(2)}, u32[]{:S(2)}) collective-permute-start(bf16[256,1024]{1,0:T(8,128)(2,1)} %get-tuple-element.226), channel_id=1, source_target_pairs={{0,2},{1,3},{2,0},{3,1},{4,6},{5,7},{6,4},{7,5},{8,10},{9,11},{10,... | collective-permute-start | bytes 1572872 | tf_op jit(solution)/shard_map/ppermute | solution.py:412
  63.1 12.9 %collective-permute-start.6 = (bf16[128,1024]{1,0:T(8,128)(2,1)S(1)}, bf16[128,1024]{1,0:T(8,128)(2,1)S(1)}, u32[]{:S(2)}, u32[]{:S(2)}) collective-permute-start(bf16[128,1024]{1,0:T(8,128)(2,1)S(1)} %get-tuple-element.122), channel_id=1, source_target_pairs={{0,1},{1,0},{2,3},{3,2},{4,5},{5,4},{6,7},{7,6},{8,9},{9,8},{10,11... | collective-permute-start | bytes 786440 | tf_op jit(solution)/shard_map/ppermute | solution.py:412
  117.2 23.6 %collective-permute-start.17 = (bf16[512,256]{1,0:T(8,128)(2,1)}, bf16[512,256]{1,0:T(8,128)(2,1)S(1)}, u32[]{:S(2)}, u32[]{:S(2)}) collective-permute-start(bf16[512,256]{1,0:T(8,128)(2,1)} %get-tuple-element.235), channel_id=1, source_target_pairs={{0,0},{1,1},{2,6},{3,7},{4,2},{5,3},{6,4},{7,5},{8,8},{9,9},{10,14... | collective-permute-start | bytes 786440 | tf_op jit(solution)/shard_map/ppermute | solution.py:412
  118.8 22.1 %collective-permute-start.18 = (bf16[512,256]{1,0:T(8,128)(2,1)}, bf16[512,256]{1,0:T(8,128)(2,1)S(1)}, u32[]{:S(2)}, u32[]{:S(2)}) collective-permute-start(bf16[512,256]{1,0:T(8,128)(2,1)} %get-tuple-element.234), channel_id=1, source_target_pairs={{0,1},{1,0},{2,7},{3,6},{4,3},{5,2},{6,5},{7,4},{8,9},{9,8},{10,15... | collective-permute-start | bytes 786440 | tf_op jit(solution)/shard_map/ppermute | solution.py:412
  119.2 21.7 %collective-permute-start.19 = (bf16[512,256]{1,0:T(8,128)(2,1)}, bf16[512,256]{1,0:T(8,128)(2,1)S(1)}, u32[]{:S(2)}, u32[]{:S(2)}) collective-permute-start(bf16[512,256]{1,0:T(8,128)(2,1)} %get-tuple-element.233), channel_id=1, source_target_pairs={{0,2},{1,3},{2,4},{3,5},{4,0},{5,1},{6,6},{7,7},{8,10},{9,11},{10,... | collective-permute-start | bytes 786440 | tf_op jit(solution)/shard_map/ppermute | solution.py:412
  132.8 10.6 %collective-permute-start.20 = (bf16[512,256]{1,0:T(8,128)(2,1)}, bf16[512,256]{1,0:T(8,128)(2,1)}, u32[]{:S(2)}, u32[]{:S(2)}) collective-permute-start(bf16[512,256]{1,0:T(8,128)(2,1)} %get-tuple-element.232), channel_id=1, source_target_pairs={{0,3},{1,2},{2,5},{3,4},{4,1},{5,0},{6,7},{7,6},{8,11},{9,10},{10,... | collective-permute-start | bytes 786440 | tf_op jit(solution)/shard_map/ppermute | solution.py:412
  149.9 23.2 %collective-permute-start.25 = (bf16[2,4,2,2,1,32,1024]{6,5,4,3,2,1,0:T(8,128)(2,1)S(1)}, bf16[2,4,2,2,1,32,1024]{6,5,4,3,2,1,0:T(8,128)(2,1)S(1)}, u32[]{:S(2)}, u32[]{:S(2)}) collective-permute-start(bf16[2,4,2,2,1,32,1024]{6,5,4,3,2,1,0:T(8,128)(2,1)S(1)} %broadcast_select_fusion), channel_id=1, source_target_pairs={{0,4},{1,5},{2,6},{3,7},{4,0},{5,1},{6,2},{7,3},{8,12},{9,13},{10,... | collective-permute-start | bytes 6291464 | tf_op jit(solution)/shard_map/ppermute | solution.py:412
  157.2 20.6 %collective-permute-start.21 = (bf16[512,256]{1,0:T(8,128)(2,1)S(1)}, bf16[512,256]{1,0:T(8,128)(2,1)S(1)}, u32[]{:S(2)}, u32[]{:S(2)}) collective-permute-start(bf16[512,256]{1,0:T(8,128)(2,1)S(1)} %get-tuple-element.146), channel_id=1, source_target_pairs={{0,0},{1,1},{2,4},{3,5},{4,6},{5,7},{6,2},{7,3},{8,8},{9,9},{10,12... | collective-permute-start | bytes 786440 | tf_op jit(solution)/shard_map/ppermute | solution.py:412
  157.9 22.6 %collective-permute-start.22 = (bf16[512,256]{1,0:T(8,128)(2,1)S(1)}, bf16[512,256]{1,0:T(8,128)(2,1)S(1)}, u32[]{:S(2)}, u32[]{:S(2)}) collective-permute-start(bf16[512,256]{1,0:T(8,128)(2,1)S(1)} %get-tuple-element.147), channel_id=1, source_target_pairs={{0,1},{1,0},{2,5},{3,4},{4,7},{5,6},{6,3},{7,2},{8,9},{9,8},{10,13... | collective-permute-start | bytes 786440 | tf_op jit(solution)/shard_map/ppermute | solution.py:412
  162.0 24.3 %collective-permute-start.23 = (bf16[512,256]{1,0:T(8,128)(2,1)S(1)}, bf16[512,256]{1,0:T(8,128)(2,1)S(1)}, u32[]{:S(2)}, u32[]{:S(2)}) collective-permute-start(bf16[512,256]{1,0:T(8,128)(2,1)S(1)} %get-tuple-element.148), channel_id=1, source_target_pairs={{0,4},{1,5},{2,0},{3,1},{4,2},{5,3},{6,6},{7,7},{8,12},{9,13},{10,... | collective-permute-start | bytes 786440 | tf_op jit(solution)/shard_map/ppermute | solution.py:412
  167.1 19.1 %collective-permute-start.24 = (bf16[512,256]{1,0:T(8,128)(2,1)S(1)}, bf16[512,256]{1,0:T(8,128)(2,1)S(1)}, u32[]{:S(2)}, u32[]{:S(2)}) collective-permute-start(bf16[512,256]{1,0:T(8,128)(2,1)S(1)} %get-tuple-element.149), channel_id=1, source_target_pairs={{0,5},{1,4},{2,1},{3,0},{4,3},{5,2},{6,7},{7,6},{8,13},{9,12},{10,... | collective-permute-start | bytes 786440 | tf_op jit(solution)/shard_map/ppermute | solution.py:412
  174.9 14.6 %collective-permute-start.27 = (bf16[4,2,1,1,32,1024]{5,4,2,1,0,3:T(8,128)(2,1)S(1)}, bf16[4,2,1,1,32,1024]{5,4,2,1,0,3:T(8,128)(2,1)S(1)}, u32[]{:S(2)}, u32[]{:S(2)}) collective-permute-start(bf16[4,2,1,1,32,1024]{5,4,2,1,0,3:T(8,128)(2,1)S(1)} %broadcast_select_fusion.7), channel_id=1, source_target_pairs={{0,16},{1,17},{2,18},{3,19},{4,20},{5,21},{6,22},{7,23},{8,24},{9,... | collective-permute-start | bytes 1572872 | tf_op jit(solution)/shard_map/ppermute | solution.py:412
  177.8 13.5 %collective-permute-start.26 = (bf16[4,1,2,1,32,1024]{5,4,0,3,2,1:T(8,128)(2,1)S(1)}, bf16[4,1,2,1,32,1024]{5,4,0,3,2,1:T(8,128)(2,1)S(1)}, u32[]{:S(2)}, u32[]{:S(2)}) collective-permute-start(bf16[4,1,2,1,32,1024]{5,4,0,3,2,1:T(8,128)(2,1)S(1)} %broadcast_select_fusion.8), channel_id=1, source_target_pairs={{0,8},{1,9},{2,10},{3,11},{4,12},{5,13},{6,14},{7,15},{8,0},{9,1},... | collective-permute-start | bytes 1572872 | tf_op jit(solution)/shard_map/ppermute | solution.py:412
  191.6 25.7 %collective-permute-start.29 = (bf16[4,1,1,1,32,1024]{5,4,2,1,0,3:T(8,128)(2,1)S(1)}, bf16[4,1,1,1,32,1024]{5,4,2,1,0,3:T(8,128)(2,1)S(1)}, u32[]{:S(2)}, u32[]{:S(2)}) collective-permute-start(bf16[4,1,1,1,32,1024]{5,4,2,1,0,3:T(8,128)(2,1)S(1)} %broadcast_select_fusion.23), channel_id=1, source_target_pairs={{0,8},{1,9},{2,10},{3,11},{4,12},{5,13},{6,14},{7,15},{8,0},{9,1},... | collective-permute-start | bytes 786440 | tf_op jit(solution)/shard_map/ppermute | solution.py:412
  191.9 25.5 %collective-permute-start.28 = (bf16[4,1,1,1,32,1024]{5,4,0,3,2,1:T(8,128)(2,1)S(1)}, bf16[4,1,1,1,32,1024]{5,4,0,3,2,1:T(8,128)(2,1)S(1)}, u32[]{:S(2)}, u32[]{:S(2)}) collective-permute-start(bf16[4,1,1,1,32,1024]{5,4,0,3,2,1:T(8,128)(2,1)S(1)} %broadcast_select_fusion.24), channel_id=1, source_target_pairs={{0,16},{1,17},{2,18},{3,19},{4,20},{5,21},{6,22},{7,23},{8,24},{9,... | collective-permute-start | bytes 786440 | tf_op jit(solution)/shard_map/ppermute | solution.py:412
  220.5 15.2 %collective-permute-start.30 = (bf16[1024,1024]{1,0:T(8,128)(2,1)S(1)}, bf16[1024,1024]{1,0:T(8,128)(2,1)S(1)}, u32[]{:S(2)}, u32[]{:S(2)}) collective-permute-start(bf16[1024,1024]{1,0:T(8,128)(2,1)S(1)} %convolution_convert_fusion.1), channel_id=1, source_target_pairs={{0,4},{1,5},{2,6},{3,7},{4,0},{5,1},{6,2},{7,3},{8,12},{9,13},{10,... | collective-permute-start | bytes 6291464 | tf_op jit(solution)/shard_map/ppermute | solution.py:412
  221.8 13.8 %collective-permute-start.31 = (bf16[2,2,32,1024]{3,2,1,0:T(8,128)(2,1)S(1)}, bf16[2,2,32,1024]{3,2,1,0:T(8,128)(2,1)S(1)}, u32[]{:S(2)}, u32[]{:S(2)}) collective-permute-start(bf16[2,2,32,1024]{3,2,1,0:T(8,128)(2,1)S(1)} %slice.265), channel_id=1, source_target_pairs={{0,2},{1,3},{2,0},{3,1},{4,6},{5,7},{6,4},{7,5},{8,10},{9,11},{10,... | collective-permute-start | bytes 786440 | tf_op jit(solution)/shard_map/ppermute | solution.py:412
  236.8 15.6 %collective-permute-start.36 = (bf16[256,1024]{1,0:T(8,128)(2,1)S(1)}, bf16[256,1024]{1,0:T(8,128)(2,1)S(1)}, u32[]{:S(2)}, u32[]{:S(2)}) collective-permute-start(bf16[256,1024]{1,0:T(8,128)(2,1)S(1)} %slice.276), channel_id=1, source_target_pairs={{0,1},{1,0},{2,3},{3,2},{4,5},{5,4},{6,7},{7,6},{8,9},{9,8},{10,11... | collective-permute-start | bytes 1572872 | tf_op jit(solution)/shard_map/ppermute | solution.py:412
  239.0 10.5 %collective-permute-start.34 = (bf16[2,1,2,96,512]{4,3,2,1,0:T(8,128)(2,1)S(1)}, bf16[2,1,2,96,512]{4,3,2,1,0:T(8,128)(2,1)S(1)}, u32[]{:S(2)}, u32[]{:S(2)}) collective-permute-start(bf16[2,1,2,96,512]{4,3,2,1,0:T(8,128)(2,1)S(1)} %broadcast_select_fusion.17), channel_id=1, source_target_pairs={{0,16},{1,17},{2,18},{3,19},{4,20},{5,21},{6,22},{7,23},{8,24},{9,... | collective-permute-start | bytes 1179656 | tf_op jit(solution)/shard_map/ppermute | solution.py:412
  240.4 10.4 %collective-permute-start.32 = (bf16[1,2,2,96,512]{4,3,2,1,0:T(8,128)(2,1)S(1)}, bf16[1,2,2,96,512]{4,3,2,1,0:T(8,128)(2,1)S(1)}, u32[]{:S(2)}, u32[]{:S(2)}) collective-permute-start(bf16[1,2,2,96,512]{4,3,2,1,0:T(8,128)(2,1)S(1)} %broadcast_select_fusion.18), channel_id=1, source_target_pairs={{0,8},{1,9},{2,10},{3,11},{4,12},{5,13},{6,14},{7,15},{8,0},{9,1},... | collective-permute-start | bytes 1179656 | tf_op jit(solution)/shard_map/ppermute | solution.py:412
  256.9 12.7 %collective-permute-start.38 = (bf16[1,1,2,96,1024]{4,3,2,1,0:T(8,128)(2,1)S(1)}, bf16[1,1,2,96,1024]{4,3,2,1,0:T(8,128)(2,1)S(1)}, u32[]{:S(2)}, u32[]{:S(2)}) collective-permute-start(bf16[1,1,2,96,1024]{4,3,2,1,0:T(8,128)(2,1)S(1)} %pad_maximum_fusion.8), channel_id=1, source_target_pairs={{0,0},{1,1},{2,2},{3,3},{4,6},{5,7},{6,4},{7,5},{8,8},{9,9},{10,10... | collective-permute-start | bytes 1179656 | tf_op jit(solution)/shard_map/ppermute | solution.py:412
  258.4 11.2 %collective-permute-start.39 = (bf16[64,1024]{1,0:T(8,128)(2,1)S(1)}, bf16[64,1024]{1,0:T(8,128)(2,1)S(1)}, u32[]{:S(2)}, u32[]{:S(2)}) collective-permute-start(bf16[64,1024]{1,0:T(8,128)(2,1)S(1)} %get-tuple-element.249), channel_id=1, source_target_pairs={{0,2},{1,3},{2,0},{3,1},{4,6},{5,7},{6,4},{7,5},{8,10},{9,11},{10,... | collective-permute-start | bytes 393224 | tf_op jit(solution)/shard_map/ppermute | solution.py:412
  274.5 9.2 %collective-permute-start.41 = (bf16[64,1024]{1,0:T(8,128)(2,1)S(1)}, bf16[64,1024]{1,0:T(8,128)(2,1)S(1)}, u32[]{:S(2)}, u32[]{:S(2)}) collective-permute-start(bf16[64,1024]{1,0:T(8,128)(2,1)S(1)} %get-tuple-element.184), channel_id=1, source_target_pairs={{0,2},{1,3},{2,0},{3,1},{4,6},{5,7},{6,4},{7,5},{8,10},{9,11},{10,... | collective-permute-start | bytes 393224 | tf_op jit(solution)/shard_map/ppermute | solution.py:412
  286.9 9.7 %collective-permute-start.46 = (bf16[128,1024]{1,0:T(8,128)(2,1)S(1)}, bf16[128,1024]{1,0:T(8,128)(2,1)S(1)}, u32[]{:S(2)}, u32[]{:S(2)}) collective-permute-start(bf16[128,1024]{1,0:T(8,128)(2,1)S(1)} %slice.247), channel_id=1, source_target_pairs={{0,1},{1,0},{2,3},{3,2},{4,5},{5,4},{6,7},{7,6},{8,9},{9,8},{10,11... | collective-permute-start | bytes 786440 | tf_op jit(solution)/shard_map/ppermute | solution.py:412
  287.0 9.7 %collective-permute-start.45 = (bf16[64,1024]{1,0:T(8,128)(2,1)S(1)}, bf16[64,1024]{1,0:T(8,128)(2,1)S(1)}, u32[]{:S(2)}, u32[]{:S(2)}) collective-permute-start(bf16[64,1024]{1,0:T(8,128)(2,1)S(1)} %get-tuple-element.193), channel_id=1, source_target_pairs={{0,2},{1,3},{2,0},{3,1},{4,6},{5,7},{6,4},{7,5},{8,10},{9,11},{10,... | collective-permute-start | bytes 393224 | tf_op jit(solution)/shard_map/ppermute | solution.py:412
  296.7 9.4 %collective-permute-start.48 = (bf16[2,1,1,176,512]{4,3,2,1,0:T(8,128)(2,1)S(1)}, bf16[2,1,1,176,512]{4,3,2,1,0:T(8,128)(2,1)S(1)}, u32[]{:S(2)}, u32[]{:S(2)}) collective-permute-start(bf16[2,1,1,176,512]{4,3,2,1,0:T(8,128)(2,1)S(1)} %pad_maximum_fusion.10), channel_id=1, source_target_pairs={{0,16},{1,17},{2,18},{3,19},{4,20},{5,21},{6,22},{7,23},{8,24},{9,... | collective-permute-start | bytes 1081352 | tf_op jit(solution)/shard_map/ppermute | solution.py:412
  317.5 9.2 %collective-permute-start.53 = (f32[2,1024]{1,0:T(2,128)S(1)}, f32[2,1024]{1,0:T(2,128)S(1)}, u32[]{:S(2)}, u32[]{:S(2)}) collective-permute-start(f32[2,1024]{1,0:T(2,128)S(1)} %slice_add_fusion), channel_id=1, source_target_pairs={{0,1},{1,0},{2,3},{3,2},{4,5},{5,4},{6,7},{7,6},{8,9},{9,8},{10,11... | collective-permute-start | bytes 24584 | tf_op jit(solution)/shard_map/ppermute | solution.py:412
  317.6 9.1 %collective-permute-start.54 = (f32[2,1024]{1,0:T(2,128)S(1)}, f32[2,1024]{1,0:T(2,128)S(1)}, u32[]{:S(2)}, u32[]{:S(2)}) collective-permute-start(f32[2,1024]{1,0:T(2,128)S(1)} %slice_add_fusion), channel_id=1, source_target_pairs={{0,2},{1,3},{2,0},{3,1},{4,6},{5,7},{6,4},{7,5},{8,10},{9,11},{10,... | collective-permute-start | bytes 24584 | tf_op jit(solution)/shard_map/ppermute | solution.py:412
  317.7 9.0 %collective-permute-start.55 = (f32[2,1024]{1,0:T(2,128)S(1)}, f32[2,1024]{1,0:T(2,128)S(1)}, u32[]{:S(2)}, u32[]{:S(2)}) collective-permute-start(f32[2,1024]{1,0:T(2,128)S(1)} %slice_add_fusion), channel_id=1, source_target_pairs={{0,3},{1,2},{2,1},{3,0},{4,7},{5,6},{6,5},{7,4},{8,11},{9,10},{10,... | collective-permute-start | bytes 24584 | tf_op jit(solution)/shard_map/ppermute | solution.py:412
  (67 other events, 448.9 us)
Sparse Core Ops, SparseCore 0:
  18.7 82.0 all-gather.2

commit v4 on v3

--- a/solution.py
+++ b/solution.py
@@ -58,7 +58,8 @@
     nh, dim, rows, blocks, low, held, sent, slopes, starts_ref, w_ref, *refs
 ):
     pieces = refs[:blocks]
-    out_ref, act_hbm, pre_hbm, dist, acc, act_ref, pre_ref, sems = refs[blocks:]
+    outs = refs[blocks : blocks + blocks // 2]
+    act_hbm, pre_hbm, dist, acc, act_ref, pre_ref, sems, out_ref = refs[blocks + blocks // 2 :]
     for b in range(blocks):
         pre = dot(pieces[b][...], w_ref[...], NT)
         half = 0.5 * pre
@@ -95,6 +96,8 @@
         return carry
 
     lax.fori_loop(0, blocks, query_block, 0)
+    for r, ref in enumerate(outs):
+        ref[...] = out_ref[2 * r * rows : 2 * (r + 1) * rows, :]
     act_copy.wait()
     pre_copy.wait()
 
@@ -177,15 +180,17 @@
     vmem = pl.BlockSpec(memory_space=pltpu.VMEM)
     return pl.pallas_call(
         functools.partial(forward_kernel, nh, dim, rows, blocks),
-        out_shape=(jax.ShapeDtypeStruct((total, nh * dim), BF), wide, wide),
+        out_shape=(jax.ShapeDtypeStruct((2 * rows, nh * dim), BF),) * (blocks // 2)
+        + (wide, wide),
         in_specs=[smem] * 4 + [vmem] * (2 + blocks),
-        out_specs=(vmem,) + (pl.BlockSpec(memory_space=pltpu.HBM),) * 2,
+        out_specs=(vmem,) * (blocks // 2) + (pl.BlockSpec(memory_space=pltpu.HBM),) * 2,
         scratch_shapes=[
             pltpu.VMEM((blocks, rows, rows), F32),
             pltpu.VMEM((rows, nh * dim), F32),
             pltpu.VMEM(wide.shape, BF),
             pltpu.VMEM(wide.shape, BF),
             pltpu.SemaphoreType.DMA((2,)),
+            pltpu.VMEM((total, nh * dim), BF),
         ],
         compiler_params=pltpu.CompilerParams(vmem_limit_bytes=40 * 2**20),
         cost_estimate=attention_cost(nh, dim, total, 2),
@@ -538,16 +543,16 @@
 
     w_qkv = jnp.where(c == 0, w_own, piece)
 
-    attended, act, pre = attend(
+    *attended, act, pre = attend(
         nh, dim, rows, tables, slopes, starts, w_qkv, mine + theirs
     )
     w_gate, w_out, pre_gate, d_gated = prepare(
-        n, n_dp, slab_o, z, everything, normed, cotangent, attended
+        n, n_dp, slab_o, z, everything, normed, cotangent, attended[0]
     )
     mine, theirs, attended = barrier((mine, theirs, attended))
     gathered = jnp.concatenate(mine + theirs, axis=0)
     arrived = [
-        move(attended[r * local_rows : (r + 1) * local_rows], send_target(r)) for r in range(n)
+        move(attended[r], send_target(r)) for r in range(n)
     ]
     arrived, w_gate, w_out, pre_gate, d_gated = barrier(
         (arrived, w_gate, w_out, pre_gate, d_gated)

time: 339 us -> 345 us (1.018)
  other arithmetic: 23.1 us -> 29.4 us
    convert_element_type x16, other arithmetic: 4.29 us -> 8.11 us  [add(): return (x.astype(F32) + y.astype(F32)).astype(BF)]
  transfers between devices with their start and end apart: 57 -> 57, of which waited for: 29 -> 26; matrix products, arithmetic and copies ran while one was open for 11% -> 13% of each run, Pallas kernels for 15% -> 15%
where the time goes in v4:
time: 345 us; the launch traced here: 341 us
  waiting for transfers between devices  116 us (34%)
  starting transfers between devices  79.8 us (23%)
  Pallas kernels  61.1 us (18%)
  other arithmetic  29.4 us (9%)
  local copies, waits for them, and re-layouts  27.1 us (8%)
  between operations  15.6 us (5%)
  matrix products  12 us (3%)
    ppermute x56, waiting for transfers between devices, move(): return lax.ppermute(x, AXES, pairs)  116 us
    ppermute x56, starting transfers between devices, move(): return lax.ppermute(x, AXES, pairs)  79.8 us
    pallas_call x1, Pallas kernels, attend_back(): pl.pallas_call(functools.partial(backward_kernel, nh, dim, rows, blocks),...  24.2 us
    pallas_call x1, Pallas kernels, attend(): pl.pallas_call(functools.partial(forward_kernel, nh, dim, rows, blocks),...  20 us
    unnamed x99, local copies, waits for them, and re-layouts  14.9 us
    dot_general x5, matrix products, dot(): return lax.dot_general(a, b, dims, preferred_element_type=F32)  12 us
    convert_element_type x16, other arithmetic, add(): return (x.astype(F32) + y.astype(F32)).astype(BF)  8.11 us
  transfers between devices with their start and end apart: 57, of which 26 were waited for; matrix products, arithmetic and copies ran while one was open for 13% of the time, Pallas kernels for 15%

profile of v4, /device:TPU:0, one launch (start us, length us, event | category | flops | bytes accessed | tf_op | source)
XLA Modules:
  0.0 341.0 jit_solution(3406441219315717288)
XLA Ops:
  12.3 3.3 shard_map.118
  19.9 3.6 %collective-permute-start.3 = (bf16[96,1024]{1,0:T(8,128)(2,1)}, bf16[96,1024]{1,0:T(8,128)(2,1)S(1)}, u32[]{:S(2)}, u32[]{:S(2)}) collective-permute-start(bf16[96,1024]{1,0:T(8,128)(2,1)} %get-tuple-element.235), channel_id=1, source_target_pairs={{0,2},{1,3},{2,0},{3,1},{4,6},{5,7},{6,4},{7,5},{8,10},{9,11},{10,... | collective-permute-start | bytes 589832 | tf_op jit(solution)/shard_map/ppermute | solution.py:417
  29.2 4.3 %collective-permute-done.3 = bf16[96,1024]{1,0:T(8,128)(2,1)S(1)} collective-permute-done((bf16[96,1024]{1,0:T(8,128)(2,1)}, bf16[96,1024]{1,0:T(8,128)(2,1)S(1)}, u32[]{:S(2)}, u32[]{:S(2)}) %collective-permute-start.3) | collective-permute-done | bytes 196640 | tf_op jit(solution)/shard_map/ppermute | solution.py:417
  33.5 22.0 %collective-permute-done.1.refs_1_ = bf16[256,1024]{1,0:T(8,128)(2,1)} collective-permute-done((bf16[256,1024]{1,0:T(8,128)(2,1)S(1)}, bf16[256,1024]{1,0:T(8,128)(2,1)}, u32[]{:S(2)}, u32[]{:S(2)}) %collective-permute-start.1) | collective-permute-done | bytes 524320 | tf_op jit(solution)/shard_map/ppermute | solution.py:417
  55.5 3.3 collective-permute-done.2
  67.2 8.7 %collective-permute-done.6 = bf16[128,1024]{1,0:T(8,128)(2,1)S(1)} collective-permute-done((bf16[128,1024]{1,0:T(8,128)(2,1)S(1)}, bf16[128,1024]{1,0:T(8,128)(2,1)S(1)}, u32[]{:S(2)}, u32[]{:S(2)}) %collective-permute-start.6) | collective-permute-done | bytes 262176 | tf_op jit(solution)/shard_map/ppermute | solution.py:417
  76.6 5.7 %collective-permute-done.11 = bf16[1,2,1,96,512]{4,3,2,1,0:T(8,128)(2,1)S(1)} collective-permute-done((bf16[1,2,1,96,512]{4,3,2,1,0:T(8,128)(2,1)S(1)}, bf16[1,2,1,96,512]{4,3,2,1,0:T(8,128)(2,1)S(1)}, u32[]{:S(2)}, u32[]{:S(2)}) %collective-permute-start.11) | collective-permute-done | bytes 196640 | tf_op jit(solution)/shard_map/ppermute | solution.py:417
  94.1 20.0 %shard_map.119 = (bf16[512,256]{1,0:T(8,128)(2,1)}, bf16[512,256]{1,0:T(8,128)(2,1)}, bf16[512,256]{1,0:T(8,128)(2,1)}, bf16[512,256]{1,0:T(8,128)(2,1)S(1)}, bf...) custom-call(s32[8]{0:T(128)S(1)} %get-tuple-element.132.low, s32[8]{0:T(128)S(1)} %multiply_add_fusion.1.held, ...), custom_call_target="tpu_custom_call" | custom-call | flops 12884889600 | bytes 4194304 | tf_op jit(solution)/shard_map/pallas_call | solution.py:181
  119.4 13.6 %collective-permute-start.19 = (bf16[512,256]{1,0:T(8,128)(2,1)}, bf16[512,256]{1,0:T(8,128)(2,1)}, u32[]{:S(2)}, u32[]{:S(2)}) collective-permute-start(bf16[512,256]{1,0:T(8,128)(2,1)} %get-tuple-element.145), channel_id=1, source_target_pairs={{0,2},{1,3},{2,4},{3,5},{4,0},{5,1},{6,6},{7,7},{8,10},{9,11},{10,... | collective-permute-start | bytes 786440 | tf_op jit(solution)/shard_map/ppermute | solution.py:417
  137.5 2.4 shard_map.120
  140.1 3.1 collective-permute-done.20.refs_3_
  143.2 6.5 %shard_map.121 = (bf16[512,256]{1,0:T(8,128)(2,1)S(1)}, bf16[512,256]{1,0:T(8,128)(2,1)S(1)}, bf16[512,256]{1,0:T(8,128)(2,1)S(1)}, bf16[512,256]{1,0:T(8,128)(2...) custom-call(f32[512,1024]{1,0:T(8,128)S(1)} %get-tuple-element.152.pre_gat, ...), custom_call_target="tpu_custom_call" | custom-call | flops 4294967296 | bytes 16777216 | tf_op jit(solution)/shard_map/pallas_call | solution.py:317
  150.0 6.3 %collective-permute-start.25 = (bf16[2,4,2,2,1,32,1024]{6,5,4,3,2,1,0:T(8,128)(2,1)S(1)}, bf16[2,4,2,2,1,32,1024]{6,5,4,3,2,1,0:T(8,128)(2,1)S(1)}, u32[]{:S(2)}, u32[]{:S(2)}) collective-permute-start(bf16[2,4,2,2,1,32,1024]{6,5,4,3,2,1,0:T(8,128)(2,1)S(1)} %broadcast_select_fusion), channel_id=1, source_target_pairs={{0,4},{1,5},{2,6},{3,7},{4,0},{5,1},{6,2},{7,3},{8,12},{9,13},{10,... | collective-permute-start | bytes 6291464 | tf_op jit(solution)/shard_map/ppermute | solution.py:417
  158.1 4.0 %collective-permute-start.22 = (bf16[512,256]{1,0:T(8,128)(2,1)S(1)}, bf16[512,256]{1,0:T(8,128)(2,1)S(1)}, u32[]{:S(2)}, u32[]{:S(2)}) collective-permute-start(bf16[512,256]{1,0:T(8,128)(2,1)S(1)} %get-tuple-element.159), channel_id=1, source_target_pairs={{0,1},{1,0},{2,5},{3,4},{4,7},{5,6},{6,3},{7,2},{8,9},{9,8},{10,13... | collective-permute-start | bytes 786440 | tf_op jit(solution)/shard_map/ppermute | solution.py:417
  162.1 5.1 %collective-permute-start.23 = (bf16[512,256]{1,0:T(8,128)(2,1)S(1)}, bf16[512,256]{1,0:T(8,128)(2,1)S(1)}, u32[]{:S(2)}, u32[]{:S(2)}) collective-permute-start(bf16[512,256]{1,0:T(8,128)(2,1)S(1)} %get-tuple-element.160), channel_id=1, source_target_pairs={{0,4},{1,5},{2,0},{3,1},{4,2},{5,3},{6,6},{7,7},{8,12},{9,13},{10,... | collective-permute-start | bytes 786440 | tf_op jit(solution)/shard_map/ppermute | solution.py:417
  167.3 3.7 %collective-permute-start.24 = (bf16[512,256]{1,0:T(8,128)(2,1)S(1)}, bf16[512,256]{1,0:T(8,128)(2,1)S(1)}, u32[]{:S(2)}, u32[]{:S(2)}) collective-permute-start(bf16[512,256]{1,0:T(8,128)(2,1)S(1)} %get-tuple-element.161), channel_id=1, source_target_pairs={{0,5},{1,4},{2,1},{3,0},{4,3},{5,2},{6,7},{7,6},{8,13},{9,12},{10,... | collective-permute-start | bytes 786440 | tf_op jit(solution)/shard_map/ppermute | solution.py:417
  177.5 2.6 fusion.23
  180.1 6.3 %collective-permute-done.23 = bf16[512,256]{1,0:T(8,128)(2,1)S(1)} collective-permute-done((bf16[512,256]{1,0:T(8,128)(2,1)S(1)}, bf16[512,256]{1,0:T(8,128)(2,1)S(1)}, u32[]{:S(2)}, u32[]{:S(2)}) %collective-permute-start.23) | collective-permute-done | bytes 262176 | tf_op jit(solution)/shard_map/ppermute | solution.py:417
  186.5 2.7 collective-permute-done.27
  193.2 24.2 %shard_map.122 = (bf16[2048,768]{1,0:T(8,128)(2,1)S(1)}, f32[2,8,256]{2,1,0:T(8,128)S(1)}) custom-call(s32[8]{0:T(128)S(1)} %get-tuple-element.132.low, s32[8]{0:T(128)S(1)} %multiply_add_fusion.1.held, s32[8]{0:T(128)S(1)} %get-tuple-element.134.sent, f32[2]{0:T(128)S(1)} %collective-permute-done.5.slopes, s32[8,1,256]{2,1,0:T(1,128)S(1)} %bitcast.72, ...), custom_call_target="tpu_custom_call" | custom-call | flops 32212224000 | bytes 10485760 | tf_op jit(solution)/shard_map/pallas_call | solution.py:377
  222.1 3.6 %convolution_convert_fusion.2 = bf16[768,1024]{1,0:T(8,128)(2,1)S(1)} fusion(bf16[2048,768]{1,0:T(8,128)(2,1)S(1)} %get-tuple-element.175, bf16[2048,1024]{1,0:T(8,128)(2,1)S(1)} %constant_dynamic-update-slice_fusion.6), kind=kOutput, calls=%fused_computation.22 | convolution fusion | flops 3222011904 | bytes 8912896 | tf_op jit(solution)/shard_map/dot_general | solution.py:20
  227.5 7.7 %collective-permute-done.31 = bf16[2,2,32,1024]{3,2,1,0:T(8,128)(2,1)S(1)} collective-permute-done((bf16[2,2,32,1024]{3,2,1,0:T(8,128)(2,1)S(1)}, bf16[2,2,32,1024]{3,2,1,0:T(8,128)(2,1)S(1)}, u32[]{:S(2)}, u32[]{:S(2)}) %collective-permute-start.31) | collective-permute-done | bytes 262176 | tf_op jit(solution)/shard_map/ppermute | solution.py:417
  241.8 8.3 %collective-permute-done.34 = bf16[2,1,2,96,512]{4,3,2,1,0:T(8,128)(2,1)S(1)} collective-permute-done((bf16[2,1,2,96,512]{4,3,2,1,0:T(8,128)(2,1)S(1)}, bf16[2,1,2,96,512]{4,3,2,1,0:T(8,128)(2,1)S(1)}, u32[]{:S(2)}, u32[]{:S(2)}) %collective-permute-start.34) | collective-permute-done | bytes 393248 | tf_op jit(solution)/shard_map/ppermute | solution.py:417
  252.9 3.1 collective-permute-done.35
  261.9 8.8 %collective-permute-done.39 = bf16[64,1024]{1,0:T(8,128)(2,1)S(1)} collective-permute-done((bf16[64,1024]{1,0:T(8,128)(2,1)S(1)}, bf16[64,1024]{1,0:T(8,128)(2,1)S(1)}, u32[]{:S(2)}, u32[]{:S(2)}) %collective-permute-start.39) | collective-permute-done | bytes 131104 | tf_op jit(solution)/shard_map/ppermute | solution.py:417
  271.8 4.0 %collective-permute-start.40 = (bf16[1,1,1,96,1024]{4,3,2,1,0:T(8,128)(2,1)S(1)}, bf16[1,1,1,96,1024]{4,3,2,1,0:T(8,128)(2,1)}, u32[]{:S(2)}, u32[]{:S(2)}) collective-permute-start(bf16[1,1,1,96,1024]{4,3,2,1,0:T(8,128)(2,1)S(1)} %broadcast_select_fusion.26), channel_id=1, source_target_pairs={{0,4},{1,5},{2,6},{3,7},{4,0},{5,1},{6,2},{7,3},{8,12},{9,13},{10,... | collective-permute-start | bytes 589832 | tf_op jit(solution)/shard_map/ppermute | solution.py:417
  280.9 6.2 %collective-permute-done.41 = bf16[64,1024]{1,0:T(8,128)(2,1)S(1)} collective-permute-done((bf16[64,1024]{1,0:T(8,128)(2,1)}, bf16[64,1024]{1,0:T(8,128)(2,1)S(1)}, u32[]{:S(2)}, u32[]{:S(2)}) %collective-permute-start.41) | collective-permute-done | bytes 131104 | tf_op jit(solution)/shard_map/ppermute | solution.py:417
  296.0 5.6 %collective-permute-done.46 = bf16[128,1024]{1,0:T(8,128)(2,1)S(1)} collective-permute-done((bf16[128,1024]{1,0:T(8,128)(2,1)S(1)}, bf16[128,1024]{1,0:T(8,128)(2,1)S(1)}, u32[]{:S(2)}, u32[]{:S(2)}) %collective-permute-start.46) | collective-permute-done | bytes 262176 | tf_op jit(solution)/shard_map/ppermute | solution.py:417
  304.8 7.0 %collective-permute-done.48 = bf16[2,1,1,176,512]{4,3,2,1,0:T(8,128)(2,1)S(1)} collective-permute-done((bf16[2,1,1,176,512]{4,3,2,1,0:T(8,128)(2,1)S(1)}, bf16[2,1,1,176,512]{4,3,2,1,0:T(8,128)(2,1)S(1)}, u32[]{:S(2)}, u32[]{:S(2)}) %collective-permute-start.48) | collective-permute-done | bytes 360480 | tf_op jit(solution)/shard_map/ppermute | solution.py:417
  316.2 2.4 collective-permute-done.50
  323.5 2.8 collective-permute-start.54
  327.9 4.7 %shard_map.123 = (f32[1024,8,128]{2,1,0:T(8,128)}, f32[256,1024]{1,0:T(8,128)}) custom-call(bf16[8,176,512]{2,1,0:T(8,128)(2,1)S(1)} %bitcast.67, bf16[8,176,512]{2,1,0:T(8,128)(2,1)S(1)} %bitcast.69), custom_call_target="tpu_custom_call" | custom-call | flops 10000000000 | bytes 8388608 | tf_op jit(solution)/shard_map/pallas_call | solution.py:356
  (303 shorter events, 109.6 us)
Async XLA Ops:
  7.2 128.2 %all-gather.3.cloned.1.call-start = ((), (), s32[]{:S(2)}) async-start(), calls=%async_computation | async-start | bytes 4325376 | tf_op jit(solution)/shard_map/all_gather | solution.py:542
  19.9 13.7 %collective-permute-start.3 = (bf16[96,1024]{1,0:T(8,128)(2,1)}, bf16[96,1024]{1,0:T(8,128)(2,1)S(1)}, u32[]{:S(2)}, u32[]{:S(2)}) collective-permute-start(bf16[96,1024]{1,0:T(8,128)(2,1)} %get-tuple-element.235), channel_id=1, source_target_pairs={{0,2},{1,3},{2,0},{3,1},{4,6},{5,7},{6,4},{7,5},{8,10},{9,11},{10,... | collective-permute-start | bytes 589832 | tf_op jit(solution)/shard_map/ppermute | solution.py:417
  26.8 28.7 %collective-permute-start.1 = (bf16[256,1024]{1,0:T(8,128)(2,1)S(1)}, bf16[256,1024]{1,0:T(8,128)(2,1)}, u32[]{:S(2)}, u32[]{:S(2)}) collective-permute-start(bf16[256,1024]{1,0:T(8,128)(2,1)S(1)} %get-tuple-element.176.refs_0_), channel_id=1, source_target_pairs={{0,1},{1,0},{2,3},{3,2},{4,5},{5,4},{6,7},{7,6},{8,9},{9,8},{10,11... | collective-permute-start | bytes 1572872 | tf_op jit(solution)/shard_map/ppermute | solution.py:417
  28.4 30.4 %collective-permute-start.2 = (bf16[256,1024]{1,0:T(8,128)(2,1)}, bf16[256,1024]{1,0:T(8,128)(2,1)}, u32[]{:S(2)}, u32[]{:S(2)}) collective-permute-start(bf16[256,1024]{1,0:T(8,128)(2,1)} %get-tuple-element.238), channel_id=1, source_target_pairs={{0,2},{1,3},{2,0},{3,1},{4,6},{5,7},{6,4},{7,5},{8,10},{9,11},{10,... | collective-permute-start | bytes 1572872 | tf_op jit(solution)/shard_map/ppermute | solution.py:417
  63.1 12.9 %collective-permute-start.6 = (bf16[128,1024]{1,0:T(8,128)(2,1)S(1)}, bf16[128,1024]{1,0:T(8,128)(2,1)S(1)}, u32[]{:S(2)}, u32[]{:S(2)}) collective-permute-start(bf16[128,1024]{1,0:T(8,128)(2,1)S(1)} %get-tuple-element.128), channel_id=1, source_target_pairs={{0,1},{1,0},{2,3},{3,2},{4,5},{5,4},{6,7},{7,6},{8,9},{9,8},{10,11... | collective-permute-start | bytes 786440 | tf_op jit(solution)/shard_map/ppermute | solution.py:417
  117.5 22.4 %collective-permute-start.17 = (bf16[512,256]{1,0:T(8,128)(2,1)}, bf16[512,256]{1,0:T(8,128)(2,1)S(1)}, u32[]{:S(2)}, u32[]{:S(2)}) collective-permute-start(bf16[512,256]{1,0:T(8,128)(2,1)} %get-tuple-element.143.after_ref), channel_id=1, source_target_pairs={{0,0},{1,1},{2,6},{3,7},{4,2},{5,3},{6,4},{7,5},{8,8},{9,9},{10,14... | collective-permute-start | bytes 786440 | tf_op jit(solution)/shard_map/ppermute | solution.py:417
  119.1 20.8 %collective-permute-start.18 = (bf16[512,256]{1,0:T(8,128)(2,1)}, bf16[512,256]{1,0:T(8,128)(2,1)S(1)}, u32[]{:S(2)}, u32[]{:S(2)}) collective-permute-start(bf16[512,256]{1,0:T(8,128)(2,1)} %get-tuple-element.144), channel_id=1, source_target_pairs={{0,1},{1,0},{2,7},{3,6},{4,3},{5,2},{6,5},{7,4},{8,9},{9,8},{10,15... | collective-permute-start | bytes 786440 | tf_op jit(solution)/shard_map/ppermute | solution.py:417
  119.4 20.7 %collective-permute-start.19 = (bf16[512,256]{1,0:T(8,128)(2,1)}, bf16[512,256]{1,0:T(8,128)(2,1)}, u32[]{:S(2)}, u32[]{:S(2)}) collective-permute-start(bf16[512,256]{1,0:T(8,128)(2,1)} %get-tuple-element.145), channel_id=1, source_target_pairs={{0,2},{1,3},{2,4},{3,5},{4,0},{5,1},{6,6},{7,7},{8,10},{9,11},{10,... | collective-permute-start | bytes 786440 | tf_op jit(solution)/shard_map/ppermute | solution.py:417
  133.0 10.2 %collective-permute-start.20 = (bf16[512,256]{1,0:T(8,128)(2,1)S(1)}, bf16[512,256]{1,0:T(8,128)(2,1)}, u32[]{:S(2)}, u32[]{:S(2)}) collective-permute-start(bf16[512,256]{1,0:T(8,128)(2,1)S(1)} %get-tuple-element.146), channel_id=1, source_target_pairs={{0,3},{1,2},{2,5},{3,4},{4,1},{5,0},{6,7},{7,6},{8,11},{9,10},{10,... | collective-permute-start | bytes 786440 | tf_op jit(solution)/shard_map/ppermute | solution.py:417
  150.0 23.3 %collective-permute-start.25 = (bf16[2,4,2,2,1,32,1024]{6,5,4,3,2,1,0:T(8,128)(2,1)S(1)}, bf16[2,4,2,2,1,32,1024]{6,5,4,3,2,1,0:T(8,128)(2,1)S(1)}, u32[]{:S(2)}, u32[]{:S(2)}) collective-permute-start(bf16[2,4,2,2,1,32,1024]{6,5,4,3,2,1,0:T(8,128)(2,1)S(1)} %broadcast_select_fusion), channel_id=1, source_target_pairs={{0,4},{1,5},{2,6},{3,7},{4,0},{5,1},{6,2},{7,3},{8,12},{9,13},{10,... | collective-permute-start | bytes 6291464 | tf_op jit(solution)/shard_map/ppermute | solution.py:417
  157.5 19.9 %collective-permute-start.21 = (bf16[512,256]{1,0:T(8,128)(2,1)S(1)}, bf16[512,256]{1,0:T(8,128)(2,1)S(1)}, u32[]{:S(2)}, u32[]{:S(2)}) collective-permute-start(bf16[512,256]{1,0:T(8,128)(2,1)S(1)} %get-tuple-element.158), channel_id=1, source_target_pairs={{0,0},{1,1},{2,4},{3,5},{4,6},{5,7},{6,2},{7,3},{8,8},{9,9},{10,12... | collective-permute-start | bytes 786440 | tf_op jit(solution)/shard_map/ppermute | solution.py:417
  158.1 21.9 %collective-permute-start.22 = (bf16[512,256]{1,0:T(8,128)(2,1)S(1)}, bf16[512,256]{1,0:T(8,128)(2,1)S(1)}, u32[]{:S(2)}, u32[]{:S(2)}) collective-permute-start(bf16[512,256]{1,0:T(8,128)(2,1)S(1)} %get-tuple-element.159), channel_id=1, source_target_pairs={{0,1},{1,0},{2,5},{3,4},{4,7},{5,6},{6,3},{7,2},{8,9},{9,8},{10,13... | collective-permute-start | bytes 786440 | tf_op jit(solution)/shard_map/ppermute | solution.py:417
  162.1 24.3 %collective-permute-start.23 = (bf16[512,256]{1,0:T(8,128)(2,1)S(1)}, bf16[512,256]{1,0:T(8,128)(2,1)S(1)}, u32[]{:S(2)}, u32[]{:S(2)}) collective-permute-start(bf16[512,256]{1,0:T(8,128)(2,1)S(1)} %get-tuple-element.160), channel_id=1, source_target_pairs={{0,4},{1,5},{2,0},{3,1},{4,2},{5,3},{6,6},{7,7},{8,12},{9,13},{10,... | collective-permute-start | bytes 786440 | tf_op jit(solution)/shard_map/ppermute | solution.py:417
  167.3 19.1 %collective-permute-start.24 = (bf16[512,256]{1,0:T(8,128)(2,1)S(1)}, bf16[512,256]{1,0:T(8,128)(2,1)S(1)}, u32[]{:S(2)}, u32[]{:S(2)}) collective-permute-start(bf16[512,256]{1,0:T(8,128)(2,1)S(1)} %get-tuple-element.161), channel_id=1, source_target_pairs={{0,5},{1,4},{2,1},{3,0},{4,3},{5,2},{6,7},{7,6},{8,13},{9,12},{10,... | collective-permute-start | bytes 786440 | tf_op jit(solution)/shard_map/ppermute | solution.py:417
  175.1 14.0 %collective-permute-start.27 = (bf16[4,2,1,1,32,1024]{5,4,2,1,0,3:T(8,128)(2,1)S(1)}, bf16[4,2,1,1,32,1024]{5,4,2,1,0,3:T(8,128)(2,1)S(1)}, u32[]{:S(2)}, u32[]{:S(2)}) collective-permute-start(bf16[4,2,1,1,32,1024]{5,4,2,1,0,3:T(8,128)(2,1)S(1)} %broadcast_select_fusion.7), channel_id=1, source_target_pairs={{0,16},{1,17},{2,18},{3,19},{4,20},{5,21},{6,22},{7,23},{8,24},{9,... | collective-permute-start | bytes 1572872 | tf_op jit(solution)/shard_map/ppermute | solution.py:417
  177.4 13.5 %collective-permute-start.26 = (bf16[4,1,2,1,32,1024]{5,4,0,3,2,1:T(8,128)(2,1)S(1)}, bf16[4,1,2,1,32,1024]{5,4,0,3,2,1:T(8,128)(2,1)S(1)}, u32[]{:S(2)}, u32[]{:S(2)}) collective-permute-start(bf16[4,1,2,1,32,1024]{5,4,0,3,2,1:T(8,128)(2,1)S(1)} %broadcast_select_fusion.8), channel_id=1, source_target_pairs={{0,8},{1,9},{2,10},{3,11},{4,12},{5,13},{6,14},{7,15},{8,0},{9,1},... | collective-permute-start | bytes 1572872 | tf_op jit(solution)/shard_map/ppermute | solution.py:417
  191.1 26.3 %collective-permute-start.29 = (bf16[4,1,1,1,32,1024]{5,4,2,1,0,3:T(8,128)(2,1)S(1)}, bf16[4,1,1,1,32,1024]{5,4,2,1,0,3:T(8,128)(2,1)S(1)}, u32[]{:S(2)}, u32[]{:S(2)}) collective-permute-start(bf16[4,1,1,1,32,1024]{5,4,2,1,0,3:T(8,128)(2,1)S(1)} %broadcast_select_fusion.23), channel_id=1, source_target_pairs={{0,8},{1,9},{2,10},{3,11},{4,12},{5,13},{6,14},{7,15},{8,0},{9,1},... | collective-permute-start | bytes 786440 | tf_op jit(solution)/shard_map/ppermute | solution.py:417
  191.5 26.1 %collective-permute-start.28 = (bf16[4,1,1,1,32,1024]{5,4,0,3,2,1:T(8,128)(2,1)S(1)}, bf16[4,1,1,1,32,1024]{5,4,0,3,2,1:T(8,128)(2,1)S(1)}, u32[]{:S(2)}, u32[]{:S(2)}) collective-permute-start(bf16[4,1,1,1,32,1024]{5,4,0,3,2,1:T(8,128)(2,1)S(1)} %broadcast_select_fusion.24), channel_id=1, source_target_pairs={{0,16},{1,17},{2,18},{3,19},{4,20},{5,21},{6,22},{7,23},{8,24},{9,... | collective-permute-start | bytes 786440 | tf_op jit(solution)/shard_map/ppermute | solution.py:417
  220.7 14.6 %collective-permute-start.30 = (bf16[1024,1024]{1,0:T(8,128)(2,1)S(1)}, bf16[1024,1024]{1,0:T(8,128)(2,1)S(1)}, u32[]{:S(2)}, u32[]{:S(2)}) collective-permute-start(bf16[1024,1024]{1,0:T(8,128)(2,1)S(1)} %convolution_convert_fusion.1), channel_id=1, source_target_pairs={{0,4},{1,5},{2,6},{3,7},{4,0},{5,1},{6,2},{7,3},{8,12},{9,13},{10,... | collective-permute-start | bytes 6291464 | tf_op jit(solution)/shard_map/ppermute | solution.py:417
  222.0 13.2 %collective-permute-start.31 = (bf16[2,2,32,1024]{3,2,1,0:T(8,128)(2,1)S(1)}, bf16[2,2,32,1024]{3,2,1,0:T(8,128)(2,1)S(1)}, u32[]{:S(2)}, u32[]{:S(2)}) collective-permute-start(bf16[2,2,32,1024]{3,2,1,0:T(8,128)(2,1)S(1)} %slice.249), channel_id=1, source_target_pairs={{0,2},{1,3},{2,0},{3,1},{4,6},{5,7},{6,4},{7,5},{8,10},{9,11},{10,... | collective-permute-start | bytes 786440 | tf_op jit(solution)/shard_map/ppermute | solution.py:417
  237.4 15.3 %collective-permute-start.36 = (bf16[256,1024]{1,0:T(8,128)(2,1)S(1)}, bf16[256,1024]{1,0:T(8,128)(2,1)S(1)}, u32[]{:S(2)}, u32[]{:S(2)}) collective-permute-start(bf16[256,1024]{1,0:T(8,128)(2,1)S(1)} %slice.260), channel_id=1, source_target_pairs={{0,1},{1,0},{2,3},{3,2},{4,5},{5,4},{6,7},{7,6},{8,9},{9,8},{10,11... | collective-permute-start | bytes 1572872 | tf_op jit(solution)/shard_map/ppermute | solution.py:417
  239.5 10.5 %collective-permute-start.34 = (bf16[2,1,2,96,512]{4,3,2,1,0:T(8,128)(2,1)S(1)}, bf16[2,1,2,96,512]{4,3,2,1,0:T(8,128)(2,1)S(1)}, u32[]{:S(2)}, u32[]{:S(2)}) collective-permute-start(bf16[2,1,2,96,512]{4,3,2,1,0:T(8,128)(2,1)S(1)} %broadcast_select_fusion.17), channel_id=1, source_target_pairs={{0,16},{1,17},{2,18},{3,19},{4,20},{5,21},{6,22},{7,23},{8,24},{9,... | collective-permute-start | bytes 1179656 | tf_op jit(solution)/shard_map/ppermute | solution.py:417
  241.1 10.3 %collective-permute-start.32 = (bf16[1,2,2,96,512]{4,3,2,1,0:T(8,128)(2,1)S(1)}, bf16[1,2,2,96,512]{4,3,2,1,0:T(8,128)(2,1)S(1)}, u32[]{:S(2)}, u32[]{:S(2)}) collective-permute-start(bf16[1,2,2,96,512]{4,3,2,1,0:T(8,128)(2,1)S(1)} %broadcast_select_fusion.18), channel_id=1, source_target_pairs={{0,8},{1,9},{2,10},{3,11},{4,12},{5,13},{6,14},{7,15},{8,0},{9,1},... | collective-permute-start | bytes 1179656 | tf_op jit(solution)/shard_map/ppermute | solution.py:417
  258.3 12.4 %collective-permute-start.38 = (bf16[1,1,2,96,1024]{4,3,2,1,0:T(8,128)(2,1)}, bf16[1,1,2,96,1024]{4,3,2,1,0:T(8,128)(2,1)S(1)}, u32[]{:S(2)}, u32[]{:S(2)}) collective-permute-start(bf16[1,1,2,96,1024]{4,3,2,1,0:T(8,128)(2,1)} %pad_maximum_fusion.8), channel_id=1, source_target_pairs={{0,0},{1,1},{2,2},{3,3},{4,6},{5,7},{6,4},{7,5},{8,8},{9,9},{10,10... | collective-permute-start | bytes 1179656 | tf_op jit(solution)/shard_map/ppermute | solution.py:417
  260.7 10.0 %collective-permute-start.39 = (bf16[64,1024]{1,0:T(8,128)(2,1)S(1)}, bf16[64,1024]{1,0:T(8,128)(2,1)S(1)}, u32[]{:S(2)}, u32[]{:S(2)}) collective-permute-start(bf16[64,1024]{1,0:T(8,128)(2,1)S(1)} %get-tuple-element.257), channel_id=1, source_target_pairs={{0,2},{1,3},{2,0},{3,1},{4,6},{5,7},{6,4},{7,5},{8,10},{9,11},{10,... | collective-permute-start | bytes 393224 | tf_op jit(solution)/shard_map/ppermute | solution.py:417
  277.8 9.3 %collective-permute-start.41 = (bf16[64,1024]{1,0:T(8,128)(2,1)}, bf16[64,1024]{1,0:T(8,128)(2,1)S(1)}, u32[]{:S(2)}, u32[]{:S(2)}) collective-permute-start(bf16[64,1024]{1,0:T(8,128)(2,1)} %get-tuple-element.196), channel_id=1, source_target_pairs={{0,2},{1,3},{2,0},{3,1},{4,6},{5,7},{6,4},{7,5},{8,10},{9,11},{10,... | collective-permute-start | bytes 393224 | tf_op jit(solution)/shard_map/ppermute | solution.py:417
  291.9 9.7 %collective-permute-start.46 = (bf16[128,1024]{1,0:T(8,128)(2,1)S(1)}, bf16[128,1024]{1,0:T(8,128)(2,1)S(1)}, u32[]{:S(2)}, u32[]{:S(2)}) collective-permute-start(bf16[128,1024]{1,0:T(8,128)(2,1)S(1)} %slice.231), channel_id=1, source_target_pairs={{0,1},{1,0},{2,3},{3,2},{4,5},{5,4},{6,7},{7,6},{8,9},{9,8},{10,11... | collective-permute-start | bytes 786440 | tf_op jit(solution)/shard_map/ppermute | solution.py:417
  292.0 10.6 %collective-permute-start.45 = (bf16[64,1024]{1,0:T(8,128)(2,1)}, bf16[64,1024]{1,0:T(8,128)(2,1)S(1)}, u32[]{:S(2)}, u32[]{:S(2)}) collective-permute-start(bf16[64,1024]{1,0:T(8,128)(2,1)} %get-tuple-element.205), channel_id=1, source_target_pairs={{0,2},{1,3},{2,0},{3,1},{4,6},{5,7},{6,4},{7,5},{8,10},{9,11},{10,... | collective-permute-start | bytes 393224 | tf_op jit(solution)/shard_map/ppermute | solution.py:417
  302.6 9.1 %collective-permute-start.48 = (bf16[2,1,1,176,512]{4,3,2,1,0:T(8,128)(2,1)S(1)}, bf16[2,1,1,176,512]{4,3,2,1,0:T(8,128)(2,1)S(1)}, u32[]{:S(2)}, u32[]{:S(2)}) collective-permute-start(bf16[2,1,1,176,512]{4,3,2,1,0:T(8,128)(2,1)S(1)} %pad_maximum_fusion.10), channel_id=1, source_target_pairs={{0,16},{1,17},{2,18},{3,19},{4,20},{5,21},{6,22},{7,23},{8,24},{9,... | collective-permute-start | bytes 1081352 | tf_op jit(solution)/shard_map/ppermute | solution.py:417
  304.7 9.3 %collective-permute-start.49 = (bf16[64,1024]{1,0:T(8,128)(2,1)S(1)}, bf16[64,1024]{1,0:T(8,128)(2,1)S(1)}, u32[]{:S(2)}, u32[]{:S(2)}) collective-permute-start(bf16[64,1024]{1,0:T(8,128)(2,1)S(1)} %copy-done.38), channel_id=1, source_target_pairs={{0,2},{1,3},{2,0},{3,1},{4,6},{5,7},{6,4},{7,5},{8,10},{9,11},{10,... | collective-permute-start | bytes 393224 | tf_op jit(solution)/shard_map/ppermute | solution.py:417
  323.4 9.2 %collective-permute-start.53 = (f32[2,1024]{1,0:T(2,128)S(1)}, f32[2,1024]{1,0:T(2,128)S(1)}, u32[]{:S(2)}, u32[]{:S(2)}) collective-permute-start(f32[2,1024]{1,0:T(2,128)S(1)} %slice_add_fusion), channel_id=1, source_target_pairs={{0,1},{1,0},{2,3},{3,2},{4,5},{5,4},{6,7},{7,6},{8,9},{9,8},{10,11... | collective-permute-start | bytes 24584 | tf_op jit(solution)/shard_map/ppermute | solution.py:417
  323.5 9.1 %collective-permute-start.54 = (f32[2,1024]{1,0:T(2,128)S(1)}, f32[2,1024]{1,0:T(2,128)S(1)}, u32[]{:S(2)}, u32[]{:S(2)}) collective-permute-start(f32[2,1024]{1,0:T(2,128)S(1)} %slice_add_fusion), channel_id=1, source_target_pairs={{0,2},{1,3},{2,0},{3,1},{4,6},{5,7},{6,4},{7,5},{8,10},{9,11},{10,... | collective-permute-start | bytes 24584 | tf_op jit(solution)/shard_map/ppermute | solution.py:417
  (67 other events, 503.2 us)
Sparse Core Ops, SparseCore 0:
  18.7 82.0 all-gather.2
